TPU v7x, 256 devices: a whole 4x4x8 slice. The times are simulated.
256 devices in a mesh: layer: 8 (over z), tok: 32 (over x, y, core).
Axes of the slice: x: 4, y: 4, z: 8, core: 2. Of those that a mesh axis runs over, the one named last changes fastest.
Arguments:
- acts: bfloat16 [8, 1024, 4096], P('layer', 'tok'), may hold values from -6 to 6
- targets: bfloat16 [8, 1024, 4096], P('layer', 'tok'), may hold values from -6 to 6
- enc_weight: bfloat16 [8, 2048, 4096], P('layer', 'tok'), may hold values from -0.09375 to 0.09375
- enc_bias: float32 [8, 2048], P('layer', 'tok'), may hold values from -3 to 3
- dec_weight: bfloat16 [8, 8, 2048, 4096], P('layer', None, 'tok'), may hold values from -0.09375 to 0.09375
Outputs:
- rebuilt: bfloat16 [8, 1024, 4096], P('layer', 'tok')
- dec_grad: bfloat16 [8, 8, 2048, 4096], P('layer', None, 'tok')
- enc_grad: bfloat16 [8, 2048, 4096], P('layer', 'tok')
All inputs are finite; a program needn't handle non-finite values.
Results may differ from a plain program's by a relative error of at most 0.022.
Values may be sent and summed in bfloat16 or wider, within the bound.
No kernel may reach another device: no remote copies, remote signals or barrier semaphores. Data moves between devices by JAX's collectives and lax.ppermute only.
A program may use at most 128 MiB of HBM per device.

v0:
```python
import math

import jax
import jax.numpy as jnp
from jax import lax
from jax.sharding import PartitionSpec as P


def source_term(carried, block):
    return lax.dot_general(
        carried, block, (((0,), (0,)), ((), ())), preferred_element_type=jnp.float32
    )


def per_device(acts, targets, enc_weight, enc_bias, dec_weight):
    layer_count = lax.axis_size("layer")
    owner_index = lax.axis_index("layer")
    tokens_all = acts.shape[1] * lax.axis_size("tok")
    grad_scale = 1.0 / math.sqrt(tokens_all)
    all_tokens = lax.all_gather(acts[0], "tok", axis=0, tiled=True)
    pre_acts = (
        lax.dot_general(
            enc_weight[0], all_tokens, (((1,), (1,)), ((), ())), preferred_element_type=jnp.float32
        )
        + enc_bias[0][:, None]
    )
    latents = jnp.maximum(pre_acts, 0.0).astype(jnp.bfloat16)
    decoder = dec_weight[0]
    model_width = decoder.shape[-1]
    recon_part = jnp.zeros((tokens_all, model_width), jnp.float32)
    sources = lax.all_gather(latents[None], "layer", axis=0, tiled=True)

    def add_source(source, running):
        return running + source_term(sources[source], decoder[source])

    recon_part = lax.fori_loop(0, owner_index + 1, add_source, recon_part)
    recon_sum = lax.psum_scatter(
        recon_part.astype(jnp.bfloat16), "tok", scatter_dimension=0, tiled=True
    ).astype(jnp.float32)
    errors = (recon_sum - targets[0].astype(jnp.float32)).astype(jnp.bfloat16)
    all_errors = lax.all_gather(errors, "tok", axis=0, tiled=True)
    latent_rows = latents.shape[0]

    def backward(source, loop_state):
        dec_grads, partials = loop_state
        block_grad = grad_scale * jnp.dot(
            sources[source], all_errors, preferred_element_type=jnp.float32
        )
        grad_term = grad_scale * lax.dot_general(
            decoder[source],
            all_errors,
            (((1,), (1,)), ((), ())),
            preferred_element_type=jnp.float32,
        )
        dec_grads = lax.dynamic_update_index_in_dim(
            dec_grads, block_grad.astype(jnp.bfloat16), source, 0
        )
        partials = lax.dynamic_update_index_in_dim(partials, grad_term, source, 0)
        return (dec_grads, partials)

    start_grads = jnp.zeros((layer_count, latent_rows, model_width), jnp.bfloat16)
    start_partials = jnp.zeros((layer_count, latent_rows, tokens_all), jnp.float32)
    dec_grads, partials = lax.fori_loop(0, owner_index + 1, backward, (start_grads, start_partials))
    latent_grad = lax.psum_scatter(
        partials.astype(jnp.bfloat16), "layer", scatter_dimension=0, tiled=True
    ).astype(jnp.float32)[0]
    pre_grad = jnp.where(pre_acts > 0, latent_grad, 0.0).astype(jnp.bfloat16)
    enc_grad = jnp.dot(pre_grad, all_tokens, preferred_element_type=jnp.float32).astype(
        jnp.bfloat16
    )
    return (recon_sum.astype(jnp.bfloat16)[None], dec_grads[None], enc_grad[None])


def solution(mesh):
    return jax.shard_map(
        per_device,
        mesh=mesh,
        in_specs=(
            P("layer", "tok", None),
            P("layer", "tok", None),
            P("layer", "tok", None),
            P("layer", "tok"),
            P("layer", None, "tok", None),
        ),
        out_specs=(P("layer", "tok", None), P("layer", None, "tok", None), P("layer", "tok", None)),
        check_vma=False,
    )
```

profile of v0, /device:TPU:1, one launch (start us, length us, event | category | flops | bytes accessed | tf_op | source)
XLA Modules:
  0.0 530.5 jit_solution(17229023548182751218)
XLA Ops:
  7.2 0.0 all-gather.8.cloned.1.call-start
  7.2 0.7 all-gather.8.cloned.1.call-update
  7.9 0.0 all-gather.10.cloned.1.call-start
  8.0 64.8 %all-gather.8.cloned.1.call-done = bf16[1,1024,4096]{2,1,0:T(8,128)(2,1)} async-done(((bf16[1,32,4096]{2,1,0:T(8,128)(2,1)}), bf16[1,1024,4096]{2,1,0:T(8,128)(2,1)}) %all-gather.8.cloned.1.call-update) | async-done | bytes 8388624 | tf_op jit(solution)/shard_map/all_gather | solution.py:20
  72.7 6.7 %maximum_convert_fusion = (bf16[64,1024]{1,0:T(8,128)(2,1)}, f32[64,1024]{1,0:T(8,128)S(1)}) fusion(f32[64]{0:T(128)} %bitcast.78, bf16[1,1024,4096]{2,1,0:T(8,128)(2,1)} %all-gather.8.cloned.1.call-done, bf16[1,64,4096]{2,1,0:T(8,128)(2,1)S(1)} %copy-done), kind=kOutput, calls=%fused_computation.31 | convolution fusion | flops 537067520 | bytes 9306368 | tf_op jit(solution)/shard_map/dot_general | solution.py:22
  79.5 0.0 reduce-scatter.3.cloned.1.call-start
  79.5 33.0 %all-gather.10.cloned.1.call-done = bf16[512,1024]{1,0:T(8,128)(2,1)} async-done(((bf16[64,1024]{1,0:T(8,128)(2,1)}), bf16[512,1024]{1,0:T(8,128)(2,1)}) %all-gather.10.cloned.1.call-update) | async-done | bytes 1048592 | tf_op jit(solution)/shard_map/all_gather | solution.py:31
  112.5 7.8 %broadcast_in_dim.31 = f32[1024,4096]{1,0:T(8,128)} broadcast(f32[]{:T(128)} %constant.21.clone.1), dimensions={} | broadcast | bytes 16777220 | tf_op jit(solution)/shard_map/broadcast_in_dim | solution.py:30
  120.3 14.1 %while.22 = (s32[]{:T(128)}, f32[1024,4096]{1,0:T(8,128)}, s32[]{:T(128)}, bf16[8,64,1024]{2,1,0:T(8,128)(2,1)}, bf16[8,64,4096]{2,1,0:T(8,128)(2,1)}, /*index=5*/s32[]{:T(128)}, s32[]{:T(128)}, s32[]{:T(128)}) while((s32[]{:T(128)}, f32[1024,4096]{1,0:T(8,128)}, s32[]{:T(128)}, bf16[8,64,1024]{2,1,0:T(8,128)(2,1)}, ...), condition=%wide.region_1.0_spmd, body=%wide.region_0.0_spmd.sunk | while | flops 541065216 | bytes 34210936 | solution.py:36
  120.3 14.1 %convolution_add_fusion.2 = f32[1024,4096]{1,0:T(8,128)} fusion(f32[1024,4096]{1,0:T(8,128)} %get-tuple-element.184, bf16[8,64,4096]{2,1,0:T(8,128)(2,1)} %get-tuple-element.195, s32[]{:T(128)S(6)} %select_n.23, bf16[8,64,1024]{2,1,0:T(8,128)(2,1)} %get-tuple-element.194), kind=kOutput, calls=%fused_computation.clone.1 | convolution fusion | flops 541065216 | bytes 34210816 | tf_op jit(solution)/shard_map/while/body/dot_general | solution.py:10
  134.4 9.0 %convert_element_type.33 = bf16[1024,4096]{1,0:T(8,128)(2,1)} convert(f32[1024,4096]{1,0:T(8,128)} %get-tuple-element.70) | non-fusion elementwise | flops 4194304 | bytes 25165824 | tf_op jit(solution)/shard_map/convert_element_type | solution.py:38
  143.4 0.0 all-gather.6.cloned.1.call-start
  143.5 199.8 %reduce-scatter.3.cloned.1.call-done = bf16[32,4096]{1,0:T(8,128)(2,1)} async-done(((bf16[1024,4096]{1,0:T(8,128)(2,1)}), bf16[32,4096]{1,0:T(8,128)(2,1)}) %reduce-scatter.3.cloned.1.call-update) | async-done | bytes 262160 | tf_op jit(solution)/shard_map/reduce_scatter | solution.py:37
  343.3 1.7 fusion.29
  345.0 0.0 reduce-scatter.5.cloned.1.call-start
  345.1 61.0 %all-gather.6.cloned.1.call-done = bf16[1024,4096]{1,0:T(8,128)(2,1)} async-done(((bf16[32,4096]{1,0:T(8,128)(2,1)}), bf16[1024,4096]{1,0:T(8,128)(2,1)}) %all-gather.6.cloned.1.call-update) | async-done | bytes 8388624 | tf_op jit(solution)/shard_map/all_gather | solution.py:41
  406.1 2.5 broadcast_in_dim.34
  408.6 0.1 broadcast_in_dim.35
  408.7 9.7 %while.23 = (s32[]{:T(128)}, bf16[8,64,4096]{2,1,0:T(8,128)(2,1)}, bf16[8,64,1024]{2,1,0:T(8,128)(2,1)S(1)}, s32[]{:T(128)}, bf16[8,64,1024]{2,1,0:T(8,128)(2,1)...) while((s32[]{:T(128)}, bf16[8,64,4096]{2,1,0:T(8,128)(2,1)}, ...), condition=%wide.region_4.5_spmd, body=%wide.region_3.4_spmd.sunk | while | flops 1074331648 | bytes 43387064 | solution.py:63
  408.7 6.0 %fusion.52 = bf16[8,64,4096]{2,1,0:T(8,128)(2,1)} fusion(bf16[8,64,4096]{2,1,0:T(8,128)(2,1)} %get-tuple-element.210, s32[]{:T(128)S(6)} %select_n.24, bf16[1024,4096]{1,0:T(8,128)(2,1)} %get-tuple-element.224, bf16[8,64,1024]{2,1,0:T(8,128)(2,1)} %get-tuple-element.223), kind=kOutput, calls=%fused_computation.9.clone.1 | convolution fusion | flops 537395200 | bytes 9044992 | tf_op jit(solution)/shard_map/while/body/dot_general | solution.py:46
  414.7 3.7 fusion.53
  418.4 1.0 copy-done.1
  419.4 98.7 %reduce-scatter.5.cloned.1.call-done = bf16[1,64,1024]{2,1,0:T(8,128)(2,1)} async-done(((bf16[8,64,1024]{2,1,0:T(8,128)(2,1)}), bf16[1,64,1024]{2,1,0:T(8,128)(2,1)}) %reduce-scatter.5.cloned.1.call-update) | async-done | bytes 131088 | tf_op jit(solution)/shard_map/reduce_scatter | solution.py:64
  518.2 5.8 %fusion.23 = bf16[1,64,4096]{2,1,0:T(8,128)(2,1)} fusion(bf16[1,1024,4096]{2,1,0:T(8,128)(2,1)} %all-gather.8.cloned.1.call-done, f32[64,1024]{1,0:T(8,128)S(1)} %get-tuple-element.98, bf16[1,64,1024]{2,1,0:T(8,128)(2,1)} %reduce-scatter.5.cloned.1.call-done), kind=kOutput, calls=%fused_computation.24 | convolution fusion | flops 537395200 | bytes 9306112 | tf_op jit(solution)/shard_map/dot_general | solution.py:68
  (14 shorter events, 0.1 us)
Async XLA Ops:
  7.2 65.6 %copy-start = (bf16[1,64,4096]{2,1,0:T(8,128)(2,1)S(1)}, bf16[1,64,4096]{2,1,0:T(8,128)(2,1)}, u32[]{:S(2)}) copy-start(bf16[1,64,4096]{2,1,0:T(8,128)(2,1)} %param.11) | copy-start | bytes 1572868
  7.2 65.6 %all-gather.8.cloned.1.call-start = ((), (), s32[]{:S(2)}) async-start(), calls=%async_computation.5 | async-start | bytes 8650752 | tf_op jit(solution)/shard_map/all_gather | solution.py:20
  7.9 104.6 %all-gather.10.cloned.1.call-start = ((), (), s32[]{:S(2)}) async-start(), calls=%async_computation.6 | async-start | bytes 1179648 | tf_op jit(solution)/shard_map/all_gather | solution.py:31
  79.5 263.8 %reduce-scatter.3.cloned.1.call-start = ((), (), s32[]{:S(2)}) async-start(), calls=%async_computation.2 | async-start | bytes 8650752 | tf_op jit(solution)/shard_map/reduce_scatter | solution.py:37
  143.4 199.9 %copy-start.2 = (bf16[1,32,4096]{2,1,0:T(8,128)(2,1)S(1)}, bf16[1,32,4096]{2,1,0:T(8,128)(2,1)}, u32[]{:S(2)}) copy-start(bf16[1,32,4096]{2,1,0:T(8,128)(2,1)} %param.10) | copy-start | bytes 786436
  143.4 262.6 %all-gather.6.cloned.1.call-start = ((), (), s32[]{:S(2)}) async-start(), calls=%async_computation.3 | async-start | bytes 8650752 | tf_op jit(solution)/shard_map/all_gather | solution.py:41
  345.0 173.2 %reduce-scatter.5.cloned.1.call-start = ((), (), s32[]{:S(2)}) async-start(), calls=%async_computation.4 | async-start | bytes 1179648 | tf_op jit(solution)/shard_map/reduce_scatter | solution.py:64
  408.7 6.0 %slice-start = ((s8[8388608]{0:T(1024)(128)(4,1)}), s8[4194304]{0:T(1024)(128)(4,1)S(1)}, s32[]{:S(2)}) async-start(s8[8388608]{0:T(1024)(128)(4,1)} %bitcast.72), calls=%async_computation.7 | async-start | bytes 8388608 | tf_op jit(solution)/shard_map/while
  408.7 6.0 %slice-start.1 = ((s8[8388608]{0:T(1024)(128)(4,1)}), s8[4194304]{0:T(1024)(128)(4,1)S(1)}, s32[]{:S(2)}) async-start(s8[8388608]{0:T(1024)(128)(4,1)} %bitcast.72), calls=%async_computation.8 | async-start | bytes 8388608 | tf_op jit(solution)/shard_map/while
  418.4 1.0 copy-start.1
Sparse Core Ops, SparseCore 0:
  10.6 62.1 all-gather.7
  79.6 32.8 all-gather.9
  143.6 199.6 reduce-scatter.2
  346.6 59.4 all-gather.5
  419.6 98.5 reduce-scatter.4
where the time goes:
time: 535 us; the launch traced here: 531 us
  waiting for transfers between devices  458 us (86%)
  matrix products  36.3 us (7%)
  between operations  13.8 us (3%)
  local copies, waits for them, and re-layouts  11.5 us (2%)
  other arithmetic  10.7 us (2%)
    reduce_scatter x1, waiting for transfers between devices, per_device(): lax.psum_scatter(recon_part.astype(jnp.bfloat16), 'tok', scatter_dimensio...  200 us
    reduce_scatter x1, waiting for transfers between devices, per_device(): lax.psum_scatter(partials.astype(jnp.bfloat16), 'layer', scatter_dimensio...  98.7 us
    all_gather x1, waiting for transfers between devices, per_device(): all_tokens = lax.all_gather(acts[0], 'tok', axis=0, tiled=True)  64.8 us
    all_gather x1, waiting for transfers between devices, per_device(): all_errors = lax.all_gather(errors, 'tok', axis=0, tiled=True)  61 us
    all_gather x1, waiting for transfers between devices, per_device(): sources = lax.all_gather(latents[None], 'layer', axis=0, tiled=True)  33 us
    dot_general x1, matrix products, source_term(): lax.dot_general(carried, block, (((0,), (0,)), ((), ())), preferred_eleme...  14.1 us
  transfers between devices with their start and end apart: 5, of which 5 were waited for; matrix products, arithmetic and copies ran while one was open for 0% of the time, Pallas kernels for 0%

commit v1 on v0

v1 whole, which is shorter than its diff:
```python
import functools
import math

import jax
import jax.numpy as jnp
from jax import lax
from jax.experimental import pallas as pl
from jax.experimental.pallas import tpu as pltpu
from jax.sharding import PartitionSpec as P

BF = jnp.bfloat16
F32 = jnp.float32
SIDE = 4
VMEM_LIMIT = 16 * 1024 * 1024
MASKS = ((1, 3), (3, 1))
AXES = (("x", "y"), ("y", "x"))


def tok_index(x, y, core):
    return (x * SIDE + y) * 2 + core


def chip_pairs(axis, which):
    pairs = []
    for x in range(SIDE):
        for y in range(SIDE):
            for core in range(2):
                mask = MASKS[core][which]
                px, py = (x ^ mask, y) if axis == "x" else (x, y ^ mask)
                pairs.append((tok_index(x, y, core), tok_index(px, py, core)))
    return pairs


CORE_PAIRS = [(i, i ^ 1) for i in range(2 * SIDE * SIDE)]


def exchange(value, axis, which):
    return lax.ppermute(value, "tok", chip_pairs(axis, which))


def swap_cores(value):
    return lax.ppermute(value, "tok", CORE_PAIRS)


def dot(a, b, ca, cb):
    return lax.dot_general(a, b, (((ca,), (cb,)), ((), ())), preferred_element_type=F32)


def tie(*values):
    return list(lax.optimization_barrier(values))


def params():
    return pltpu.CompilerParams(vmem_limit_bytes=VMEM_LIMIT)


def cost(flops, nbytes):
    return pl.CostEstimate(flops=flops, bytes_accessed=nbytes, transcendentals=0)


def recon_body(start, layer_ref, lat_ref, own_dec, other_dec, *refs):
    outs, (own_ref, other_ref) = refs[:-2], refs[-2:]
    layers, _, both = lat_ref.shape
    tokens = own_ref.shape[0]
    half = both // 2
    block = outs[0].shape[1]

    @pl.when(pl.program_id(0) == 0)
    def _():
        for k, ref in enumerate((own_ref, other_ref)):
            pieces = []
            for s in range(layers):
                piece = lat_ref[s, start : start + tokens, k * half : (k + 1) * half]
                pieces.append(jnp.where(s <= layer_ref[0], piece, jnp.zeros_like(piece)))
            ref[...] = jnp.concatenate(pieces, axis=1)

    columns = pl.ds(pl.multiple_of(pl.program_id(0) * block, block), block)
    part = jnp.dot(own_ref[...], own_dec[:, columns], preferred_element_type=F32)
    part += jnp.dot(other_ref[...], other_dec[:, columns], preferred_element_type=F32)
    part = part.astype(BF)
    rows = outs[0].shape[0]
    for i, out in enumerate(outs):
        out[...] = part[i * rows : (i + 1) * rows]


def recon(layer, latents, start, tokens, decs, streams=4, block=2048):
    depth, width = decs[0].shape
    rows = tokens // streams
    column = lambda i, layer_ref: (0, i)
    whole = lambda i, layer_ref: (0, 0)
    return pl.pallas_call(
        functools.partial(recon_body, start),
        grid_spec=pltpu.PrefetchScalarGridSpec(
            num_scalar_prefetch=1,
            grid=(width // block,),
            in_specs=[pl.BlockSpec(memory_space=pltpu.VMEM)] * 3,
            out_specs=[pl.BlockSpec((rows, block), column)] * streams
            + [pl.BlockSpec((tokens, depth), whole)] * 2,
        ),
        out_shape=[jax.ShapeDtypeStruct((rows, width), BF)] * streams
        + [jax.ShapeDtypeStruct((tokens, depth), BF)] * 2,
        compiler_params=params(),
        cost_estimate=cost(4 * tokens * depth * width, 4 * depth * width),
    )(layer, latents, *decs)


def grads_body(scale, layer_ref, own_dec, other_dec, *refs):
    errs, refs = refs[:4], refs[4:]
    before, (out, err_ref), totals = refs[:-4], refs[-4:-2], refs[-2:]
    layers, both, _ = out.shape
    half = both // 2
    tokens, block = err_ref.shape
    at = out.shape[2] - tokens

    @pl.when(pl.program_id(0) == 0)
    def _():
        for total in totals:
            total[...] = jnp.zeros_like(total)

    err = jnp.concatenate([e[...] for e in errs], axis=0)
    err_ref[...] = err
    columns = pl.ds(pl.multiple_of(pl.program_id(0) * block, block), block)
    for total, dec in zip(totals, (own_dec, other_dec)):
        total[...] += dot(dec[:, columns], err, 1, 1)

    @pl.when(pl.program_id(0) == pl.num_programs(0) - 1)
    def _():
        for s in range(layers):
            for k, total in enumerate(totals):
                value = scale * total[s * half : (s + 1) * half, :]
                value = jnp.where(s <= layer_ref[0], value, 0.0)
                out[s, k * half : (k + 1) * half, at:] = value.astype(BF)
        for ref in before:
            out[:, :, :at] = ref[...]


def latent_grads(layer, decs, errs, before, scale, layers, block=2048):
    depth, width = decs[0].shape
    rows = errs[0].shape[0]
    tokens = rows * len(errs)
    both = 2 * depth // layers
    span = tokens + sum(b.shape[2] for b in before)
    column = lambda i, layer_ref: (0, i)
    return pl.pallas_call(
        functools.partial(grads_body, scale),
        grid_spec=pltpu.PrefetchScalarGridSpec(
            num_scalar_prefetch=1,
            grid=(width // block,),
            in_specs=[pl.BlockSpec(memory_space=pltpu.VMEM)] * 2
            + [pl.BlockSpec((rows, block), column)] * len(errs)
            + [pl.BlockSpec(memory_space=pltpu.VMEM)] * len(before),
            out_specs=[
                pl.BlockSpec((layers, both, span), lambda i, layer_ref: (0, 0, 0)),
                pl.BlockSpec((tokens, block), column),
            ],
            scratch_shapes=[pltpu.VMEM((depth, tokens), F32)] * 2,
        ),
        out_shape=[
            jax.ShapeDtypeStruct((layers, both, span), BF),
            jax.ShapeDtypeStruct((tokens, width), BF),
        ],
        compiler_params=params(),
        cost_estimate=cost(4 * tokens * depth * width, 4 * depth * width),
    )(layer, *decs, *errs, *before)


def encode_body(*refs):
    blocks, (own, other, bias, latents, mask, tokens, total) = refs[:-7], refs[-7:]

    @pl.when(pl.program_id(0) == 0)
    def _():
        total[...] = jnp.zeros_like(total)

    value = jnp.concatenate([b[...] for b in blocks], axis=0)
    tokens[...] = value
    total[...] += dot(value, jnp.concatenate([own[...], other[...]], axis=0), 1, 1)

    @pl.when(pl.program_id(0) == pl.num_programs(0) - 1)
    def _():
        pre = total[...] + bias[...]
        latents[...] = jnp.maximum(pre, 0.0).astype(BF)
        mask[...] = jnp.where(pre > 0, 1.0, 0.0).T.astype(BF)


def encode(blocks, encs, bias, block=1024):
    rows, width = blocks[0].shape
    count = rows * len(blocks)
    both = bias.shape[1]
    column = lambda i: (0, i)
    whole = lambda i: (0, 0)
    return pl.pallas_call(
        encode_body,
        grid=(width // block,),
        in_specs=[pl.BlockSpec((rows, block), column)] * len(blocks)
        + [pl.BlockSpec((both // 2, block), column)] * 2
        + [pl.BlockSpec((1, both), whole)],
        out_specs=[
            pl.BlockSpec((count, both), whole),
            pl.BlockSpec((both, count), whole),
            pl.BlockSpec((count, block), column),
        ],
        out_shape=[
            jax.ShapeDtypeStruct((count, both), BF),
            jax.ShapeDtypeStruct((both, count), BF),
            jax.ShapeDtypeStruct((count, width), BF),
        ],
        scratch_shapes=[pltpu.VMEM((count, both), F32)],
        compiler_params=params(),
        cost_estimate=cost(2 * count * both * width, 4 * count * width),
    )(*blocks, *encs, bias)


def dec_grad_body(scale, *refs):
    lats, errs, out = refs[:4], refs[4:8], refs[8]
    total = dot(lats[0][...], errs[0][...], 0, 0)
    for lat, err in zip(lats[1:], errs[1:]):
        total += dot(lat[...], err[...], 0, 0)
    out[...] = (scale * total).astype(BF)


def dec_grads(lats, errs, scale, block=1024):
    tokens, depth = lats[0].shape
    width = errs[0].shape[1]
    return pl.pallas_call(
        functools.partial(dec_grad_body, scale),
        grid=(width // block,),
        in_specs=[pl.BlockSpec((tokens, depth), lambda i: (0, 0))] * 4
        + [pl.BlockSpec((tokens, block), lambda i: (0, i))] * 4,
        out_specs=pl.BlockSpec((depth, block), lambda i: (0, i)),
        out_shape=jax.ShapeDtypeStruct((depth, width), BF),
        compiler_params=params(),
        cost_estimate=cost(8 * tokens * depth * width, 8 * tokens * width + 2 * depth * width),
    )(*lats, *errs)


def vmem_call(body, outs, *operands):
    spec = pl.BlockSpec(memory_space=pltpu.VMEM)
    return pl.pallas_call(
        body,
        in_specs=[spec] * len(operands),
        out_specs=[spec] * len(outs),
        out_shape=[jax.ShapeDtypeStruct(shape, dtype) for shape, dtype in outs],
        compiler_params=params(),
        cost_estimate=cost(
            sum(o.size for o in operands), sum(o.size * o.dtype.itemsize for o in operands)
        ),
    )(*operands)


def add_half_body(*refs):
    keep, got, send, rest = refs[:4], refs[4:8], refs[8:12], refs[12:16]
    for k, g, s, r in zip(keep, got, send, rest):
        total = k[...].astype(F32) + g[...].astype(F32)
        span = s.shape[0]
        s[...] = total[span:].astype(BF)
        r[...] = total[:span]


ORDERS = ((1, 0, 3, 2), (2, 3, 0, 1))


def group_step(turn, totals, values, target, sends):
    part = target.shape[0] // 2
    wide = sends[0].shape[1]
    for c in range(2):
        for h in range(2):
            at = slice(h * wide, (h + 1) * wide)
            value = values(c, h, at)
            totals[c][:, at] = value
            own = target[c * part : (c + 1) * part, at].astype(F32)
            for i, b in enumerate(ORDERS[h ^ turn]):
                block = value[b * part : (b + 1) * part]
                if b == 0:
                    block = block - own
                sends[2 * c + h][i * part : (i + 1) * part, :] = block.astype(BF)


def add_last_body(*refs):
    rest, got, target, totals, sends = refs[:4], refs[4:8], refs[8], refs[9:11], refs[11:15]

    def values(c, h, at):
        pieces = [rest[2 * c + j][:, at] + got[2 * c + j][:, at].astype(F32) for j in range(2)]
        return jnp.concatenate(pieces, axis=0)

    group_step(1, totals, values, target, sends)


def add_group_body(*refs):
    before, got, target, totals, sends = refs[:2], refs[2:6], refs[6], refs[7:9], refs[9:13]
    values = lambda c, h, at: before[c][:, at] + got[2 * c + h][...].astype(F32)
    group_step(0, totals, values, target, sends)


def finish_body(*refs):
    before, got, target, rebuilt, halves = refs[:2], refs[2:6], refs[6], refs[7], refs[8:12]
    part = target.shape[0] // 2
    wide = got[0].shape[1]
    for c in range(2):
        rows = slice(c * part, (c + 1) * part)
        for h in range(2):
            at = slice(h * wide, (h + 1) * wide)
            value = before[c][:, at] + got[2 * c + h][...].astype(F32)
            rebuilt[rows, at] = value[:part].astype(BF)
            for i in range(4):
                block = value[i * part : (i + 1) * part]
                if i == 0:
                    block = block - target[rows, at].astype(F32)
                where = slice((i % 2) * part, (i % 2 + 1) * part)
                halves[2 * c + i // 2][where, at] = block.astype(BF)


def per_device(acts, targets, enc_weight, enc_bias, dec_weight):
    layers = lax.axis_size("layer")
    layer_arr = lax.axis_index("layer").astype(jnp.int32).reshape(1)
    own_tokens, width = acts.shape[1:]
    tokens_all = own_tokens * lax.axis_size("tok")
    grad_scale = 1.0 / math.sqrt(tokens_all)
    rows = enc_weight.shape[1]
    both = 2 * rows
    part = own_tokens // 2
    chunks = range(2)
    streams = [(c, j) for c in chunks for j in range(2)]
    first = lambda c, j: (AXES[c][1], j)
    second = lambda c, j: (AXES[c][1], 1 - j)

    def gather_across(halves):
        got = [exchange(h, *first(c, j)) for h, (c, j) in zip(halves, streams)]
        near = tie(*[jnp.concatenate([h, g], axis=0) for h, g in zip(halves, got)])
        far = [exchange(n, *second(c, j)) for n, (c, j) in zip(near, streams)]
        return near, far

    def along_layers(value):
        return lax.all_to_all(value, "layer", 0, 0, tiled=True)

    group = [acts[0, c * part : (c + 1) * part] for c in chunks]
    bias = jnp.concatenate([enc_bias, swap_cores(enc_bias)], axis=1)
    got = [exchange(group[c], AXES[c][0], 0) for c in chunks]
    group = [jnp.concatenate([group[c], got[c]], axis=0) for c in chunks]
    got = [exchange(group[c], AXES[c][0], 1) for c in chunks]
    halves = [(group, got)[j][c] for c, j in streams]
    *halves, enc_own, dec_own = tie(*halves, enc_weight[0], dec_weight[0])
    encs = [enc_own, swap_cores(enc_own)]
    decs = [dec_own.reshape(layers * rows, width)]
    decs.append(swap_cores(decs[0]))
    near, far = gather_across(halves)

    near_latents, near_mask, near_acts = encode(near, encs, bias)
    *far, near_latents = tie(*far, near_latents)
    far_latents, far_mask, far_acts = encode(far, encs, bias)
    latents = jnp.concatenate([near_latents, far_latents], axis=0)
    all_latents = along_layers(jnp.broadcast_to(latents, (layers,) + latents.shape))
    span = near_latents.shape[0]

    *send, far_own, far_other = recon(layer_arr, all_latents, span, span, decs)
    got = [exchange(s, *second(c, j)) for s, (c, j) in zip(send, streams)]
    *keep, near_own, near_other = recon(layer_arr, all_latents, 0, span, decs)
    half = ((2 * part, width), BF)
    sums = ((2 * part, width), F32)
    *send_rest, = vmem_call(add_half_body, [half] * 4 + [sums] * 4, *keep, *got)
    send, rest = send_rest[:4], send_rest[4:]
    got = [exchange(s, *first(c, j)) for s, (c, j) in zip(send, streams)]
    target = targets[0]
    group_outs = [((4 * part, width), F32)] * 2 + [((4 * part, width // 2), BF)] * 4
    *sends, = vmem_call(add_last_body, group_outs, *rest, *got, target)
    for turn, body in ((1, add_group_body), (0, finish_body)):
        total, sends = sends[:2], sends[2:]
        got = [exchange(s, AXES[i // 2][0], (i % 2) ^ turn) for i, s in enumerate(sends)]
        outs = group_outs if turn else [((own_tokens, width), BF)] + [half] * 4
        *sends, = vmem_call(body, outs, *total, *got, target)
    rebuilt, *halves = sends
    near, far = gather_across(halves)

    near_partial, near_err = latent_grads(layer_arr, decs, near, [], grad_scale, layers)
    *far, near_partial = tie(*far, near_partial)
    partial, far_err = latent_grads(layer_arr, decs, far, [near_partial], grad_scale, layers)
    grad = along_layers(partial)

    lats = [near_own, far_own, swap_cores(near_other), swap_cores(far_other)]
    errs = [near_err, far_err, swap_cores(near_err), swap_cores(far_err)]
    dec_grad = dec_grads(lats, errs, grad_scale).reshape(layers, rows, width)

    mask = jnp.concatenate([near_mask, far_mask], axis=1).astype(F32)
    grad = (jnp.sum(grad.astype(F32), axis=0) * mask).astype(BF)
    near_grad, far_grad = grad[:, :span], grad[:, span:]

    def enc_part(which):
        return dot(near_grad[which], near_acts, 1, 0) + dot(far_grad[which], far_acts, 1, 0)

    got = swap_cores(enc_part(slice(rows, None)).astype(BF))
    enc_grad = (enc_part(slice(0, rows)) + got.astype(F32)).astype(BF)
    return (rebuilt[None], dec_grad[None], enc_grad[None])


def solution(mesh):
    return jax.shard_map(
        per_device,
        mesh=mesh,
        in_specs=(
            P("layer", "tok", None),
            P("layer", "tok", None),
            P("layer", "tok", None),
            P("layer", "tok"),
            P("layer", None, "tok", None),
        ),
        out_specs=(P("layer", "tok", None), P("layer", None, "tok", None), P("layer", "tok", None)),
        check_vma=False,
    )
```

time: 535 us -> 236 us (0.44)
  waiting for transfers between devices: 458 us -> 122 us
  starting transfers between devices: 0.2 us -> 59.8 us
  Pallas kernels: 0 us -> 34.6 us
  matrix products: 36.3 us -> 4.32 us
  between operations: 13.8 us -> 0.99 us
  other arithmetic: 10.7 us -> 1.82 us
    reduce_scatter x2 -> x0, waiting for transfers between devices: 299 us -> none  [the longest x1 200 us: per_device(): lax.psum_scatter(recon_part.astype(jnp.bfloat16), 'tok', scatter_dimensio...]
    all_gather x3 -> x0, waiting for transfers between devices: 159 us -> none  [the longest x1 64.8 us: per_device(): all_tokens = lax.all_gather(acts[0], 'tok', axis=0, tiled=True)]
    ppermute x0 -> x44, waiting for transfers between devices: none -> 64.6 us  [the longest x36 62 us: exchange(): return lax.ppermute(value, 'tok', chip_pairs(axis, which))]
    all_to_all x0 -> x2, waiting for transfers between devices: none -> 57 us  [along_layers(): return lax.all_to_all(value, 'layer', 0, 0, tiled=True)]
    ppermute x0 -> x44, starting transfers between devices: none -> 47.2 us  [the longest x36 39.5 us: exchange(): return lax.ppermute(value, 'tok', chip_pairs(axis, which))]
    pallas_call x0 -> x11, Pallas kernels: none -> 34.6 us  [the longest x2 11.3 us: latent_grads(): pl.pallas_call(functools.partial(grads_body, scale), grid_spec=pltpu.Pref...]
    dot_general x5 -> x4, matrix products: 36.3 us -> 4.32 us  [dot(): lax.dot_general(a, b, (((ca,), (cb,)), ((), ())), preferred_element_type=...]
    all_to_all x0 -> x2, starting transfers between devices: none -> 12.6 us  [along_layers(): return lax.all_to_all(value, 'layer', 0, 0, tiled=True)]
  transfers between devices with their start and end apart: 5 -> 46, of which waited for: 5 -> 29; matrix products, arithmetic and copies ran while one was open for 0% -> 3% of each run, Pallas kernels for 0% -> 9%
where the time goes in v1:
time: 236 us; the launch traced here: 235 us
  waiting for transfers between devices  122 us (52%)
  starting transfers between devices  59.8 us (25%)
  Pallas kernels  34.6 us (15%)
  local copies, waits for them, and re-layouts  11.8 us (5%)
  matrix products  4.32 us (2%)
    ppermute x36, waiting for transfers between devices, exchange(): return lax.ppermute(value, 'tok', chip_pairs(axis, which))  62 us
    all_to_all x2, waiting for transfers between devices, along_layers(): return lax.all_to_all(value, 'layer', 0, 0, tiled=True)  57 us
    ppermute x36, starting transfers between devices, exchange(): return lax.ppermute(value, 'tok', chip_pairs(axis, which))  39.5 us
    all_to_all x2, starting transfers between devices, along_layers(): return lax.all_to_all(value, 'layer', 0, 0, tiled=True)  12.6 us
    pallas_call x2, Pallas kernels, latent_grads(): pl.pallas_call(functools.partial(grads_body, scale), grid_spec=pltpu.Pref...  11.3 us
    pallas_call x2, Pallas kernels, recon(): pl.pallas_call(functools.partial(recon_body, start), grid_spec=pltpu.Pref...  10.1 us
    unnamed x34, local copies, waits for them, and re-layouts  9.62 us
    pallas_call x1, Pallas kernels, dec_grads(): pl.pallas_call(functools.partial(dec_grad_body, scale), grid=(width // bl...  7.79 us
  transfers between devices with their start and end apart: 46, of which 29 were waited for; matrix products, arithmetic and copies ran while one was open for 3% of the time, Pallas kernels for 9%

profile of v1, /device:TPU:1, one launch (start us, length us, event | category | flops | bytes accessed | tf_op | source)
XLA Modules:
  0.0 235.0 jit_solution(6334007179307795933)
XLA Ops:
  1.7 3.4 %collective-permute-start = (bf16[16,4096]{1,0:T(8,128)(2,1)S(1)}, bf16[16,4096]{1,0:T(8,128)(2,1)S(1)}, u32[]{:S(2)}, u32[]{:S(2)}) collective-permute-start(bf16[16,4096]{1,0:T(8,128)(2,1)S(1)} %get-tuple-element.146), channel_id=1, source_target_pairs={{0,8},{1,25},{2,10},{3,27},{4,12},{5,29},{6,14},{7,31},{8,0},{9,17... | collective-permute-start | bytes 393224 | tf_op jit(solution)/shard_map/ppermute | solution.py:38
  5.1 2.7 %collective-permute-start.2 = (bf16[16,4096]{1,0:T(8,128)(2,1)S(1)}, bf16[16,4096]{1,0:T(8,128)(2,1)S(1)}, u32[]{:S(2)}, u32[]{:S(2)}) collective-permute-start(bf16[16,4096]{1,0:T(8,128)(2,1)S(1)} %get-tuple-element.145), channel_id=1, source_target_pairs={{0,2},{1,7},{2,0},{3,5},{4,6},{5,3},{6,4},{7,1},{8,10},{9,15},{10,... | collective-permute-start | bytes 393224 | tf_op jit(solution)/shard_map/ppermute | solution.py:38
  15.8 2.7 %collective-permute-start.4 = (bf16[32,4096]{1,0:T(8,128)(2,1)S(1)}, bf16[32,4096]{1,0:T(8,128)(2,1)S(1)}, u32[]{:S(2)}, u32[]{:S(2)}) collective-permute-start(bf16[32,4096]{1,0:T(8,128)(2,1)S(1)} %pad_maximum_fusion.8), channel_id=1, source_target_pairs={{0,2},{1,7},{2,0},{3,5},{4,6},{5,3},{6,4},{7,1},{8,10},{9,15},{10,... | collective-permute-start | bytes 786440 | tf_op jit(solution)/shard_map/ppermute | solution.py:38
  22.9 5.0 %collective-permute-start.14 = (bf16[512,4096]{1,0:T(8,128)(2,1)}, bf16[512,4096]{1,0:T(8,128)(2,1)}, u32[]{:S(2)}, u32[]{:S(2)}) collective-permute-start(bf16[512,4096]{1,0:T(8,128)(2,1)} %bitcast.17), channel_id=1, source_target_pairs={{0,1},{1,0},{2,3},{3,2},{4,5},{5,4},{6,7},{7,6},{8,9},{9,8},{10,11... | collective-permute-start | bytes 12582920 | tf_op jit(solution)/shard_map/ppermute | solution.py:42
  41.0 4.7 %collective-permute-done.9.refs_1_ = bf16[64,4096]{1,0:T(8,128)(2,1)S(1)} collective-permute-done((bf16[64,4096]{1,0:T(8,128)(2,1)S(1)}, bf16[64,4096]{1,0:T(8,128)(2,1)S(1)}, u32[]{:S(2)}, u32[]{:S(2)}) %collective-permute-start.9) | collective-permute-done | bytes 524320 | tf_op jit(solution)/shard_map/ppermute | solution.py:38
  45.7 2.9 %collective-permute-done.11.refs_3_ = bf16[64,4096]{1,0:T(8,128)(2,1)S(1)} collective-permute-done((bf16[64,4096]{1,0:T(8,128)(2,1)S(1)}, bf16[64,4096]{1,0:T(8,128)(2,1)S(1)}, u32[]{:S(2)}, u32[]{:S(2)}) %collective-permute-start.11) | collective-permute-done | bytes 524320 | tf_op jit(solution)/shard_map/ppermute | solution.py:38
  52.9 8.2 %all-to-all-start = ((bf16[8,512,128]{2,1,0:T(8,128)(2,1)}), bf16[8,512,128]{2,1,0:T(8,128)(2,1)S(1)}, u32[]{:S(2)}, u32[]{:S(2)}) async-start(bf16[8,512,128]{2,1,0:T(8,128)(2,1)} %broadcast_in_dim.9), calls=%async_computation | async-start | bytes 2097152 | tf_op jit(solution)/shard_map/all_to_all | solution.py:333
  61.1 29.2 %all-to-all-done.lat_ref = bf16[8,512,128]{2,1,0:T(8,128)(2,1)S(1)} async-done(((bf16[8,512,128]{2,1,0:T(8,128)(2,1)}), bf16[8,512,128]{2,1,0:T(8,128)(2,1)S(1)}, u32[]{:S(2)}, u32[]{:S(2)}) %all-to-all-start) | async-done | bytes 1048608 | tf_op jit(solution)/shard_map/all_to_all | solution.py:333
  92.5 5.0 %shard_map.79 = (bf16[64,4096]{1,0:T(8,128)(2,1)S(1)}, bf16[64,4096]{1,0:T(8,128)(2,1)S(1)}, bf16[64,4096]{1,0:T(8,128)(2,1)S(1)}, bf16[64,4096]{1,0:T(8,128)(2,...) custom-call(s32[1]{0:T(128)} %bitcast.layer_ref, bf16[8,512,128]{2,1,0:T(8,128)(2,1)S(1)} %all-to-all-done.lat_ref, ...), custom_call_target="tpu_custom_call" | custom-call | flops 2147483648 | bytes 8388608 | tf_op jit(solution)/shard_map/pallas_call | solution.py:91
  101.0 5.0 %shard_map.78 = (bf16[64,4096]{1,0:T(8,128)(2,1)S(1)}, bf16[64,4096]{1,0:T(8,128)(2,1)S(1)}, bf16[64,4096]{1,0:T(8,128)(2,1)S(1)}, bf16[64,4096]{1,0:T(8,128)(2,...) custom-call(s32[1]{0:T(128)} %bitcast.layer_ref, bf16[8,512,128]{2,1,0:T(8,128)(2,1)S(1)} %all-to-all-done.lat_ref, ...), custom_call_target="tpu_custom_call" | custom-call | flops 2147483648 | bytes 8388608 | tf_op jit(solution)/shard_map/pallas_call | solution.py:91
  107.4 3.4 %collective-permute-done.15.refs_4_ = bf16[64,4096]{1,0:T(8,128)(2,1)S(1)} collective-permute-done((bf16[64,4096]{1,0:T(8,128)(2,1)S(1)}, bf16[64,4096]{1,0:T(8,128)(2,1)S(1)}, u32[]{:S(2)}, u32[]{:S(2)}) %collective-permute-start.15) | collective-permute-done | bytes 524320 | tf_op jit(solution)/shard_map/ppermute | solution.py:38
  110.8 3.4 %collective-permute-done.16.refs_5_ = bf16[64,4096]{1,0:T(8,128)(2,1)S(1)} collective-permute-done((bf16[64,4096]{1,0:T(8,128)(2,1)S(1)}, bf16[64,4096]{1,0:T(8,128)(2,1)S(1)}, u32[]{:S(2)}, u32[]{:S(2)}) %collective-permute-start.16) | collective-permute-done | bytes 524320 | tf_op jit(solution)/shard_map/ppermute | solution.py:38
  117.0 5.8 %collective-permute-done.19.refs_4_ = bf16[32,4096]{1,0:T(8,128)(2,1)S(1)} collective-permute-done((bf16[32,4096]{1,0:T(8,128)(2,1)S(1)}, bf16[32,4096]{1,0:T(8,128)(2,1)S(1)}, u32[]{:S(2)}, u32[]{:S(2)}) %collective-permute-start.19) | collective-permute-done | bytes 262176 | tf_op jit(solution)/shard_map/ppermute | solution.py:38
  125.0 2.7 %collective-permute-start.24 = (bf16[64,2048]{1,0:T(8,128)(2,1)S(1)}, bf16[64,2048]{1,0:T(8,128)(2,1)S(1)}, u32[]{:S(2)}, u32[]{:S(2)}) collective-permute-start(bf16[64,2048]{1,0:T(8,128)(2,1)S(1)} %get-tuple-element.110), channel_id=1, source_target_pairs={{0,8},{1,25},{2,10},{3,27},{4,12},{5,29},{6,14},{7,31},{8,0},{9,17... | collective-permute-start | bytes 786440 | tf_op jit(solution)/shard_map/ppermute | solution.py:38
  133.3 4.7 %collective-permute-done.26.refs_5_ = bf16[64,2048]{1,0:T(8,128)(2,1)S(1)} collective-permute-done((bf16[64,2048]{1,0:T(8,128)(2,1)S(1)}, bf16[64,2048]{1,0:T(8,128)(2,1)S(1)}, u32[]{:S(2)}, u32[]{:S(2)}) %collective-permute-start.26) | collective-permute-done | bytes 262176 | tf_op jit(solution)/shard_map/ppermute | solution.py:38
  140.0 5.7 %collective-permute-done.27.refs_2_ = bf16[64,2048]{1,0:T(8,128)(2,1)S(1)} collective-permute-done((bf16[64,2048]{1,0:T(8,128)(2,1)S(1)}, bf16[64,2048]{1,0:T(8,128)(2,1)S(1)}, u32[]{:S(2)}, u32[]{:S(2)}) %collective-permute-start.27) | collective-permute-done | bytes 262176 | tf_op jit(solution)/shard_map/ppermute | solution.py:38
  148.7 2.9 %collective-permute-start.35 = (bf16[32,4096]{1,0:T(8,128)(2,1)S(1)}, bf16[32,4096]{1,0:T(8,128)(2,1)S(1)}, u32[]{:S(2)}, u32[]{:S(2)}) collective-permute-start(bf16[32,4096]{1,0:T(8,128)(2,1)S(1)} %get-tuple-element.126), channel_id=1, source_target_pairs={{0,8},{1,25},{2,10},{3,27},{4,12},{5,29},{6,14},{7,31},{8,0},{9,17... | collective-permute-start | bytes 786440 | tf_op jit(solution)/shard_map/ppermute | solution.py:38
  155.7 4.5 %collective-permute-done.36 = bf16[32,4096]{1,0:T(8,128)(2,1)S(1)} collective-permute-done((bf16[32,4096]{1,0:T(8,128)(2,1)S(1)}, bf16[32,4096]{1,0:T(8,128)(2,1)S(1)}, u32[]{:S(2)}, u32[]{:S(2)}) %collective-permute-start.36) | collective-permute-done | bytes 262176 | tf_op jit(solution)/shard_map/ppermute | solution.py:38
  164.5 5.2 %shard_map.84 = (bf16[8,128,256]{2,1,0:T(8,128)(2,1)S(1)}, bf16[256,4096]{1,0:T(8,128)(2,1)S(1)}) custom-call(s32[1]{0:T(128)} %bitcast.layer_ref, bf16[512,4096]{1,0:T(8,128)(2,1)S(1)} %bitcast.20, bf16[512,4096]{1,0:T(8,128)(2,1)} %collective-permute-done.14.other_dec, bf16[64,4096]{1,0:T(8,128)(2,1)S(1)} %pad_maximum_fusion.4.refs_0_, ...), custom_call_target="tpu_custom_call" | custom-call | flops 2147483648 | bytes 8388608 | tf_op jit(solution)/shard_map/pallas_call | solution.py:144
  171.5 5.1 %collective-permute-done.38.refs_1_ = bf16[64,4096]{1,0:T(8,128)(2,1)S(1)} collective-permute-done((bf16[64,4096]{1,0:T(8,128)(2,1)S(1)}, bf16[64,4096]{1,0:T(8,128)(2,1)S(1)}, u32[]{:S(2)}, u32[]{:S(2)}) %collective-permute-start.38) | collective-permute-done | bytes 524320 | tf_op jit(solution)/shard_map/ppermute | solution.py:38
  178.4 6.1 %shard_map.85 = (bf16[8,128,512]{2,1,0:T(8,128)(2,1)}, bf16[256,4096]{1,0:T(8,128)(2,1)S(1)}) custom-call(s32[1]{0:T(128)} %bitcast.layer_ref, bf16[512,4096]{1,0:T(8,128)(2,1)S(1)} %bitcast.21, bf16[512,4096]{1,0:T(8,128)(2,1)} %collective-permute-done.14.other_dec, bf16[64,4096]{1,0:T(8,128)(2,1)S(1)} %collective-permute-done.37.refs_0_, ...), custom_call_target="tpu_custom_call" | custom-call | flops 2147483648 | bytes 8388608 | tf_op jit(solution)/shard_map/pallas_call | solution.py:144
  185.8 4.4 %all-to-all-start.1 = ((bf16[8,128,512]{2,1,0:T(8,128)(2,1)}), bf16[8,128,512]{2,1,0:T(8,128)(2,1)}, u32[]{:S(2)}, u32[]{:S(2)}) async-start(bf16[8,128,512]{2,1,0:T(8,128)(2,1)} %get-tuple-element.140), calls=%async_computation.1 | async-start | bytes 2097152 | tf_op jit(solution)/shard_map/all_to_all | solution.py:333
  191.5 27.8 %all-to-all-done.1 = bf16[8,128,512]{2,1,0:T(8,128)(2,1)} async-done(((bf16[8,128,512]{2,1,0:T(8,128)(2,1)}), bf16[8,128,512]{2,1,0:T(8,128)(2,1)}, u32[]{:S(2)}, u32[]{:S(2)}) %all-to-all-start.1) | async-done | bytes 1048608 | tf_op jit(solution)/shard_map/all_to_all | solution.py:333
  225.9 7.8 %shard_map.86 = bf16[512,4096]{1,0:T(8,128)(2,1)} custom-call(bf16[256,512]{1,0:T(8,128)(2,1)S(1)} %copy-done.13, bf16[256,512]{1,0:T(8,128)(2,1)S(1)} %get-tuple-element.121.refs_1_, bf16[256,512]{1,0:T(8,128)(2,1)S(1)} %collective-permute-done.31.refs_2_, bf16[256,512]{1,0:T(8,128)(2,1)S(1)} %collective-permute-done.32.refs_3_, ...), custom_call_target="tpu_custom_call" | custom-call | flops 4294967296 | bytes 12582912 | tf_op jit(solution)/shard_map/pallas_call | solution.py:224
  (133 shorter events, 75.5 us)
Async XLA Ops:
  18.5 14.3 %collective-permute-start.13 = (f32[1,64]{1,0:T(1,128)}, f32[1,64]{1,0:T(1,128)S(1)}, u32[]{:S(2)}, u32[]{:S(2)}) collective-permute-start(f32[1,64]{1,0:T(1,128)} %param.8), channel_id=1, source_target_pairs={{0,1},{1,0},{2,3},{3,2},{4,5},{5,4},{6,7},{7,6},{8,9},{9,8},{10,11... | collective-permute-start | bytes 776 | tf_op jit(solution)/shard_map/ppermute | solution.py:42
  19.2 8.8 %collective-permute-start.5 = (bf16[32,4096]{1,0:T(8,128)(2,1)S(1)}, bf16[32,4096]{1,0:T(8,128)(2,1)S(1)}, u32[]{:S(2)}, u32[]{:S(2)}) collective-permute-start(bf16[32,4096]{1,0:T(8,128)(2,1)S(1)} %collective-permute-done.1), channel_id=1, source_target_pairs={{0,6},{1,3},{2,4},{3,1},{4,2},{5,7},{6,0},{7,5},{8,14},{9,11},{10,... | collective-permute-start | bytes 786440 | tf_op jit(solution)/shard_map/ppermute | solution.py:38
  22.9 67.4 %collective-permute-start.14 = (bf16[512,4096]{1,0:T(8,128)(2,1)}, bf16[512,4096]{1,0:T(8,128)(2,1)}, u32[]{:S(2)}, u32[]{:S(2)}) collective-permute-start(bf16[512,4096]{1,0:T(8,128)(2,1)} %bitcast.17), channel_id=1, source_target_pairs={{0,1},{1,0},{2,3},{3,2},{4,5},{5,4},{6,7},{7,6},{8,9},{9,8},{10,11... | collective-permute-start | bytes 12582920 | tf_op jit(solution)/shard_map/ppermute | solution.py:42
  30.4 10.7 %collective-permute-start.8 = (bf16[64,4096]{1,0:T(8,128)(2,1)S(1)}, bf16[64,4096]{1,0:T(8,128)(2,1)S(1)}, u32[]{:S(2)}, u32[]{:S(2)}) collective-permute-start(bf16[64,4096]{1,0:T(8,128)(2,1)S(1)} %pad_maximum_fusion.refs_0_), channel_id=1, source_target_pairs={{0,6},{1,3},{2,4},{3,1},{4,2},{5,7},{6,0},{7,5},{8,14},{9,11},{10,... | collective-permute-start | bytes 1572872 | tf_op jit(solution)/shard_map/ppermute | solution.py:38
  30.9 14.9 %collective-permute-start.9 = (bf16[64,4096]{1,0:T(8,128)(2,1)S(1)}, bf16[64,4096]{1,0:T(8,128)(2,1)S(1)}, u32[]{:S(2)}, u32[]{:S(2)}) collective-permute-start(bf16[64,4096]{1,0:T(8,128)(2,1)S(1)} %pad_maximum_fusion.1.refs_1_), channel_id=1, source_target_pairs={{0,2},{1,7},{2,0},{3,5},{4,6},{5,3},{6,4},{7,1},{8,10},{9,15},{10,... | collective-permute-start | bytes 1572872 | tf_op jit(solution)/shard_map/ppermute | solution.py:38
  32.8 12.9 %collective-permute-start.10 = (bf16[64,4096]{1,0:T(8,128)(2,1)S(1)}, bf16[64,4096]{1,0:T(8,128)(2,1)S(1)}, u32[]{:S(2)}, u32[]{:S(2)}) collective-permute-start(bf16[64,4096]{1,0:T(8,128)(2,1)S(1)} %pad_maximum_fusion.2.refs_2_), channel_id=1, source_target_pairs={{0,24},{1,9},{2,26},{3,11},{4,28},{5,13},{6,30},{7,15},{8,16},{9,1... | collective-permute-start | bytes 1572872 | tf_op jit(solution)/shard_map/ppermute | solution.py:38
  35.3 13.3 %collective-permute-start.11 = (bf16[64,4096]{1,0:T(8,128)(2,1)S(1)}, bf16[64,4096]{1,0:T(8,128)(2,1)S(1)}, u32[]{:S(2)}, u32[]{:S(2)}) collective-permute-start(bf16[64,4096]{1,0:T(8,128)(2,1)S(1)} %pad_maximum_fusion.3.refs_3_), channel_id=1, source_target_pairs={{0,8},{1,25},{2,10},{3,27},{4,12},{5,29},{6,14},{7,31},{8,0},{9,17... | collective-permute-start | bytes 1572872 | tf_op jit(solution)/shard_map/ppermute | solution.py:38
  52.9 37.4 %all-to-all-start = ((bf16[8,512,128]{2,1,0:T(8,128)(2,1)}), bf16[8,512,128]{2,1,0:T(8,128)(2,1)S(1)}, u32[]{:S(2)}, u32[]{:S(2)}) async-start(bf16[8,512,128]{2,1,0:T(8,128)(2,1)} %broadcast_in_dim.9), calls=%async_computation | async-start | bytes 2097152 | tf_op jit(solution)/shard_map/all_to_all | solution.py:333
  98.2 12.6 %collective-permute-start.15 = (bf16[64,4096]{1,0:T(8,128)(2,1)S(1)}, bf16[64,4096]{1,0:T(8,128)(2,1)S(1)}, u32[]{:S(2)}, u32[]{:S(2)}) collective-permute-start(bf16[64,4096]{1,0:T(8,128)(2,1)S(1)} %get-tuple-element.95), channel_id=1, source_target_pairs={{0,6},{1,3},{2,4},{3,1},{4,2},{5,7},{6,0},{7,5},{8,14},{9,11},{10,... | collective-permute-start | bytes 1572872 | tf_op jit(solution)/shard_map/ppermute | solution.py:38
  99.1 15.1 %collective-permute-start.16 = (bf16[64,4096]{1,0:T(8,128)(2,1)S(1)}, bf16[64,4096]{1,0:T(8,128)(2,1)S(1)}, u32[]{:S(2)}, u32[]{:S(2)}) collective-permute-start(bf16[64,4096]{1,0:T(8,128)(2,1)S(1)} %get-tuple-element.96), channel_id=1, source_target_pairs={{0,2},{1,7},{2,0},{3,5},{4,6},{5,3},{6,4},{7,1},{8,10},{9,15},{10,... | collective-permute-start | bytes 1572872 | tf_op jit(solution)/shard_map/ppermute | solution.py:38
  100.4 13.9 %collective-permute-start.17 = (bf16[64,4096]{1,0:T(8,128)(2,1)S(1)}, bf16[64,4096]{1,0:T(8,128)(2,1)S(1)}, u32[]{:S(2)}, u32[]{:S(2)}) collective-permute-start(bf16[64,4096]{1,0:T(8,128)(2,1)S(1)} %get-tuple-element.97), channel_id=1, source_target_pairs={{0,24},{1,9},{2,26},{3,11},{4,28},{5,13},{6,30},{7,15},{8,16},{9,1... | collective-permute-start | bytes 1572872 | tf_op jit(solution)/shard_map/ppermute | solution.py:38
  100.4 14.3 %collective-permute-start.18 = (bf16[64,4096]{1,0:T(8,128)(2,1)S(1)}, bf16[64,4096]{1,0:T(8,128)(2,1)S(1)}, u32[]{:S(2)}, u32[]{:S(2)}) collective-permute-start(bf16[64,4096]{1,0:T(8,128)(2,1)S(1)} %get-tuple-element.98), channel_id=1, source_target_pairs={{0,8},{1,25},{2,10},{3,27},{4,12},{5,29},{6,14},{7,31},{8,0},{9,17... | collective-permute-start | bytes 1572872 | tf_op jit(solution)/shard_map/ppermute | solution.py:38
  128.7 9.2 %collective-permute-start.26 = (bf16[64,2048]{1,0:T(8,128)(2,1)S(1)}, bf16[64,2048]{1,0:T(8,128)(2,1)S(1)}, u32[]{:S(2)}, u32[]{:S(2)}) collective-permute-start(bf16[64,2048]{1,0:T(8,128)(2,1)S(1)} %get-tuple-element.112), channel_id=1, source_target_pairs={{0,2},{1,7},{2,0},{3,5},{4,6},{5,3},{6,4},{7,1},{8,10},{9,15},{10,... | collective-permute-start | bytes 786440 | tf_op jit(solution)/shard_map/ppermute | solution.py:38
  151.6 8.6 %collective-permute-start.36 = (bf16[32,4096]{1,0:T(8,128)(2,1)S(1)}, bf16[32,4096]{1,0:T(8,128)(2,1)S(1)}, u32[]{:S(2)}, u32[]{:S(2)}) collective-permute-start(bf16[32,4096]{1,0:T(8,128)(2,1)S(1)} %get-tuple-element.127), channel_id=1, source_target_pairs={{0,24},{1,9},{2,26},{3,11},{4,28},{5,13},{6,30},{7,15},{8,16},{9,1... | collective-permute-start | bytes 786440 | tf_op jit(solution)/shard_map/ppermute | solution.py:38
  160.2 11.3 %collective-permute-start.37 = (bf16[64,4096]{1,0:T(8,128)(2,1)S(1)}, bf16[64,4096]{1,0:T(8,128)(2,1)S(1)}, u32[]{:S(2)}, u32[]{:S(2)}) collective-permute-start(bf16[64,4096]{1,0:T(8,128)(2,1)S(1)} %pad_maximum_fusion.4.refs_0_), channel_id=1, source_target_pairs={{0,6},{1,3},{2,4},{3,1},{4,2},{5,7},{6,0},{7,5},{8,14},{9,11},{10,... | collective-permute-start | bytes 1572872 | tf_op jit(solution)/shard_map/ppermute | solution.py:38
  161.5 15.1 %collective-permute-start.38 = (bf16[64,4096]{1,0:T(8,128)(2,1)S(1)}, bf16[64,4096]{1,0:T(8,128)(2,1)S(1)}, u32[]{:S(2)}, u32[]{:S(2)}) collective-permute-start(bf16[64,4096]{1,0:T(8,128)(2,1)S(1)} %pad_maximum_fusion.5.refs_1_), channel_id=1, source_target_pairs={{0,2},{1,7},{2,0},{3,5},{4,6},{5,3},{6,4},{7,1},{8,10},{9,15},{10,... | collective-permute-start | bytes 1572872 | tf_op jit(solution)/shard_map/ppermute | solution.py:38
  162.8 13.8 %collective-permute-start.39 = (bf16[64,4096]{1,0:T(8,128)(2,1)S(1)}, bf16[64,4096]{1,0:T(8,128)(2,1)S(1)}, u32[]{:S(2)}, u32[]{:S(2)}) collective-permute-start(bf16[64,4096]{1,0:T(8,128)(2,1)S(1)} %pad_maximum_fusion.6.refs_2_), channel_id=1, source_target_pairs={{0,24},{1,9},{2,26},{3,11},{4,28},{5,13},{6,30},{7,15},{8,16},{9,1... | collective-permute-start | bytes 1572872 | tf_op jit(solution)/shard_map/ppermute | solution.py:38
  163.5 14.9 %collective-permute-start.40 = (bf16[64,4096]{1,0:T(8,128)(2,1)S(1)}, bf16[64,4096]{1,0:T(8,128)(2,1)S(1)}, u32[]{:S(2)}, u32[]{:S(2)}) collective-permute-start(bf16[64,4096]{1,0:T(8,128)(2,1)S(1)} %pad_maximum_fusion.7.refs_3_), channel_id=1, source_target_pairs={{0,8},{1,25},{2,10},{3,27},{4,12},{5,29},{6,14},{7,31},{8,0},{9,17... | collective-permute-start | bytes 1572872 | tf_op jit(solution)/shard_map/ppermute | solution.py:38
  185.8 33.6 %all-to-all-start.1 = ((bf16[8,128,512]{2,1,0:T(8,128)(2,1)}), bf16[8,128,512]{2,1,0:T(8,128)(2,1)}, u32[]{:S(2)}, u32[]{:S(2)}) async-start(bf16[8,128,512]{2,1,0:T(8,128)(2,1)} %get-tuple-element.140), calls=%async_computation.1 | async-start | bytes 2097152 | tf_op jit(solution)/shard_map/all_to_all | solution.py:333
  190.2 34.8 %collective-permute-start.41 = (bf16[256,4096]{1,0:T(8,128)(2,1)}, bf16[256,4096]{1,0:T(8,128)(2,1)}, u32[]{:S(2)}, u32[]{:S(2)}) collective-permute-start(bf16[256,4096]{1,0:T(8,128)(2,1)} %copy-done.6), channel_id=1, source_target_pairs={{0,1},{1,0},{2,3},{3,2},{4,5},{5,4},{6,7},{7,6},{8,9},{9,8},{10,11... | collective-permute-start | bytes 6291464 | tf_op jit(solution)/shard_map/ppermute | solution.py:42
  190.9 34.1 %collective-permute-start.42 = (bf16[256,4096]{1,0:T(8,128)(2,1)}, bf16[256,4096]{1,0:T(8,128)(2,1)}, u32[]{:S(2)}, u32[]{:S(2)}) collective-permute-start(bf16[256,4096]{1,0:T(8,128)(2,1)} %copy-done.8), channel_id=1, source_target_pairs={{0,1},{1,0},{2,3},{3,2},{4,5},{5,4},{6,7},{7,6},{8,9},{9,8},{10,11... | collective-permute-start | bytes 6291464 | tf_op jit(solution)/shard_map/ppermute | solution.py:42
  191.0 33.9 %collective-permute-start.32 = (bf16[256,512]{1,0:T(8,128)(2,1)S(1)}, bf16[256,512]{1,0:T(8,128)(2,1)S(1)}, u32[]{:S(2)}, u32[]{:S(2)}) collective-permute-start(bf16[256,512]{1,0:T(8,128)(2,1)S(1)} %copy-done.11), channel_id=1, source_target_pairs={{0,1},{1,0},{2,3},{3,2},{4,5},{5,4},{6,7},{7,6},{8,9},{9,8},{10,11... | collective-permute-start | bytes 786440 | tf_op jit(solution)/shard_map/ppermute | solution.py:42
  191.4 33.5 %collective-permute-start.31 = (bf16[256,512]{1,0:T(8,128)(2,1)S(1)}, bf16[256,512]{1,0:T(8,128)(2,1)S(1)}, u32[]{:S(2)}, u32[]{:S(2)}) collective-permute-start(bf16[256,512]{1,0:T(8,128)(2,1)S(1)} %copy-done.15), channel_id=1, source_target_pairs={{0,1},{1,0},{2,3},{3,2},{4,5},{5,4},{6,7},{7,6},{8,9},{9,8},{10,11... | collective-permute-start | bytes 786440 | tf_op jit(solution)/shard_map/ppermute | solution.py:42
  223.4 10.2 %collective-permute-start.43 = (bf16[64,4096]{1,0:T(8,128)(2,1)S(1)}, bf16[64,4096]{1,0:T(8,128)(2,1)S(1)}, u32[]{:S(2)}, u32[]{:S(2)}) collective-permute-start(bf16[64,4096]{1,0:T(8,128)(2,1)S(1)} %fusion.2), channel_id=1, source_target_pairs={{0,1},{1,0},{2,3},{3,2},{4,5},{5,4},{6,7},{7,6},{8,9},{9,8},{10,11... | collective-permute-start | bytes 1572872 | tf_op jit(solution)/shard_map/ppermute | solution.py:42
  (39 other events, 242.9 us)

commit v2 on v1

v2 whole, which is shorter than its diff:
```python
import functools
import math

import jax
import jax.numpy as jnp
from jax import lax
from jax.experimental import pallas as pl
from jax.experimental.pallas import tpu as pltpu
from jax.sharding import PartitionSpec as P

BF = jnp.bfloat16
F32 = jnp.float32
SIDE = 4
VMEM_LIMIT = 16 * 1024 * 1024
MASKS = ((3, 1), (1, 3))
AXES = (("x", "y"), ("y", "x"))


def tok_index(x, y, core):
    return (x * SIDE + y) * 2 + core


def chip_pairs(axis, which):
    pairs = []
    for x in range(SIDE):
        for y in range(SIDE):
            for core in range(2):
                mask = MASKS[core][which]
                px, py = (x ^ mask, y) if axis == "x" else (x, y ^ mask)
                pairs.append((tok_index(x, y, core), tok_index(px, py, core)))
    return pairs


CORE_PAIRS = [(i, i ^ 1) for i in range(2 * SIDE * SIDE)]


def exchange(value, axis, which):
    return lax.ppermute(value, "tok", chip_pairs(axis, which))


def swap_cores(value):
    return lax.ppermute(value, "tok", CORE_PAIRS)


def dot(a, b, ca, cb):
    return lax.dot_general(a, b, (((ca,), (cb,)), ((), ())), preferred_element_type=F32)


def tie(*values):
    return list(lax.optimization_barrier(values))


def params():
    return pltpu.CompilerParams(vmem_limit_bytes=VMEM_LIMIT)


def cost(flops, nbytes):
    return pl.CostEstimate(flops=flops, bytes_accessed=nbytes, transcendentals=0)


def recon_body(start, layer_ref, lat_ref, own_dec, other_dec, *refs):
    outs, (own_ref, other_ref) = refs[:-2], refs[-2:]
    layers, _, both = lat_ref.shape
    tokens = own_ref.shape[0]
    half = both // 2
    block = outs[0].shape[1]

    @pl.when(pl.program_id(0) == 0)
    def _():
        for k, ref in enumerate((own_ref, other_ref)):
            pieces = []
            for s in range(layers):
                piece = lat_ref[s, start : start + tokens, k * half : (k + 1) * half]
                pieces.append(jnp.where(s <= layer_ref[0], piece, jnp.zeros_like(piece)))
            ref[...] = jnp.concatenate(pieces, axis=1)

    columns = pl.ds(pl.multiple_of(pl.program_id(0) * block, block), block)
    part = jnp.dot(own_ref[...], own_dec[...], preferred_element_type=F32)
    part += jnp.dot(other_ref[...], other_dec[:, columns], preferred_element_type=F32)
    part = part.astype(BF)
    rows = outs[0].shape[0]
    for i, out in enumerate(outs):
        out[...] = part[i * rows : (i + 1) * rows]


def recon(layer, latents, start, tokens, decs, streams=2, block=1024):
    depth, width = decs[0].shape
    rows = tokens // streams
    column = lambda i, layer_ref: (0, i)
    whole = lambda i, layer_ref: (0, 0)
    return pl.pallas_call(
        functools.partial(recon_body, start),
        grid_spec=pltpu.PrefetchScalarGridSpec(
            num_scalar_prefetch=1,
            grid=(width // block,),
            in_specs=[
                pl.BlockSpec(memory_space=pltpu.VMEM),
                pl.BlockSpec((depth, block), column),
                pl.BlockSpec(memory_space=pltpu.VMEM),
            ],
            out_specs=[pl.BlockSpec((rows, block), column)] * streams
            + [pl.BlockSpec((tokens, depth), whole)] * 2,
        ),
        out_shape=[jax.ShapeDtypeStruct((rows, width), BF)] * streams
        + [jax.ShapeDtypeStruct((tokens, depth), BF)] * 2,
        compiler_params=params(),
        cost_estimate=cost(4 * tokens * depth * width, 4 * depth * width),
    )(layer, latents, *decs)


def grads_body(scale, layer_ref, own_dec, other_dec, *refs):
    errs, refs = refs[:2], refs[2:]
    before, (out, err_ref), totals = refs[:-4], refs[-4:-2], refs[-2:]
    layers, both, _ = out.shape
    half = both // 2
    tokens, block = err_ref.shape
    at = out.shape[2] - tokens

    @pl.when(pl.program_id(0) == 0)
    def _():
        for total in totals:
            total[...] = jnp.zeros_like(total)

    err = jnp.concatenate([e[...] for e in errs], axis=0)
    err_ref[...] = err
    columns = pl.ds(pl.multiple_of(pl.program_id(0) * block, block), block)
    totals[0][...] += dot(own_dec[...], err, 1, 1)
    totals[1][...] += dot(other_dec[:, columns], err, 1, 1)

    @pl.when(pl.program_id(0) == pl.num_programs(0) - 1)
    def _():
        for s in range(layers):
            for k, total in enumerate(totals):
                value = scale * total[s * half : (s + 1) * half, :]
                value = jnp.where(s <= layer_ref[0], value, 0.0)
                out[s, k * half : (k + 1) * half, at:] = value.astype(BF)
        for ref in before:
            out[:, :, :at] = ref[...]


def latent_grads(layer, decs, errs, before, scale, layers, block=1024):
    depth, width = decs[0].shape
    rows = errs[0].shape[0]
    tokens = rows * len(errs)
    both = 2 * depth // layers
    span = tokens + sum(b.shape[2] for b in before)
    column = lambda i, layer_ref: (0, i)
    return pl.pallas_call(
        functools.partial(grads_body, scale),
        grid_spec=pltpu.PrefetchScalarGridSpec(
            num_scalar_prefetch=1,
            grid=(width // block,),
            in_specs=[pl.BlockSpec((depth, block), column), pl.BlockSpec(memory_space=pltpu.VMEM)]
            + [pl.BlockSpec((rows, block), column)] * len(errs)
            + [pl.BlockSpec(memory_space=pltpu.VMEM)] * len(before),
            out_specs=[
                pl.BlockSpec((layers, both, span), lambda i, layer_ref: (0, 0, 0)),
                pl.BlockSpec((tokens, block), column),
            ],
            scratch_shapes=[pltpu.VMEM((depth, tokens), F32)] * 2,
        ),
        out_shape=[
            jax.ShapeDtypeStruct((layers, both, span), BF),
            jax.ShapeDtypeStruct((tokens, width), BF),
        ],
        compiler_params=params(),
        cost_estimate=cost(4 * tokens * depth * width, 4 * depth * width),
    )(layer, *decs, *errs, *before)


def encode_body(count, *refs):
    blocks, (own, other, bias), refs = refs[:count], refs[count : count + 3], refs[count + 3 :]
    before, (latents, mask, tokens, total) = refs[:-4], refs[-4:]

    @pl.when(pl.program_id(0) == 0)
    def _():
        total[...] = jnp.zeros_like(total)

    value = jnp.concatenate([b[...] for b in blocks], axis=0)
    tokens[...] = value
    total[...] += dot(value, jnp.concatenate([own[...], other[...]], axis=0), 1, 1)

    @pl.when(pl.program_id(0) == pl.num_programs(0) - 1)
    def _():
        pre = total[...] + bias[...]
        value = jnp.maximum(pre, 0.0).astype(BF)
        mask[...] = jnp.where(pre > 0, 1.0, 0.0).T.astype(BF)
        if before:
            at = before[0].shape[0]
            for i in range(latents.shape[0]):
                latents[i, :at, :] = before[0][...]
                latents[i, at:, :] = value
        else:
            latents[...] = value


def encode(blocks, encs, bias, before=(), layers=0, block=1024):
    rows, width = blocks[0].shape
    count = rows * len(blocks)
    both = bias.shape[1]
    column = lambda i: (0, i)
    whole = lambda i: (0, 0)
    if before:
        shape = (layers, before[0].shape[0] + count, both)
        spec = pl.BlockSpec(shape, lambda i: (0, 0, 0))
    else:
        shape = (count, both)
        spec = pl.BlockSpec(shape, whole)
    return pl.pallas_call(
        functools.partial(encode_body, len(blocks)),
        grid=(width // block,),
        in_specs=[pl.BlockSpec((rows, block), column)] * len(blocks)
        + [pl.BlockSpec((both // 2, block), column)] * 2
        + [pl.BlockSpec((1, both), whole)]
        + [pl.BlockSpec(b.shape, whole) for b in before],
        out_specs=[
            spec,
            pl.BlockSpec((both, count), whole),
            pl.BlockSpec((count, block), column),
        ],
        out_shape=[
            jax.ShapeDtypeStruct(shape, BF),
            jax.ShapeDtypeStruct((both, count), BF),
            jax.ShapeDtypeStruct((count, width), BF),
        ],
        scratch_shapes=[pltpu.VMEM((count, both), F32)],
        compiler_params=params(),
        cost_estimate=cost(2 * count * both * width, 4 * count * width),
    )(*blocks, *encs, bias, *before)


def dec_grad_body(scale, *refs):
    lats, errs, out = refs[:4], refs[4:8], refs[8]
    total = dot(lats[0][...], errs[0][...], 0, 0)
    for lat, err in zip(lats[1:], errs[1:]):
        total += dot(lat[...], err[...], 0, 0)
    out[...] = (scale * total).astype(BF)


def dec_grads(lats, errs, scale, block=1024):
    tokens, depth = lats[0].shape
    width = errs[0].shape[1]
    return pl.pallas_call(
        functools.partial(dec_grad_body, scale),
        grid=(width // block,),
        in_specs=[pl.BlockSpec((tokens, depth), lambda i: (0, 0))] * 4
        + [pl.BlockSpec((tokens, block), lambda i: (0, i))] * 4,
        out_specs=pl.BlockSpec((depth, block), lambda i: (0, i)),
        out_shape=jax.ShapeDtypeStruct((depth, width), BF),
        compiler_params=params(),
        cost_estimate=cost(8 * tokens * depth * width, 8 * tokens * width + 2 * depth * width),
    )(*lats, *errs)


def vmem_call(body, outs, *operands):
    spec = pl.BlockSpec(memory_space=pltpu.VMEM)
    return pl.pallas_call(
        body,
        in_specs=[spec] * len(operands),
        out_specs=[spec] * len(outs),
        out_shape=[jax.ShapeDtypeStruct(shape, dtype) for shape, dtype in outs],
        compiler_params=params(),
        cost_estimate=cost(
            sum(o.size for o in operands), sum(o.size * o.dtype.itemsize for o in operands)
        ),
    )(*operands)


def add_half_body(*refs):
    keep, got, send, rest = refs[:2], refs[2:4], refs[4:6], refs[6:8]
    for k, g, s, r in zip(keep, got, send, rest):
        total = k[...].astype(F32) + g[...].astype(F32)
        span = s.shape[0]
        s[...] = total[span:].astype(BF)
        r[...] = total[:span]


ORDERS = ((1, 0, 3, 2), (2, 3, 0, 1))


def group_body(which, *refs):
    before, got, target, totals, sends = refs[:2], refs[2:4], refs[4], refs[5:7], refs[7:9]
    part = target.shape[0] // 2
    for c in range(2):
        value = before[c][...] + got[c][...].astype(F32)
        totals[c][...] = value
        own = target[c * part : (c + 1) * part, :].astype(F32)
        for i, b in enumerate(ORDERS[which]):
            block = value[b * part : (b + 1) * part]
            if b == 0:
                block = block - own
            sends[c][i * part : (i + 1) * part, :] = block.astype(BF)


def finish_body(*refs):
    before, got, target, rebuilt, errs = refs[:2], refs[2:4], refs[4], refs[5], refs[6:8]
    part = target.shape[0] // 2
    for c in range(2):
        rows = slice(c * part, (c + 1) * part)
        value = before[c][...] + got[c][...].astype(F32)
        rebuilt[rows, :] = value[:part].astype(BF)
        own = value[:part] - target[rows, :].astype(F32)
        errs[c][...] = jnp.concatenate([own, value[part:]], axis=0).astype(BF)


def per_device(acts, targets, enc_weight, enc_bias, dec_weight):
    layers = lax.axis_size("layer")
    layer_arr = lax.axis_index("layer").astype(jnp.int32).reshape(1)
    own_tokens, width = acts.shape[1:]
    tokens_all = own_tokens * lax.axis_size("tok")
    grad_scale = 1.0 / math.sqrt(tokens_all)
    rows = enc_weight.shape[1]
    part = own_tokens // 2
    chunks = range(2)

    def in_group(values, which):
        return [exchange(v, AXES[c][0], which) for c, v in zip(chunks, values)]

    def across(values, which):
        return [exchange(v, AXES[c][1], which) for c, v in zip(chunks, values)]

    def join(values, others):
        return [jnp.concatenate(pair, axis=0) for pair in zip(values, others)]

    group = [acts[0, c * part : (c + 1) * part] for c in chunks]
    bias = jnp.concatenate([enc_bias, swap_cores(enc_bias)], axis=1)
    group = join(group, in_group(group, 0))
    group = join(group, in_group(group, 1))
    *group, enc_own = tie(*group, enc_weight[0])
    encs = [enc_own, swap_cores(enc_own)]
    near = join(group, across(group, 0))
    *near, dec_own = tie(*near, dec_weight[0])
    decs = [dec_own.reshape(layers * rows, width)]
    decs.append(swap_cores(decs[0]))
    far = across(near, 1)

    def along_layers(value):
        return lax.all_to_all(value, "layer", 0, 0, tiled=True)

    near_latents, near_mask, near_acts = encode(near, encs, bias)
    *far, near_latents = tie(*far, near_latents)
    latents, far_mask, far_acts = encode(far, encs, bias, [near_latents], layers)
    latents = along_layers(latents)
    span = near_latents.shape[0]

    *send, far_own, far_other = recon(layer_arr, latents, span, span, decs)
    far_swapped = swap_cores(far_other)
    send, far_swapped = tie(send, far_swapped)
    got = across(send, 1)
    *keep, near_own, near_other = recon(layer_arr, latents, 0, span, decs)
    target = targets[0]
    half = ((4 * part, width), BF)
    sums = ((4 * part, width), F32)
    out = vmem_call(add_half_body, [half] * 2 + [sums] * 2, *keep, *got)
    others = [swap_cores(near_other), far_swapped]
    body = lambda which: functools.partial(group_body, which)
    out = vmem_call(body(1), [sums] * 2 + [half] * 2, *out[2:], *across(out[:2], 0), target)
    out = vmem_call(body(0), [sums] * 2 + [half] * 2, *out[:2], *in_group(out[2:], 1), target)
    outs = [((own_tokens, width), BF)] + [half] * 2
    rebuilt, *errs = vmem_call(finish_body, outs, *out[:2], *in_group(out[2:], 0), target)
    near = tie(*join(errs, across(errs, 0)))
    far = across(near, 1)

    near_partial, near_err = latent_grads(layer_arr, decs, near, [], grad_scale, layers)
    far, near_partial, near_err = tie(far, near_partial, near_err)
    partial, far_err = latent_grads(layer_arr, decs, far, [near_partial], grad_scale, layers)
    grad = along_layers(partial)

    lats = [near_own, others[0], far_own, others[1]]
    errs = [near_err, swap_cores(near_err), far_err, swap_cores(far_err)]
    dec_grad = dec_grads(lats, errs, grad_scale).reshape(layers, rows, width)
    grad, dec_grad = tie(grad, dec_grad)

    mask = jnp.concatenate([near_mask, far_mask], axis=1).astype(F32)
    grad = (jnp.sum(grad.astype(F32), axis=0) * mask).astype(BF)
    near_grad, far_grad = grad[:, :span], grad[:, span:]

    def enc_part(which):
        return dot(near_grad[which], near_acts, 1, 0) + dot(far_grad[which], far_acts, 1, 0)

    got = swap_cores(enc_part(slice(rows, None)).astype(BF))
    enc_grad = (enc_part(slice(0, rows)) + got.astype(F32)).astype(BF)
    return (rebuilt[None], dec_grad[None], enc_grad[None])


def solution(mesh):
    return jax.shard_map(
        per_device,
        mesh=mesh,
        in_specs=(
            P("layer", "tok", None),
            P("layer", "tok", None),
            P("layer", "tok", None),
            P("layer", "tok"),
            P("layer", None, "tok", None),
        ),
        out_specs=(P("layer", "tok", None), P("layer", None, "tok", None), P("layer", "tok", None)),
        check_vma=False,
    )
```

time: 236 us -> 228 us (0.966)
  Pallas kernels: 34.6 us -> 41.7 us
  local copies, waits for them, and re-layouts: 11.8 us -> 5.99 us
  waiting for transfers between devices: 122 us -> 117 us
  starting transfers between devices: 59.8 us -> 55.4 us
    ppermute x36 -> x20, starting transfers between devices: 39.5 us -> 26.5 us  [exchange(): return lax.ppermute(value, 'tok', chip_pairs(axis, which))]
    all_to_all x2, waiting for transfers between devices: 57 us -> 46.6 us  [along_layers(): return lax.all_to_all(value, 'layer', 0, 0, tiled=True)]
    ppermute x8, starting transfers between devices: 7.78 us -> 16.4 us  [swap_cores(): return lax.ppermute(value, 'tok', CORE_PAIRS)]
    ppermute x8, waiting for transfers between devices: 2.54 us -> 7.6 us  [swap_cores(): return lax.ppermute(value, 'tok', CORE_PAIRS)]
    unnamed x34 -> x24, local copies, waits for them, and re-layouts: 9.62 us -> 5 us
    pallas_call x2, Pallas kernels: 11.3 us -> 15.2 us  [latent_grads(): pl.pallas_call(functools.partial(grads_body, scale), grid_spec=pltpu.Pref...]
    pallas_call x2, Pallas kernels: 10.1 us -> 12.6 us  [recon(): pl.pallas_call(functools.partial(recon_body, start), grid_spec=pltpu.Pref...]
    ppermute x36 -> x20, waiting for transfers between devices: 62 us -> 62.9 us  [exchange(): return lax.ppermute(value, 'tok', chip_pairs(axis, which))]
  transfers between devices with their start and end apart: 46 -> 30, of which waited for: 29 -> 25; matrix products, arithmetic and copies ran while one was open for 3% -> 0% of each run, Pallas kernels for 9% -> 11%
where the time goes in v2:
time: 228 us; the launch traced here: 227 us
  waiting for transfers between devices  117 us (51%)
  starting transfers between devices  55.4 us (24%)
  Pallas kernels  41.7 us (18%)
  local copies, waits for them, and re-layouts  5.99 us (3%)
  matrix products  4.32 us (2%)
    ppermute x20, waiting for transfers between devices, exchange(): return lax.ppermute(value, 'tok', chip_pairs(axis, which))  62.9 us
    all_to_all x2, waiting for transfers between devices, along_layers(): return lax.all_to_all(value, 'layer', 0, 0, tiled=True)  46.6 us
    ppermute x20, starting transfers between devices, exchange(): return lax.ppermute(value, 'tok', chip_pairs(axis, which))  26.5 us
    ppermute x8, starting transfers between devices, swap_cores(): return lax.ppermute(value, 'tok', CORE_PAIRS)  16.4 us
    pallas_call x2, Pallas kernels, latent_grads(): pl.pallas_call(functools.partial(grads_body, scale), grid_spec=pltpu.Pref...  15.2 us
    pallas_call x2, Pallas kernels, recon(): pl.pallas_call(functools.partial(recon_body, start), grid_spec=pltpu.Pref...  12.6 us
    all_to_all x2, starting transfers between devices, along_layers(): return lax.all_to_all(value, 'layer', 0, 0, tiled=True)  12.5 us
    pallas_call x1, Pallas kernels, dec_grads(): pl.pallas_call(functools.partial(dec_grad_body, scale), grid=(width // bl...  8.42 us
  transfers between devices with their start and end apart: 30, of which 25 were waited for; matrix products, arithmetic and copies ran while one was open for 0% of the time, Pallas kernels for 11%

profile of v2, /device:TPU:1, one launch (start us, length us, event | category | flops | bytes accessed | tf_op | source)
XLA Modules:
  0.0 227.3 jit_solution(14139203328914674562)
XLA Ops:
  6.2 3.0 %collective-permute-start.3 = (bf16[32,4096]{1,0:T(8,128)(2,1)S(1)}, bf16[32,4096]{1,0:T(8,128)(2,1)S(1)}, u32[]{:S(2)}, u32[]{:S(2)}) collective-permute-start(bf16[32,4096]{1,0:T(8,128)(2,1)S(1)} %pad_maximum_fusion.7), channel_id=1, source_target_pairs={{0,2},{1,7},{2,0},{3,5},{4,6},{5,3},{6,4},{7,1},{8,10},{9,15},{10,... | collective-permute-start | bytes 786440 | tf_op jit(solution)/shard_map/ppermute | solution.py:38
  9.2 2.6 %collective-permute-start.1 = (bf16[32,4096]{1,0:T(8,128)(2,1)S(1)}, bf16[32,4096]{1,0:T(8,128)(2,1)S(1)}, u32[]{:S(2)}, u32[]{:S(2)}) collective-permute-start(bf16[32,4096]{1,0:T(8,128)(2,1)S(1)} %pad_maximum_fusion.6), channel_id=1, source_target_pairs={{0,8},{1,25},{2,10},{3,27},{4,12},{5,29},{6,14},{7,31},{8,0},{9,17... | collective-permute-start | bytes 786440 | tf_op jit(solution)/shard_map/ppermute | solution.py:38
  16.6 7.6 %collective-permute-done.4 = bf16[64,4096]{1,0:T(8,128)(2,1)S(1)} collective-permute-done((bf16[64,4096]{1,0:T(8,128)(2,1)S(1)}, bf16[64,4096]{1,0:T(8,128)(2,1)S(1)}, u32[]{:S(2)}, u32[]{:S(2)}) %collective-permute-start.4) | collective-permute-done | bytes 524320 | tf_op jit(solution)/shard_map/ppermute | solution.py:38
  24.5 7.2 %collective-permute-start.10 = (bf16[512,4096]{1,0:T(8,128)(2,1)}, bf16[512,4096]{1,0:T(8,128)(2,1)}, u32[]{:S(2)}, u32[]{:S(2)}) collective-permute-start(bf16[512,4096]{1,0:T(8,128)(2,1)} %bitcast.5.own_dec), channel_id=1, source_target_pairs={{0,1},{1,0},{2,3},{3,2},{4,5},{5,4},{6,7},{7,6},{8,9},{9,8},{10,11... | collective-permute-start | bytes 12582920 | tf_op jit(solution)/shard_map/ppermute | solution.py:42
  32.6 2.5 %collective-permute-start.7 = (bf16[128,4096]{1,0:T(8,128)(2,1)S(1)}, bf16[128,4096]{1,0:T(8,128)(2,1)S(1)}, u32[]{:S(2)}, u32[]{:S(2)}) collective-permute-start(bf16[128,4096]{1,0:T(8,128)(2,1)S(1)} %pad_maximum_fusion.1.refs_1_), channel_id=1, source_target_pairs={{0,8},{1,25},{2,10},{3,27},{4,12},{5,29},{6,14},{7,31},{8,0},{9,17... | collective-permute-start | bytes 3145736 | tf_op jit(solution)/shard_map/ppermute | solution.py:38
  35.6 3.6 %collective-permute-done.9 = f32[1,64]{1,0:T(1,128)S(1)} collective-permute-done((f32[1,64]{1,0:T(1,128)S(1)}, f32[1,64]{1,0:T(1,128)S(1)}, u32[]{:S(2)}, u32[]{:S(2)}) %collective-permute-start.9) | collective-permute-done | bytes 288 | tf_op jit(solution)/shard_map/ppermute | solution.py:42
  41.0 5.5 %collective-permute-done.6.refs_0_ = bf16[128,4096]{1,0:T(8,128)(2,1)S(1)} collective-permute-done((bf16[128,4096]{1,0:T(8,128)(2,1)S(1)}, bf16[128,4096]{1,0:T(8,128)(2,1)S(1)}, u32[]{:S(2)}, u32[]{:S(2)}) %collective-permute-start.6) | collective-permute-done | bytes 1048608 | tf_op jit(solution)/shard_map/ppermute | solution.py:38
  51.6 8.2 %all-to-all-start = ((bf16[8,512,128]{2,1,0:T(8,128)(2,1)}), bf16[8,512,128]{2,1,0:T(8,128)(2,1)S(1)}, u32[]{:S(2)}, u32[]{:S(2)}) async-start(bf16[8,512,128]{2,1,0:T(8,128)(2,1)} %copy-done.4), calls=%async_computation | async-start | bytes 2097152 | tf_op jit(solution)/shard_map/all_to_all | solution.py:338
  59.7 28.6 %all-to-all-done.lat_ref = bf16[8,512,128]{2,1,0:T(8,128)(2,1)S(1)} async-done(((bf16[8,512,128]{2,1,0:T(8,128)(2,1)}), bf16[8,512,128]{2,1,0:T(8,128)(2,1)S(1)}, u32[]{:S(2)}, u32[]{:S(2)}) %all-to-all-start) | async-done | bytes 1048608 | tf_op jit(solution)/shard_map/all_to_all | solution.py:338
  88.3 6.3 %shard_map.79 = (bf16[128,4096]{1,0:T(8,128)(2,1)S(1)}, bf16[128,4096]{1,0:T(8,128)(2,1)S(1)}, bf16[256,512]{1,0:T(8,128)(2,1)S(1)}, bf16[256,512]{1,0:T(8,128)(2,1)S(1)}) custom-call(s32[1]{0:T(128)} %bitcast.layer_ref, bf16[8,512,128]{2,1,0:T(8,128)(2,1)S(1)} %all-to-all-done.lat_ref, bf16[512,4096]{1,0:T(8,128)(2,1)} %bitcast.5.own_dec, ...), custom_call_target="tpu_custom_call" | custom-call | flops 2147483648 | bytes 8388608 | tf_op jit(solution)/shard_map/pallas_call | solution.py:91
  100.3 6.3 %shard_map.78 = (bf16[128,4096]{1,0:T(8,128)(2,1)S(1)}, bf16[128,4096]{1,0:T(8,128)(2,1)S(1)}, bf16[256,512]{1,0:T(8,128)(2,1)S(1)}, bf16[256,512]{1,0:T(8,128)(2,1)S(1)}) custom-call(s32[1]{0:T(128)} %bitcast.layer_ref, bf16[8,512,128]{2,1,0:T(8,128)(2,1)S(1)} %all-to-all-done.lat_ref, bf16[512,4096]{1,0:T(8,128)(2,1)} %bitcast.5.own_dec, ...), custom_call_target="tpu_custom_call" | custom-call | flops 2147483648 | bytes 8388608 | tf_op jit(solution)/shard_map/pallas_call | solution.py:91
  108.0 3.9 %collective-permute-done.12.refs_2_ = bf16[128,4096]{1,0:T(8,128)(2,1)S(1)} collective-permute-done((bf16[128,4096]{1,0:T(8,128)(2,1)S(1)}, bf16[128,4096]{1,0:T(8,128)(2,1)S(1)}, u32[]{:S(2)}, u32[]{:S(2)}) %collective-permute-start.12) | collective-permute-done | bytes 1048608 | tf_op jit(solution)/shard_map/ppermute | solution.py:38
  113.6 8.0 %collective-permute-done.14.refs_2_ = bf16[64,4096]{1,0:T(8,128)(2,1)S(1)} collective-permute-done((bf16[64,4096]{1,0:T(8,128)(2,1)S(1)}, bf16[64,4096]{1,0:T(8,128)(2,1)S(1)}, u32[]{:S(2)}, u32[]{:S(2)}) %collective-permute-start.14) | collective-permute-done | bytes 524320 | tf_op jit(solution)/shard_map/ppermute | solution.py:38
  122.2 2.5 %collective-permute-start.16 = (bf16[64,4096]{1,0:T(8,128)(2,1)S(1)}, bf16[64,4096]{1,0:T(8,128)(2,1)S(1)}, u32[]{:S(2)}, u32[]{:S(2)}) collective-permute-start(bf16[64,4096]{1,0:T(8,128)(2,1)S(1)} %get-tuple-element.80), channel_id=1, source_target_pairs={{0,8},{1,25},{2,10},{3,27},{4,12},{5,29},{6,14},{7,31},{8,0},{9,17... | collective-permute-start | bytes 1572872 | tf_op jit(solution)/shard_map/ppermute | solution.py:38
  126.7 4.9 %collective-permute-done.16.refs_2_ = bf16[64,4096]{1,0:T(8,128)(2,1)S(1)} collective-permute-done((bf16[64,4096]{1,0:T(8,128)(2,1)S(1)}, bf16[64,4096]{1,0:T(8,128)(2,1)S(1)}, u32[]{:S(2)}, u32[]{:S(2)}) %collective-permute-start.16) | collective-permute-done | bytes 524320 | tf_op jit(solution)/shard_map/ppermute | solution.py:38
  134.7 8.0 %collective-permute-done.18.refs_2_ = bf16[64,4096]{1,0:T(8,128)(2,1)S(1)} collective-permute-done((bf16[64,4096]{1,0:T(8,128)(2,1)S(1)}, bf16[64,4096]{1,0:T(8,128)(2,1)S(1)}, u32[]{:S(2)}, u32[]{:S(2)}) %collective-permute-start.18) | collective-permute-done | bytes 524320 | tf_op jit(solution)/shard_map/ppermute | solution.py:38
  145.3 6.4 %collective-permute-done.20 = bf16[64,4096]{1,0:T(8,128)(2,1)S(1)} collective-permute-done((bf16[64,4096]{1,0:T(8,128)(2,1)S(1)}, bf16[64,4096]{1,0:T(8,128)(2,1)S(1)}, u32[]{:S(2)}, u32[]{:S(2)}) %collective-permute-start.20) | collective-permute-done | bytes 524320 | tf_op jit(solution)/shard_map/ppermute | solution.py:38
  155.3 7.4 %shard_map.84 = (bf16[8,128,256]{2,1,0:T(8,128)(2,1)S(1)}, bf16[256,4096]{1,0:T(8,128)(2,1)}) custom-call(s32[1]{0:T(128)} %bitcast.layer_ref, bf16[512,4096]{1,0:T(8,128)(2,1)} %bitcast.5.own_dec, bf16[512,4096]{1,0:T(8,128)(2,1)} %collective-permute-done.10.other_dec, bf16[128,4096]{1,0:T(8,128)(2,1)S(1)} %pad_maximum_fusion.2.refs_0_, ...), custom_call_target="tpu_custom_call" | custom-call | flops 2147483648 | bytes 8388608 | tf_op jit(solution)/shard_map/pallas_call | solution.py:148
  162.7 7.2 %collective-permute-done.22.refs_0_ = bf16[128,4096]{1,0:T(8,128)(2,1)S(1)} collective-permute-done((bf16[128,4096]{1,0:T(8,128)(2,1)S(1)}, bf16[128,4096]{1,0:T(8,128)(2,1)S(1)}, u32[]{:S(2)}, u32[]{:S(2)}) %collective-permute-start.22) | collective-permute-done | bytes 1048608 | tf_op jit(solution)/shard_map/ppermute | solution.py:38
  171.5 7.7 %shard_map.85 = (bf16[8,128,512]{2,1,0:T(8,128)(2,1)}, bf16[256,4096]{1,0:T(8,128)(2,1)}) custom-call(s32[1]{0:T(128)} %bitcast.layer_ref, bf16[512,4096]{1,0:T(8,128)(2,1)} %bitcast.5.own_dec, bf16[512,4096]{1,0:T(8,128)(2,1)} %collective-permute-done.10.other_dec, bf16[128,4096]{1,0:T(8,128)(2,1)S(1)} %collective-permute-done.22.refs_0_, ...), custom_call_target="tpu_custom_call" | custom-call | flops 2147483648 | bytes 8388608 | tf_op jit(solution)/shard_map/pallas_call | solution.py:148
  179.2 7.1 %collective-permute-start.26 = (bf16[256,4096]{1,0:T(8,128)(2,1)}, bf16[256,4096]{1,0:T(8,128)(2,1)}, u32[]{:S(2)}, u32[]{:S(2)}) collective-permute-start(bf16[256,4096]{1,0:T(8,128)(2,1)} %get-tuple-element.102.refs_6_), channel_id=1, source_target_pairs={{0,1},{1,0},{2,3},{3,2},{4,5},{5,4},{6,7},{7,6},{8,9},{9,8},{10,11... | collective-permute-start | bytes 6291464 | tf_op jit(solution)/shard_map/ppermute | solution.py:42
  186.4 4.3 %all-to-all-start.1 = ((bf16[8,128,512]{2,1,0:T(8,128)(2,1)}), bf16[8,128,512]{2,1,0:T(8,128)(2,1)}, u32[]{:S(2)}, u32[]{:S(2)}) async-start(bf16[8,128,512]{2,1,0:T(8,128)(2,1)} %get-tuple-element.96), calls=%async_computation.1 | async-start | bytes 2097152 | tf_op jit(solution)/shard_map/all_to_all | solution.py:338
  193.5 8.4 %shard_map.86 = bf16[512,4096]{1,0:T(8,128)(2,1)} custom-call(bf16[256,512]{1,0:T(8,128)(2,1)S(1)} %copy-done.8, bf16[256,512]{1,0:T(8,128)(2,1)S(1)} %collective-permute-done.24.refs_1_, bf16[256,512]{1,0:T(8,128)(2,1)S(1)} %get-tuple-element.99.refs_2_, bf16[256,512]{1,0:T(8,128)(2,1)S(1)} %copy-done.6, bf16[256,4096]{1,0:T(8,128)(2,1)} %get-tuple-element.101.refs_4_, ...), custom_call_target="tpu_custom_call" | custom-call | flops 4294967296 | bytes 12582912 | tf_op jit(solution)/shard_map/pallas_call | solution.py:243
  201.9 18.0 %all-to-all-done.1 = bf16[8,128,512]{2,1,0:T(8,128)(2,1)} async-done(((bf16[8,128,512]{2,1,0:T(8,128)(2,1)}), bf16[8,128,512]{2,1,0:T(8,128)(2,1)}, u32[]{:S(2)}, u32[]{:S(2)}) %all-to-all-start.1) | async-done | bytes 1048608 | tf_op jit(solution)/shard_map/all_to_all | solution.py:338
  (87 shorter events, 51.4 us)
Async XLA Ops:
  3.8 5.4 %collective-permute-start = (bf16[16,4096]{1,0:T(8,128)(2,1)S(1)}, bf16[16,4096]{1,0:T(8,128)(2,1)S(1)}, u32[]{:S(2)}, u32[]{:S(2)}) collective-permute-start(bf16[16,4096]{1,0:T(8,128)(2,1)S(1)} %get-tuple-element.110), channel_id=1, source_target_pairs={{0,24},{1,9},{2,26},{3,11},{4,28},{5,13},{6,30},{7,15},{8,16},{9,1... | collective-permute-start | bytes 393224 | tf_op jit(solution)/shard_map/ppermute | solution.py:38
  6.2 7.0 %collective-permute-start.3 = (bf16[32,4096]{1,0:T(8,128)(2,1)S(1)}, bf16[32,4096]{1,0:T(8,128)(2,1)S(1)}, u32[]{:S(2)}, u32[]{:S(2)}) collective-permute-start(bf16[32,4096]{1,0:T(8,128)(2,1)S(1)} %pad_maximum_fusion.7), channel_id=1, source_target_pairs={{0,2},{1,7},{2,0},{3,5},{4,6},{5,3},{6,4},{7,1},{8,10},{9,15},{10,... | collective-permute-start | bytes 786440 | tf_op jit(solution)/shard_map/ppermute | solution.py:38
  9.2 6.5 %collective-permute-start.1 = (bf16[32,4096]{1,0:T(8,128)(2,1)S(1)}, bf16[32,4096]{1,0:T(8,128)(2,1)S(1)}, u32[]{:S(2)}, u32[]{:S(2)}) collective-permute-start(bf16[32,4096]{1,0:T(8,128)(2,1)S(1)} %pad_maximum_fusion.6), channel_id=1, source_target_pairs={{0,8},{1,25},{2,10},{3,27},{4,12},{5,29},{6,14},{7,31},{8,0},{9,17... | collective-permute-start | bytes 786440 | tf_op jit(solution)/shard_map/ppermute | solution.py:38
  15.8 8.4 %collective-permute-start.4 = (bf16[64,4096]{1,0:T(8,128)(2,1)S(1)}, bf16[64,4096]{1,0:T(8,128)(2,1)S(1)}, u32[]{:S(2)}, u32[]{:S(2)}) collective-permute-start(bf16[64,4096]{1,0:T(8,128)(2,1)S(1)} %pad_maximum_fusion.4), channel_id=1, source_target_pairs={{0,6},{1,3},{2,4},{3,1},{4,2},{5,7},{6,0},{7,5},{8,14},{9,11},{10,... | collective-permute-start | bytes 1572872 | tf_op jit(solution)/shard_map/ppermute | solution.py:38
  16.0 8.3 %collective-permute-start.5 = (bf16[64,4096]{1,0:T(8,128)(2,1)S(1)}, bf16[64,4096]{1,0:T(8,128)(2,1)S(1)}, u32[]{:S(2)}, u32[]{:S(2)}) collective-permute-start(bf16[64,4096]{1,0:T(8,128)(2,1)S(1)} %pad_maximum_fusion.5), channel_id=1, source_target_pairs={{0,24},{1,9},{2,26},{3,11},{4,28},{5,13},{6,30},{7,15},{8,16},{9,1... | collective-permute-start | bytes 1572872 | tf_op jit(solution)/shard_map/ppermute | solution.py:38
  24.5 63.9 %collective-permute-start.10 = (bf16[512,4096]{1,0:T(8,128)(2,1)}, bf16[512,4096]{1,0:T(8,128)(2,1)}, u32[]{:S(2)}, u32[]{:S(2)}) collective-permute-start(bf16[512,4096]{1,0:T(8,128)(2,1)} %bitcast.5.own_dec), channel_id=1, source_target_pairs={{0,1},{1,0},{2,3},{3,2},{4,5},{5,4},{6,7},{7,6},{8,9},{9,8},{10,11... | collective-permute-start | bytes 12582920 | tf_op jit(solution)/shard_map/ppermute | solution.py:42
  31.6 14.9 %collective-permute-start.6 = (bf16[128,4096]{1,0:T(8,128)(2,1)S(1)}, bf16[128,4096]{1,0:T(8,128)(2,1)S(1)}, u32[]{:S(2)}, u32[]{:S(2)}) collective-permute-start(bf16[128,4096]{1,0:T(8,128)(2,1)S(1)} %pad_maximum_fusion.refs_0_), channel_id=1, source_target_pairs={{0,2},{1,7},{2,0},{3,5},{4,6},{5,3},{6,4},{7,1},{8,10},{9,15},{10,... | collective-permute-start | bytes 3145736 | tf_op jit(solution)/shard_map/ppermute | solution.py:38
  32.6 14.9 %collective-permute-start.7 = (bf16[128,4096]{1,0:T(8,128)(2,1)S(1)}, bf16[128,4096]{1,0:T(8,128)(2,1)S(1)}, u32[]{:S(2)}, u32[]{:S(2)}) collective-permute-start(bf16[128,4096]{1,0:T(8,128)(2,1)S(1)} %pad_maximum_fusion.1.refs_1_), channel_id=1, source_target_pairs={{0,8},{1,25},{2,10},{3,27},{4,12},{5,29},{6,14},{7,31},{8,0},{9,17... | collective-permute-start | bytes 3145736 | tf_op jit(solution)/shard_map/ppermute | solution.py:38
  51.6 36.8 %all-to-all-start = ((bf16[8,512,128]{2,1,0:T(8,128)(2,1)}), bf16[8,512,128]{2,1,0:T(8,128)(2,1)S(1)}, u32[]{:S(2)}, u32[]{:S(2)}) async-start(bf16[8,512,128]{2,1,0:T(8,128)(2,1)} %copy-done.4), calls=%async_computation | async-start | bytes 2097152 | tf_op jit(solution)/shard_map/all_to_all | solution.py:338
  97.0 14.9 %collective-permute-start.12 = (bf16[128,4096]{1,0:T(8,128)(2,1)S(1)}, bf16[128,4096]{1,0:T(8,128)(2,1)S(1)}, u32[]{:S(2)}, u32[]{:S(2)}) collective-permute-start(bf16[128,4096]{1,0:T(8,128)(2,1)S(1)} %get-tuple-element.72), channel_id=1, source_target_pairs={{0,2},{1,7},{2,0},{3,5},{4,6},{5,3},{6,4},{7,1},{8,10},{9,15},{10,... | collective-permute-start | bytes 3145736 | tf_op jit(solution)/shard_map/ppermute | solution.py:38
  97.8 14.9 %collective-permute-start.13 = (bf16[128,4096]{1,0:T(8,128)(2,1)S(1)}, bf16[128,4096]{1,0:T(8,128)(2,1)S(1)}, u32[]{:S(2)}, u32[]{:S(2)}) collective-permute-start(bf16[128,4096]{1,0:T(8,128)(2,1)S(1)} %get-tuple-element.73), channel_id=1, source_target_pairs={{0,8},{1,25},{2,10},{3,27},{4,12},{5,29},{6,14},{7,31},{8,0},{9,17... | collective-permute-start | bytes 3145736 | tf_op jit(solution)/shard_map/ppermute | solution.py:38
  113.2 8.4 %collective-permute-start.14 = (bf16[64,4096]{1,0:T(8,128)(2,1)S(1)}, bf16[64,4096]{1,0:T(8,128)(2,1)S(1)}, u32[]{:S(2)}, u32[]{:S(2)}) collective-permute-start(bf16[64,4096]{1,0:T(8,128)(2,1)S(1)} %get-tuple-element.76), channel_id=1, source_target_pairs={{0,6},{1,3},{2,4},{3,1},{4,2},{5,7},{6,0},{7,5},{8,14},{9,11},{10,... | collective-permute-start | bytes 1572872 | tf_op jit(solution)/shard_map/ppermute | solution.py:38
  113.3 8.6 %collective-permute-start.15 = (bf16[64,4096]{1,0:T(8,128)(2,1)S(1)}, bf16[64,4096]{1,0:T(8,128)(2,1)S(1)}, u32[]{:S(2)}, u32[]{:S(2)}) collective-permute-start(bf16[64,4096]{1,0:T(8,128)(2,1)S(1)} %get-tuple-element.77), channel_id=1, source_target_pairs={{0,24},{1,9},{2,26},{3,11},{4,28},{5,13},{6,30},{7,15},{8,16},{9,1... | collective-permute-start | bytes 1572872 | tf_op jit(solution)/shard_map/ppermute | solution.py:38
  122.2 9.3 %collective-permute-start.16 = (bf16[64,4096]{1,0:T(8,128)(2,1)S(1)}, bf16[64,4096]{1,0:T(8,128)(2,1)S(1)}, u32[]{:S(2)}, u32[]{:S(2)}) collective-permute-start(bf16[64,4096]{1,0:T(8,128)(2,1)S(1)} %get-tuple-element.80), channel_id=1, source_target_pairs={{0,8},{1,25},{2,10},{3,27},{4,12},{5,29},{6,14},{7,31},{8,0},{9,17... | collective-permute-start | bytes 1572872 | tf_op jit(solution)/shard_map/ppermute | solution.py:38
  124.8 9.2 %collective-permute-start.17 = (bf16[64,4096]{1,0:T(8,128)(2,1)S(1)}, bf16[64,4096]{1,0:T(8,128)(2,1)S(1)}, u32[]{:S(2)}, u32[]{:S(2)}) collective-permute-start(bf16[64,4096]{1,0:T(8,128)(2,1)S(1)} %get-tuple-element.81), channel_id=1, source_target_pairs={{0,2},{1,7},{2,0},{3,5},{4,6},{5,3},{6,4},{7,1},{8,10},{9,15},{10,... | collective-permute-start | bytes 1572872 | tf_op jit(solution)/shard_map/ppermute | solution.py:38
  134.3 8.4 %collective-permute-start.18 = (bf16[64,4096]{1,0:T(8,128)(2,1)S(1)}, bf16[64,4096]{1,0:T(8,128)(2,1)S(1)}, u32[]{:S(2)}, u32[]{:S(2)}) collective-permute-start(bf16[64,4096]{1,0:T(8,128)(2,1)S(1)} %get-tuple-element.84), channel_id=1, source_target_pairs={{0,24},{1,9},{2,26},{3,11},{4,28},{5,13},{6,30},{7,15},{8,16},{9,1... | collective-permute-start | bytes 1572872 | tf_op jit(solution)/shard_map/ppermute | solution.py:38
  134.4 8.4 %collective-permute-start.19 = (bf16[64,4096]{1,0:T(8,128)(2,1)S(1)}, bf16[64,4096]{1,0:T(8,128)(2,1)S(1)}, u32[]{:S(2)}, u32[]{:S(2)}) collective-permute-start(bf16[64,4096]{1,0:T(8,128)(2,1)S(1)} %get-tuple-element.85), channel_id=1, source_target_pairs={{0,6},{1,3},{2,4},{3,1},{4,2},{5,7},{6,0},{7,5},{8,14},{9,11},{10,... | collective-permute-start | bytes 1572872 | tf_op jit(solution)/shard_map/ppermute | solution.py:38
  143.7 8.0 %collective-permute-start.20 = (bf16[64,4096]{1,0:T(8,128)(2,1)S(1)}, bf16[64,4096]{1,0:T(8,128)(2,1)S(1)}, u32[]{:S(2)}, u32[]{:S(2)}) collective-permute-start(bf16[64,4096]{1,0:T(8,128)(2,1)S(1)} %get-tuple-element.87), channel_id=1, source_target_pairs={{0,6},{1,3},{2,4},{3,1},{4,2},{5,7},{6,0},{7,5},{8,14},{9,11},{10,... | collective-permute-start | bytes 1572872 | tf_op jit(solution)/shard_map/ppermute | solution.py:38
  143.9 8.0 %collective-permute-start.21 = (bf16[64,4096]{1,0:T(8,128)(2,1)S(1)}, bf16[64,4096]{1,0:T(8,128)(2,1)S(1)}, u32[]{:S(2)}, u32[]{:S(2)}) collective-permute-start(bf16[64,4096]{1,0:T(8,128)(2,1)S(1)} %get-tuple-element.88), channel_id=1, source_target_pairs={{0,24},{1,9},{2,26},{3,11},{4,28},{5,13},{6,30},{7,15},{8,16},{9,1... | collective-permute-start | bytes 1572872 | tf_op jit(solution)/shard_map/ppermute | solution.py:38
  152.0 17.8 %collective-permute-start.22 = (bf16[128,4096]{1,0:T(8,128)(2,1)S(1)}, bf16[128,4096]{1,0:T(8,128)(2,1)S(1)}, u32[]{:S(2)}, u32[]{:S(2)}) collective-permute-start(bf16[128,4096]{1,0:T(8,128)(2,1)S(1)} %pad_maximum_fusion.2.refs_0_), channel_id=1, source_target_pairs={{0,2},{1,7},{2,0},{3,5},{4,6},{5,3},{6,4},{7,1},{8,10},{9,15},{10,... | collective-permute-start | bytes 3145736 | tf_op jit(solution)/shard_map/ppermute | solution.py:38
  154.1 17.4 %collective-permute-start.23 = (bf16[128,4096]{1,0:T(8,128)(2,1)S(1)}, bf16[128,4096]{1,0:T(8,128)(2,1)S(1)}, u32[]{:S(2)}, u32[]{:S(2)}) collective-permute-start(bf16[128,4096]{1,0:T(8,128)(2,1)S(1)} %pad_maximum_fusion.3.refs_1_), channel_id=1, source_target_pairs={{0,8},{1,25},{2,10},{3,27},{4,12},{5,29},{6,14},{7,31},{8,0},{9,17... | collective-permute-start | bytes 3145736 | tf_op jit(solution)/shard_map/ppermute | solution.py:38
  179.2 14.2 %collective-permute-start.26 = (bf16[256,4096]{1,0:T(8,128)(2,1)}, bf16[256,4096]{1,0:T(8,128)(2,1)}, u32[]{:S(2)}, u32[]{:S(2)}) collective-permute-start(bf16[256,4096]{1,0:T(8,128)(2,1)} %get-tuple-element.102.refs_6_), channel_id=1, source_target_pairs={{0,1},{1,0},{2,3},{3,2},{4,5},{5,4},{6,7},{7,6},{8,9},{9,8},{10,11... | collective-permute-start | bytes 6291464 | tf_op jit(solution)/shard_map/ppermute | solution.py:42
  186.3 7.2 %collective-permute-start.25 = (bf16[256,4096]{1,0:T(8,128)(2,1)}, bf16[256,4096]{1,0:T(8,128)(2,1)}, u32[]{:S(2)}, u32[]{:S(2)}) collective-permute-start(bf16[256,4096]{1,0:T(8,128)(2,1)} %get-tuple-element.101.refs_4_), channel_id=1, source_target_pairs={{0,1},{1,0},{2,3},{3,2},{4,5},{5,4},{6,7},{7,6},{8,9},{9,8},{10,11... | collective-permute-start | bytes 6291464 | tf_op jit(solution)/shard_map/ppermute | solution.py:42
  186.4 33.5 %all-to-all-start.1 = ((bf16[8,128,512]{2,1,0:T(8,128)(2,1)}), bf16[8,128,512]{2,1,0:T(8,128)(2,1)}, u32[]{:S(2)}, u32[]{:S(2)}) async-start(bf16[8,128,512]{2,1,0:T(8,128)(2,1)} %get-tuple-element.96), calls=%async_computation.1 | async-start | bytes 2097152 | tf_op jit(solution)/shard_map/all_to_all | solution.py:338
  (18 other events, 113.2 us)

commit v3 on v2

--- a/solution.py
+++ b/solution.py
@@ -63,7 +63,6 @@
     layers, _, both = lat_ref.shape
     tokens = own_ref.shape[0]
     half = both // 2
-    block = outs[0].shape[1]
 
     @pl.when(pl.program_id(0) == 0)
     def _():
@@ -74,16 +73,15 @@
                 pieces.append(jnp.where(s <= layer_ref[0], piece, jnp.zeros_like(piece)))
             ref[...] = jnp.concatenate(pieces, axis=1)
 
-    columns = pl.ds(pl.multiple_of(pl.program_id(0) * block, block), block)
     part = jnp.dot(own_ref[...], own_dec[...], preferred_element_type=F32)
-    part += jnp.dot(other_ref[...], other_dec[:, columns], preferred_element_type=F32)
+    part += jnp.dot(other_ref[...], other_dec[...], preferred_element_type=F32)
     part = part.astype(BF)
     rows = outs[0].shape[0]
     for i, out in enumerate(outs):
         out[...] = part[i * rows : (i + 1) * rows]
 
 
-def recon(layer, latents, start, tokens, decs, streams=2, block=1024):
+def recon(layer, latents, start, tokens, decs, streams, block=1024):
     depth, width = decs[0].shape
     rows = tokens // streams
     column = lambda i, layer_ref: (0, i)
@@ -93,11 +91,8 @@
         grid_spec=pltpu.PrefetchScalarGridSpec(
             num_scalar_prefetch=1,
             grid=(width // block,),
-            in_specs=[
-                pl.BlockSpec(memory_space=pltpu.VMEM),
-                pl.BlockSpec((depth, block), column),
-                pl.BlockSpec(memory_space=pltpu.VMEM),
-            ],
+            in_specs=[pl.BlockSpec(memory_space=pltpu.VMEM)]
+            + [pl.BlockSpec((depth, block), column)] * 2,
             out_specs=[pl.BlockSpec((rows, block), column)] * streams
             + [pl.BlockSpec((tokens, depth), whole)] * 2,
         ),
@@ -108,12 +103,12 @@
     )(layer, latents, *decs)
 
 
-def grads_body(scale, layer_ref, own_dec, other_dec, *refs):
-    errs, refs = refs[:2], refs[2:]
+def grads_body(scale, count, layer_ref, own_dec, other_dec, *refs):
+    errs, refs = refs[:count], refs[count:]
     before, (out, err_ref), totals = refs[:-4], refs[-4:-2], refs[-2:]
     layers, both, _ = out.shape
     half = both // 2
-    tokens, block = err_ref.shape
+    tokens = err_ref.shape[0]
     at = out.shape[2] - tokens
 
     @pl.when(pl.program_id(0) == 0)
@@ -123,9 +118,8 @@
 
     err = jnp.concatenate([e[...] for e in errs], axis=0)
     err_ref[...] = err
-    columns = pl.ds(pl.multiple_of(pl.program_id(0) * block, block), block)
     totals[0][...] += dot(own_dec[...], err, 1, 1)
-    totals[1][...] += dot(other_dec[:, columns], err, 1, 1)
+    totals[1][...] += dot(other_dec[...], err, 1, 1)
 
     @pl.when(pl.program_id(0) == pl.num_programs(0) - 1)
     def _():
@@ -146,11 +140,11 @@
     span = tokens + sum(b.shape[2] for b in before)
     column = lambda i, layer_ref: (0, i)
     return pl.pallas_call(
-        functools.partial(grads_body, scale),
+        functools.partial(grads_body, scale, len(errs)),
         grid_spec=pltpu.PrefetchScalarGridSpec(
             num_scalar_prefetch=1,
             grid=(width // block,),
-            in_specs=[pl.BlockSpec((depth, block), column), pl.BlockSpec(memory_space=pltpu.VMEM)]
+            in_specs=[pl.BlockSpec((depth, block), column)] * 2
             + [pl.BlockSpec((rows, block), column)] * len(errs)
             + [pl.BlockSpec(memory_space=pltpu.VMEM)] * len(before),
             out_specs=[
@@ -238,13 +232,13 @@
 
 
 def dec_grads(lats, errs, scale, block=1024):
-    tokens, depth = lats[0].shape
-    width = errs[0].shape[1]
+    tokens = sum(lat.shape[0] for lat in lats) // 4
+    depth, width = lats[0].shape[1], errs[0].shape[1]
     return pl.pallas_call(
         functools.partial(dec_grad_body, scale),
         grid=(width // block,),
-        in_specs=[pl.BlockSpec((tokens, depth), lambda i: (0, 0))] * 4
-        + [pl.BlockSpec((tokens, block), lambda i: (0, i))] * 4,
+        in_specs=[pl.BlockSpec(lat.shape, lambda i: (0, 0)) for lat in lats]
+        + [pl.BlockSpec((err.shape[0], block), lambda i: (0, i)) for err in errs],
         out_specs=pl.BlockSpec((depth, block), lambda i: (0, i)),
         out_shape=jax.ShapeDtypeStruct((depth, width), BF),
         compiler_params=params(),
@@ -266,23 +260,21 @@
     )(*operands)
 
 
-def add_half_body(*refs):
-    keep, got, send, rest = refs[:2], refs[2:4], refs[4:6], refs[6:8]
-    for k, g, s, r in zip(keep, got, send, rest):
-        total = k[...].astype(F32) + g[...].astype(F32)
-        span = s.shape[0]
-        s[...] = total[span:].astype(BF)
-        r[...] = total[:span]
+def add_body(*refs):
+    count = len(refs) // 3
+    for a, b, out in zip(refs[:count], refs[count : 2 * count], refs[2 * count :]):
+        out[...] = (a[...].astype(F32) + b[...].astype(F32)).astype(out.dtype)
 
 
 ORDERS = ((1, 0, 3, 2), (2, 3, 0, 1))
 
 
 def group_body(which, *refs):
-    before, got, target, totals, sends = refs[:2], refs[2:4], refs[4], refs[5:7], refs[7:9]
+    terms, (target, *outs) = refs[:-5], refs[-5:]
+    totals, sends = outs[:2], outs[2:]
     part = target.shape[0] // 2
     for c in range(2):
-        value = before[c][...] + got[c][...].astype(F32)
+        value = sum(t[...].astype(F32) for t in terms[c::2])
         totals[c][...] = value
         own = target[c * part : (c + 1) * part, :].astype(F32)
         for i, b in enumerate(ORDERS[which]):
@@ -326,57 +318,61 @@
     bias = jnp.concatenate([enc_bias, swap_cores(enc_bias)], axis=1)
     group = join(group, in_group(group, 0))
     group = join(group, in_group(group, 1))
-    *group, enc_own = tie(*group, enc_weight[0])
+    *group, enc_own, dec_own = tie(*group, enc_weight[0], dec_weight[0])
     encs = [enc_own, swap_cores(enc_own)]
-    near = join(group, across(group, 0))
-    *near, dec_own = tie(*near, dec_weight[0])
     decs = [dec_own.reshape(layers * rows, width)]
-    decs.append(swap_cores(decs[0]))
-    far = across(near, 1)
+
+    def spread(group):
+        direct = across(group, 0)
+        early = [*group, *direct, *across(group, 1)]
+        return early, across(direct, 1)
+
+    early, late = spread(group)
+    *early, dec_own = tie(*early, decs[0])
+    decs.append(swap_cores(dec_own))
 
     def along_layers(value):
         return lax.all_to_all(value, "layer", 0, 0, tiled=True)
 
-    near_latents, near_mask, near_acts = encode(near, encs, bias)
-    *far, near_latents = tie(*far, near_latents)
-    latents, far_mask, far_acts = encode(far, encs, bias, [near_latents], layers)
+    early_latents, early_mask, early_acts = encode(early, encs, bias)
+    *late, early_latents = tie(*late, early_latents)
+    latents, late_mask, late_acts = encode(late, encs, bias, [early_latents], layers)
     latents = along_layers(latents)
-    span = near_latents.shape[0]
-
-    *send, far_own, far_other = recon(layer_arr, latents, span, span, decs)
-    far_swapped = swap_cores(far_other)
-    send, far_swapped = tie(send, far_swapped)
+    span, count = early_latents.shape[0], late_mask.shape[1]
+
+    *send, late_own, late_other = recon(layer_arr, latents, span, count, decs, 2)
+    late_swapped = swap_cores(late_other)
+    send, late_swapped = tie(send, late_swapped)
     got = across(send, 1)
-    *keep, near_own, near_other = recon(layer_arr, latents, 0, span, decs)
+    *parts, early_own, early_other = recon(layer_arr, latents, 0, span, decs, 6)
+    others = [swap_cores(early_other), late_swapped]
     target = targets[0]
     half = ((4 * part, width), BF)
     sums = ((4 * part, width), F32)
-    out = vmem_call(add_half_body, [half] * 2 + [sums] * 2, *keep, *got)
-    others = [swap_cores(near_other), far_swapped]
+    send = vmem_call(add_body, [half] * 2, *parts[2:4], *got)
+    got = across(send, 0) + across(parts[4:], 1)
     body = lambda which: functools.partial(group_body, which)
-    out = vmem_call(body(1), [sums] * 2 + [half] * 2, *out[2:], *across(out[:2], 0), target)
+    out = vmem_call(body(1), [sums] * 2 + [half] * 2, *parts[:2], *got, target)
     out = vmem_call(body(0), [sums] * 2 + [half] * 2, *out[:2], *in_group(out[2:], 1), target)
     outs = [((own_tokens, width), BF)] + [half] * 2
     rebuilt, *errs = vmem_call(finish_body, outs, *out[:2], *in_group(out[2:], 0), target)
-    near = tie(*join(errs, across(errs, 0)))
-    far = across(near, 1)
-
-    near_partial, near_err = latent_grads(layer_arr, decs, near, [], grad_scale, layers)
-    far, near_partial, near_err = tie(far, near_partial, near_err)
-    partial, far_err = latent_grads(layer_arr, decs, far, [near_partial], grad_scale, layers)
+    early, late = spread(errs)
+    partial, early_err = latent_grads(layer_arr, decs, early, [], grad_scale, layers)
+    late, partial, early_err = tie(late, partial, early_err)
+    partial, late_err = latent_grads(layer_arr, decs, late, [partial], grad_scale, layers)
     grad = along_layers(partial)
 
-    lats = [near_own, others[0], far_own, others[1]]
-    errs = [near_err, swap_cores(near_err), far_err, swap_cores(far_err)]
+    lats = [early_own, others[0], late_own, others[1]]
+    errs = [early_err, swap_cores(early_err), late_err, swap_cores(late_err)]
     dec_grad = dec_grads(lats, errs, grad_scale).reshape(layers, rows, width)
     grad, dec_grad = tie(grad, dec_grad)
 
-    mask = jnp.concatenate([near_mask, far_mask], axis=1).astype(F32)
+    mask = jnp.concatenate([early_mask, late_mask], axis=1).astype(F32)
     grad = (jnp.sum(grad.astype(F32), axis=0) * mask).astype(BF)
-    near_grad, far_grad = grad[:, :span], grad[:, span:]
+    early_grad, late_grad = grad[:, :span], grad[:, span:]
 
     def enc_part(which):
-        return dot(near_grad[which], near_acts, 1, 0) + dot(far_grad[which], far_acts, 1, 0)
+        return dot(early_grad[which], early_acts, 1, 0) + dot(late_grad[which], late_acts, 1, 0)
 
     got = swap_cores(enc_part(slice(rows, None)).astype(BF))
     enc_grad = (enc_part(slice(0, rows)) + got.astype(F32)).astype(BF)

time: 228 us -> 218 us (0.956)
  waiting for transfers between devices: 117 us -> 107 us
  local copies, waits for them, and re-layouts: 5.99 us -> 9.35 us
    ppermute x20 -> x26, waiting for transfers between devices: 62.9 us -> 53.8 us  [exchange(): return lax.ppermute(value, 'tok', chip_pairs(axis, which))]
    all_to_all x2, waiting for transfers between devices: 46.6 us -> 43 us  [along_layers(): return lax.all_to_all(value, 'layer', 0, 0, tiled=True)]
    ppermute x20 -> x26, starting transfers between devices: 26.5 us -> 30.1 us  [exchange(): return lax.ppermute(value, 'tok', chip_pairs(axis, which))]
    ppermute x8, starting transfers between devices: 16.4 us -> 12.9 us  [swap_cores(): return lax.ppermute(value, 'tok', CORE_PAIRS)]
    unnamed x24 -> x28, local copies, waits for them, and re-layouts: 5 us -> 8.31 us
  transfers between devices with their start and end apart: 30 -> 36, of which waited for: 25 -> 25; matrix products, arithmetic and copies ran while one was open for 0% -> 0% of each run, Pallas kernels for 11% -> 15%
where the time goes in v3:
time: 218 us; the launch traced here: 217 us
  waiting for transfers between devices  107 us (49%)
  starting transfers between devices  55.4 us (25%)
  Pallas kernels  39.5 us (18%)
  local copies, waits for them, and re-layouts  9.35 us (4%)
  matrix products  4.15 us (2%)
    ppermute x26, waiting for transfers between devices, exchange(): return lax.ppermute(value, 'tok', chip_pairs(axis, which))  53.8 us
    all_to_all x2, waiting for transfers between devices, along_layers(): return lax.all_to_all(value, 'layer', 0, 0, tiled=True)  43 us
    ppermute x26, starting transfers between devices, exchange(): return lax.ppermute(value, 'tok', chip_pairs(axis, which))  30.1 us
    pallas_call x2, Pallas kernels, latent_grads(): pl.pallas_call(functools.partial(grads_body, scale, len(errs)), grid_spec...  13.3 us
    ppermute x8, starting transfers between devices, swap_cores(): return lax.ppermute(value, 'tok', CORE_PAIRS)  12.9 us
    all_to_all x2, starting transfers between devices, along_layers(): return lax.all_to_all(value, 'layer', 0, 0, tiled=True)  12.4 us
    pallas_call x2, Pallas kernels, recon(): pl.pallas_call(functools.partial(recon_body, start), grid_spec=pltpu.Pref...  11.1 us
    ppermute x8, waiting for transfers between devices, swap_cores(): return lax.ppermute(value, 'tok', CORE_PAIRS)  9.84 us
  transfers between devices with their start and end apart: 36, of which 25 were waited for; matrix products, arithmetic and copies ran while one was open for 0% of the time, Pallas kernels for 15%

profile of v3, /device:TPU:1, one launch (start us, length us, event | category | flops | bytes accessed | tf_op | source)
XLA Modules:
  0.0 217.5 jit_solution(15501053991709384413)
XLA Ops:
  6.3 3.0 %collective-permute-start.3 = (bf16[32,4096]{1,0:T(8,128)(2,1)S(1)}, bf16[32,4096]{1,0:T(8,128)(2,1)S(1)}, u32[]{:S(2)}, u32[]{:S(2)}) collective-permute-start(bf16[32,4096]{1,0:T(8,128)(2,1)S(1)} %pad_maximum_fusion.3), channel_id=1, source_target_pairs={{0,2},{1,7},{2,0},{3,5},{4,6},{5,3},{6,4},{7,1},{8,10},{9,15},{10,... | collective-permute-start | bytes 786440 | tf_op jit(solution)/shard_map/ppermute | solution.py:38
  9.3 2.6 %collective-permute-start.1 = (bf16[32,4096]{1,0:T(8,128)(2,1)S(1)}, bf16[32,4096]{1,0:T(8,128)(2,1)S(1)}, u32[]{:S(2)}, u32[]{:S(2)}) collective-permute-start(bf16[32,4096]{1,0:T(8,128)(2,1)S(1)} %pad_maximum_fusion.2), channel_id=1, source_target_pairs={{0,8},{1,25},{2,10},{3,27},{4,12},{5,29},{6,14},{7,31},{8,0},{9,17... | collective-permute-start | bytes 786440 | tf_op jit(solution)/shard_map/ppermute | solution.py:38
  13.4 2.5 %collective-permute-done.1 = bf16[32,4096]{1,0:T(8,128)(2,1)S(1)} collective-permute-done((bf16[32,4096]{1,0:T(8,128)(2,1)S(1)}, bf16[32,4096]{1,0:T(8,128)(2,1)S(1)}, u32[]{:S(2)}, u32[]{:S(2)}) %collective-permute-start.1) | collective-permute-done | bytes 262176 | tf_op jit(solution)/shard_map/ppermute | solution.py:38
  17.0 2.5 %collective-permute-start.9 = (bf16[64,4096]{1,0:T(8,128)(2,1)S(1)}, bf16[64,4096]{1,0:T(8,128)(2,1)S(1)}, u32[]{:S(2)}, u32[]{:S(2)}) collective-permute-start(bf16[64,4096]{1,0:T(8,128)(2,1)S(1)} %pad_maximum_fusion.1.refs_1_), channel_id=1, source_target_pairs={{0,8},{1,25},{2,10},{3,27},{4,12},{5,29},{6,14},{7,31},{8,0},{9,17... | collective-permute-start | bytes 1572872 | tf_op jit(solution)/shard_map/ppermute | solution.py:38
  19.5 6.8 %collective-permute-done.8.refs_4_ = bf16[64,4096]{1,0:T(8,128)(2,1)S(1)} collective-permute-done((bf16[64,4096]{1,0:T(8,128)(2,1)S(1)}, bf16[64,4096]{1,0:T(8,128)(2,1)S(1)}, u32[]{:S(2)}, u32[]{:S(2)}) %collective-permute-start.8) | collective-permute-done | bytes 524320 | tf_op jit(solution)/shard_map/ppermute | solution.py:38
  27.1 4.0 %collective-permute-done.6.refs_3_ = bf16[64,4096]{1,0:T(8,128)(2,1)S(1)} collective-permute-done((bf16[64,4096]{1,0:T(8,128)(2,1)S(1)}, bf16[64,4096]{1,0:T(8,128)(2,1)S(1)}, u32[]{:S(2)}, u32[]{:S(2)}) %collective-permute-start.6) | collective-permute-done | bytes 524320 | tf_op jit(solution)/shard_map/ppermute | solution.py:38
  31.1 2.7 %collective-permute-start.12 = (bf16[512,4096]{1,0:T(8,128)(2,1)}, bf16[512,4096]{1,0:T(8,128)(2,1)}, u32[]{:S(2)}, u32[]{:S(2)}) collective-permute-start(bf16[512,4096]{1,0:T(8,128)(2,1)} %bitcast.18), channel_id=1, source_target_pairs={{0,1},{1,0},{2,3},{3,2},{4,5},{5,4},{6,7},{7,6},{8,9},{9,8},{10,11... | collective-permute-start | bytes 12582920 | tf_op jit(solution)/shard_map/ppermute | solution.py:42
  36.7 4.7 %collective-permute-done.11 = f32[1,64]{1,0:T(1,128)S(1)} collective-permute-done((f32[1,64]{1,0:T(1,128)S(1)}, f32[1,64]{1,0:T(1,128)S(1)}, u32[]{:S(2)}, u32[]{:S(2)}) %collective-permute-start.11) | collective-permute-done | bytes 288 | tf_op jit(solution)/shard_map/ppermute | solution.py:42
  41.4 2.2 %shard_map.76 = (bf16[384,128]{1,0:T(8,128)(2,1)S(1)}, bf16[128,384]{1,0:T(8,128)(2,1)S(1)}, bf16[384,4096]{1,0:T(8,128)(2,1)S(1)}) custom-call(bf16[64,4096]{1,0:T(8,128)(2,1)S(1)} %pad_maximum_fusion.refs_0_, bf16[64,4096]{1,0:T(8,128)(2,1)S(1)} %pad_maximum_fusion.1.refs_1_, bf16[64,4096]{1,0:T(8,128)(2,1)S(1)} %collective-permute-done.4.refs_2_, ...), custom_call_target="tpu_custom_call" | custom-call | flops 402653184 | bytes 6291456 | tf_op jit(solution)/shard_map/pallas_call | solution.py:203
  48.1 8.2 %all-to-all-start = ((bf16[8,512,128]{2,1,0:T(8,128)(2,1)}), bf16[8,512,128]{2,1,0:T(8,128)(2,1)}, u32[]{:S(2)}, u32[]{:S(2)}) async-start(bf16[8,512,128]{2,1,0:T(8,128)(2,1)} %copy-done.7), calls=%async_computation | async-start | bytes 2097152 | tf_op jit(solution)/shard_map/all_to_all | solution.py:335
  56.3 29.4 %all-to-all-done.lat_ref = bf16[8,512,128]{2,1,0:T(8,128)(2,1)} async-done(((bf16[8,512,128]{2,1,0:T(8,128)(2,1)}), bf16[8,512,128]{2,1,0:T(8,128)(2,1)}, u32[]{:S(2)}, u32[]{:S(2)}) %all-to-all-start) | async-done | bytes 1048608 | tf_op jit(solution)/shard_map/all_to_all | solution.py:335
  87.9 4.6 %shard_map.79 = (bf16[64,4096]{1,0:T(8,128)(2,1)S(1)}, bf16[64,4096]{1,0:T(8,128)(2,1)S(1)}, bf16[128,512]{1,0:T(8,128)(2,1)S(1)}, bf16[128,512]{1,0:T(8,128)(2,1)S(1)}) custom-call(s32[1]{0:T(128)} %bitcast.layer_ref, bf16[8,512,128]{2,1,0:T(8,128)(2,1)} %all-to-all-done.lat_ref, bf16[512,4096]{1,0:T(8,128)(2,1)S(1)} %bitcast.19, ...), custom_call_target="tpu_custom_call" | custom-call | flops 1073741824 | bytes 8388608 | tf_op jit(solution)/shard_map/pallas_call | solution.py:89
  96.2 6.5 %shard_map.78 = (bf16[64,4096]{1,0:T(8,128)(2,1)S(1)}, bf16[64,4096]{1,0:T(8,128)(2,1)S(1)}, bf16[64,4096]{1,0:T(8,128)(2,1)S(1)}, bf16[64,4096]{1,0:T(8,128)(2,...) custom-call(s32[1]{0:T(128)} %bitcast.layer_ref, ...), custom_call_target="tpu_custom_call" | custom-call | flops 3221225472 | bytes 8388608 | tf_op jit(solution)/shard_map/pallas_call | solution.py:89
  106.6 8.3 %collective-permute-done.18.refs_4_ = bf16[64,4096]{1,0:T(8,128)(2,1)S(1)} collective-permute-done((bf16[64,4096]{1,0:T(8,128)(2,1)S(1)}, bf16[64,4096]{1,0:T(8,128)(2,1)S(1)}, u32[]{:S(2)}, u32[]{:S(2)}) %collective-permute-start.18) | collective-permute-done | bytes 524320 | tf_op jit(solution)/shard_map/ppermute | solution.py:38
  120.3 7.1 %collective-permute-done.20.refs_2_ = bf16[64,4096]{1,0:T(8,128)(2,1)S(1)} collective-permute-done((bf16[64,4096]{1,0:T(8,128)(2,1)S(1)}, bf16[64,4096]{1,0:T(8,128)(2,1)S(1)}, u32[]{:S(2)}, u32[]{:S(2)}) %collective-permute-start.20) | collective-permute-done | bytes 524320 | tf_op jit(solution)/shard_map/ppermute | solution.py:38
  129.8 7.8 %collective-permute-done.22.refs_2_ = bf16[64,4096]{1,0:T(8,128)(2,1)S(1)} collective-permute-done((bf16[64,4096]{1,0:T(8,128)(2,1)S(1)}, bf16[64,4096]{1,0:T(8,128)(2,1)S(1)}, u32[]{:S(2)}, u32[]{:S(2)}) %collective-permute-start.22) | collective-permute-done | bytes 524320 | tf_op jit(solution)/shard_map/ppermute | solution.py:38
  142.5 4.5 %collective-permute-done.24.refs_2_ = bf16[64,4096]{1,0:T(8,128)(2,1)S(1)} collective-permute-done((bf16[64,4096]{1,0:T(8,128)(2,1)S(1)}, bf16[64,4096]{1,0:T(8,128)(2,1)S(1)}, u32[]{:S(2)}, u32[]{:S(2)}) %collective-permute-start.24) | collective-permute-done | bytes 524320 | tf_op jit(solution)/shard_map/ppermute | solution.py:38
  151.4 8.1 %shard_map.84 = (bf16[8,128,384]{2,1,0:T(8,128)(2,1)S(1)}, bf16[384,4096]{1,0:T(8,128)(2,1)}) custom-call(s32[1]{0:T(128)} %bitcast.layer_ref, bf16[512,4096]{1,0:T(8,128)(2,1)S(1)} %bitcast.21, bf16[512,4096]{1,0:T(8,128)(2,1)} %collective-permute-done.12.other_dec, bf16[64,4096]{1,0:T(8,128)(2,1)S(1)} %get-tuple-element.99.refs_0_, ...), custom_call_target="tpu_custom_call" | custom-call | flops 3221225472 | bytes 8388608 | tf_op jit(solution)/shard_map/pallas_call | solution.py:142
  161.2 8.2 %collective-permute-start.31 = (bf16[384,4096]{1,0:T(8,128)(2,1)}, bf16[384,4096]{1,0:T(8,128)(2,1)}, u32[]{:S(2)}, u32[]{:S(2)}) collective-permute-start(bf16[384,4096]{1,0:T(8,128)(2,1)} %get-tuple-element.111.refs_4_), channel_id=1, source_target_pairs={{0,1},{1,0},{2,3},{3,2},{4,5},{5,4},{6,7},{7,6},{8,9},{9,8},{10,11... | collective-permute-start | bytes 9437192 | tf_op jit(solution)/shard_map/ppermute | solution.py:42
  169.4 5.2 %shard_map.85 = (bf16[8,128,512]{2,1,0:T(8,128)(2,1)S(1)}, bf16[128,4096]{1,0:T(8,128)(2,1)S(1)}) custom-call(s32[1]{0:T(128)} %bitcast.layer_ref, bf16[512,4096]{1,0:T(8,128)(2,1)S(1)} %bitcast.22, bf16[512,4096]{1,0:T(8,128)(2,1)} %collective-permute-done.12.other_dec, bf16[64,4096]{1,0:T(8,128)(2,1)S(1)} %collective-permute-done.25.refs_0_, ...), custom_call_target="tpu_custom_call" | custom-call | flops 1073741824 | bytes 8388608 | tf_op jit(solution)/shard_map/pallas_call | solution.py:142
  176.6 4.3 %all-to-all-start.1 = ((bf16[8,128,512]{2,1,0:T(8,128)(2,1)}), bf16[8,128,512]{2,1,0:T(8,128)(2,1)}, u32[]{:S(2)}, u32[]{:S(2)}) async-start(bf16[8,128,512]{2,1,0:T(8,128)(2,1)} %copy-done.6), calls=%async_computation.1 | async-start | bytes 2097152 | tf_op jit(solution)/shard_map/all_to_all | solution.py:335
  181.6 2.9 %collective-permute-done.30.refs_1_ = bf16[384,512]{1,0:T(8,128)(2,1)S(1)} collective-permute-done((bf16[384,512]{1,0:T(8,128)(2,1)}, bf16[384,512]{1,0:T(8,128)(2,1)S(1)}, u32[]{:S(2)}, u32[]{:S(2)}) %collective-permute-start.30) | collective-permute-done | bytes 393248 | tf_op jit(solution)/shard_map/ppermute | solution.py:42
  186.8 9.7 %shard_map.86 = bf16[512,4096]{1,0:T(8,128)(2,1)} custom-call(bf16[384,512]{1,0:T(8,128)(2,1)S(1)} %copy-done.12, bf16[384,512]{1,0:T(8,128)(2,1)S(1)} %collective-permute-done.30.refs_1_, bf16[128,512]{1,0:T(8,128)(2,1)S(1)} %get-tuple-element.109.refs_2_, bf16[128,512]{1,0:T(8,128)(2,1)S(1)} %collective-permute-done.13.refs_3_, ...), custom_call_target="tpu_custom_call" | custom-call | flops 4294967296 | bytes 12582912 | tf_op jit(solution)/shard_map/pallas_call | solution.py:237
  196.5 13.6 %all-to-all-done.1 = bf16[8,128,512]{2,1,0:T(8,128)(2,1)} async-done(((bf16[8,128,512]{2,1,0:T(8,128)(2,1)}), bf16[8,128,512]{2,1,0:T(8,128)(2,1)}, u32[]{:S(2)}, u32[]{:S(2)}) %all-to-all-start.1) | async-done | bytes 1048608 | tf_op jit(solution)/shard_map/all_to_all | solution.py:335
  (99 shorter events, 57.4 us)
Async XLA Ops:
  15.9 10.4 %collective-permute-start.8 = (bf16[64,4096]{1,0:T(8,128)(2,1)S(1)}, bf16[64,4096]{1,0:T(8,128)(2,1)S(1)}, u32[]{:S(2)}, u32[]{:S(2)}) collective-permute-start(bf16[64,4096]{1,0:T(8,128)(2,1)S(1)} %pad_maximum_fusion.refs_0_), channel_id=1, source_target_pairs={{0,2},{1,7},{2,0},{3,5},{4,6},{5,3},{6,4},{7,1},{8,10},{9,15},{10,... | collective-permute-start | bytes 1572872 | tf_op jit(solution)/shard_map/ppermute | solution.py:38
  16.4 10.7 %collective-permute-start.4 = (bf16[64,4096]{1,0:T(8,128)(2,1)S(1)}, bf16[64,4096]{1,0:T(8,128)(2,1)S(1)}, u32[]{:S(2)}, u32[]{:S(2)}) collective-permute-start(bf16[64,4096]{1,0:T(8,128)(2,1)S(1)} %pad_maximum_fusion.refs_0_), channel_id=1, source_target_pairs={{0,6},{1,3},{2,4},{3,1},{4,2},{5,7},{6,0},{7,5},{8,14},{9,11},{10,... | collective-permute-start | bytes 1572872 | tf_op jit(solution)/shard_map/ppermute | solution.py:38
  17.0 10.2 %collective-permute-start.9 = (bf16[64,4096]{1,0:T(8,128)(2,1)S(1)}, bf16[64,4096]{1,0:T(8,128)(2,1)S(1)}, u32[]{:S(2)}, u32[]{:S(2)}) collective-permute-start(bf16[64,4096]{1,0:T(8,128)(2,1)S(1)} %pad_maximum_fusion.1.refs_1_), channel_id=1, source_target_pairs={{0,8},{1,25},{2,10},{3,27},{4,12},{5,29},{6,14},{7,31},{8,0},{9,17... | collective-permute-start | bytes 1572872 | tf_op jit(solution)/shard_map/ppermute | solution.py:38
  19.5 11.7 %collective-permute-start.6 = (bf16[64,4096]{1,0:T(8,128)(2,1)S(1)}, bf16[64,4096]{1,0:T(8,128)(2,1)S(1)}, u32[]{:S(2)}, u32[]{:S(2)}) collective-permute-start(bf16[64,4096]{1,0:T(8,128)(2,1)S(1)} %pad_maximum_fusion.1.refs_1_), channel_id=1, source_target_pairs={{0,24},{1,9},{2,26},{3,11},{4,28},{5,13},{6,30},{7,15},{8,16},{9,1... | collective-permute-start | bytes 1572872 | tf_op jit(solution)/shard_map/ppermute | solution.py:38
  31.1 54.6 %collective-permute-start.12 = (bf16[512,4096]{1,0:T(8,128)(2,1)}, bf16[512,4096]{1,0:T(8,128)(2,1)}, u32[]{:S(2)}, u32[]{:S(2)}) collective-permute-start(bf16[512,4096]{1,0:T(8,128)(2,1)} %bitcast.18), channel_id=1, source_target_pairs={{0,1},{1,0},{2,3},{3,2},{4,5},{5,4},{6,7},{7,6},{8,9},{9,8},{10,11... | collective-permute-start | bytes 12582920 | tf_op jit(solution)/shard_map/ppermute | solution.py:42
  33.9 9.8 %collective-permute-start.5 = (bf16[64,4096]{1,0:T(8,128)(2,1)S(1)}, bf16[64,4096]{1,0:T(8,128)(2,1)S(1)}, u32[]{:S(2)}, u32[]{:S(2)}) collective-permute-start(bf16[64,4096]{1,0:T(8,128)(2,1)S(1)} %collective-permute-done.4.refs_2_), channel_id=1, source_target_pairs={{0,2},{1,7},{2,0},{3,5},{4,6},{5,3},{6,4},{7,1},{8,10},{9,15},{10,... | collective-permute-start | bytes 1572872 | tf_op jit(solution)/shard_map/ppermute | solution.py:38
  35.5 9.2 %collective-permute-start.7 = (bf16[64,4096]{1,0:T(8,128)(2,1)S(1)}, bf16[64,4096]{1,0:T(8,128)(2,1)S(1)}, u32[]{:S(2)}, u32[]{:S(2)}) collective-permute-start(bf16[64,4096]{1,0:T(8,128)(2,1)S(1)} %collective-permute-done.6.refs_3_), channel_id=1, source_target_pairs={{0,8},{1,25},{2,10},{3,27},{4,12},{5,29},{6,14},{7,31},{8,0},{9,17... | collective-permute-start | bytes 1572872 | tf_op jit(solution)/shard_map/ppermute | solution.py:38
  48.1 37.6 %all-to-all-start = ((bf16[8,512,128]{2,1,0:T(8,128)(2,1)}), bf16[8,512,128]{2,1,0:T(8,128)(2,1)}, u32[]{:S(2)}, u32[]{:S(2)}) async-start(bf16[8,512,128]{2,1,0:T(8,128)(2,1)} %copy-done.7), calls=%async_computation | async-start | bytes 2097152 | tf_op jit(solution)/shard_map/all_to_all | solution.py:335
  94.1 12.1 %collective-permute-start.14 = (bf16[64,4096]{1,0:T(8,128)(2,1)S(1)}, bf16[64,4096]{1,0:T(8,128)(2,1)S(1)}, u32[]{:S(2)}, u32[]{:S(2)}) collective-permute-start(bf16[64,4096]{1,0:T(8,128)(2,1)S(1)} %get-tuple-element.84), channel_id=1, source_target_pairs={{0,2},{1,7},{2,0},{3,5},{4,6},{5,3},{6,4},{7,1},{8,10},{9,15},{10,... | collective-permute-start | bytes 1572872 | tf_op jit(solution)/shard_map/ppermute | solution.py:38
  95.0 11.2 %collective-permute-start.15 = (bf16[64,4096]{1,0:T(8,128)(2,1)S(1)}, bf16[64,4096]{1,0:T(8,128)(2,1)S(1)}, u32[]{:S(2)}, u32[]{:S(2)}) collective-permute-start(bf16[64,4096]{1,0:T(8,128)(2,1)S(1)} %get-tuple-element.85), channel_id=1, source_target_pairs={{0,8},{1,25},{2,10},{3,27},{4,12},{5,29},{6,14},{7,31},{8,0},{9,17... | collective-permute-start | bytes 1572872 | tf_op jit(solution)/shard_map/ppermute | solution.py:38
  102.7 12.2 %collective-permute-start.18 = (bf16[64,4096]{1,0:T(8,128)(2,1)S(1)}, bf16[64,4096]{1,0:T(8,128)(2,1)S(1)}, u32[]{:S(2)}, u32[]{:S(2)}) collective-permute-start(bf16[64,4096]{1,0:T(8,128)(2,1)S(1)} %get-tuple-element.88), channel_id=1, source_target_pairs={{0,2},{1,7},{2,0},{3,5},{4,6},{5,3},{6,4},{7,1},{8,10},{9,15},{10,... | collective-permute-start | bytes 1572872 | tf_op jit(solution)/shard_map/ppermute | solution.py:38
  104.6 12.4 %collective-permute-start.19 = (bf16[64,4096]{1,0:T(8,128)(2,1)S(1)}, bf16[64,4096]{1,0:T(8,128)(2,1)S(1)}, u32[]{:S(2)}, u32[]{:S(2)}) collective-permute-start(bf16[64,4096]{1,0:T(8,128)(2,1)S(1)} %get-tuple-element.89), channel_id=1, source_target_pairs={{0,8},{1,25},{2,10},{3,27},{4,12},{5,29},{6,14},{7,31},{8,0},{9,17... | collective-permute-start | bytes 1572872 | tf_op jit(solution)/shard_map/ppermute | solution.py:38
  106.4 10.6 %collective-permute-start.16 = (bf16[64,4096]{1,0:T(8,128)(2,1)S(1)}, bf16[64,4096]{1,0:T(8,128)(2,1)S(1)}, u32[]{:S(2)}, u32[]{:S(2)}) collective-permute-start(bf16[64,4096]{1,0:T(8,128)(2,1)S(1)} %get-tuple-element.86), channel_id=1, source_target_pairs={{0,6},{1,3},{2,4},{3,1},{4,2},{5,7},{6,0},{7,5},{8,14},{9,11},{10,... | collective-permute-start | bytes 1572872 | tf_op jit(solution)/shard_map/ppermute | solution.py:38
  106.5 11.1 %collective-permute-start.17 = (bf16[64,4096]{1,0:T(8,128)(2,1)S(1)}, bf16[64,4096]{1,0:T(8,128)(2,1)S(1)}, u32[]{:S(2)}, u32[]{:S(2)}) collective-permute-start(bf16[64,4096]{1,0:T(8,128)(2,1)S(1)} %get-tuple-element.87), channel_id=1, source_target_pairs={{0,24},{1,9},{2,26},{3,11},{4,28},{5,13},{6,30},{7,15},{8,16},{9,1... | collective-permute-start | bytes 1572872 | tf_op jit(solution)/shard_map/ppermute | solution.py:38
  118.1 9.3 %collective-permute-start.20 = (bf16[64,4096]{1,0:T(8,128)(2,1)S(1)}, bf16[64,4096]{1,0:T(8,128)(2,1)S(1)}, u32[]{:S(2)}, u32[]{:S(2)}) collective-permute-start(bf16[64,4096]{1,0:T(8,128)(2,1)S(1)} %get-tuple-element.92), channel_id=1, source_target_pairs={{0,8},{1,25},{2,10},{3,27},{4,12},{5,29},{6,14},{7,31},{8,0},{9,17... | collective-permute-start | bytes 1572872 | tf_op jit(solution)/shard_map/ppermute | solution.py:38
  119.6 9.2 %collective-permute-start.21 = (bf16[64,4096]{1,0:T(8,128)(2,1)S(1)}, bf16[64,4096]{1,0:T(8,128)(2,1)S(1)}, u32[]{:S(2)}, u32[]{:S(2)}) collective-permute-start(bf16[64,4096]{1,0:T(8,128)(2,1)S(1)} %get-tuple-element.93), channel_id=1, source_target_pairs={{0,2},{1,7},{2,0},{3,5},{4,6},{5,3},{6,4},{7,1},{8,10},{9,15},{10,... | collective-permute-start | bytes 1572872 | tf_op jit(solution)/shard_map/ppermute | solution.py:38
  129.1 8.4 %collective-permute-start.22 = (bf16[64,4096]{1,0:T(8,128)(2,1)S(1)}, bf16[64,4096]{1,0:T(8,128)(2,1)S(1)}, u32[]{:S(2)}, u32[]{:S(2)}) collective-permute-start(bf16[64,4096]{1,0:T(8,128)(2,1)S(1)} %get-tuple-element.96), channel_id=1, source_target_pairs={{0,24},{1,9},{2,26},{3,11},{4,28},{5,13},{6,30},{7,15},{8,16},{9,1... | collective-permute-start | bytes 1572872 | tf_op jit(solution)/shard_map/ppermute | solution.py:38
  138.9 9.0 %collective-permute-start.26 = (bf16[64,4096]{1,0:T(8,128)(2,1)S(1)}, bf16[64,4096]{1,0:T(8,128)(2,1)S(1)}, u32[]{:S(2)}, u32[]{:S(2)}) collective-permute-start(bf16[64,4096]{1,0:T(8,128)(2,1)S(1)} %get-tuple-element.100.refs_1_), channel_id=1, source_target_pairs={{0,24},{1,9},{2,26},{3,11},{4,28},{5,13},{6,30},{7,15},{8,16},{9,1... | collective-permute-start | bytes 1572872 | tf_op jit(solution)/shard_map/ppermute | solution.py:38
  139.9 11.0 %collective-permute-start.28 = (bf16[64,4096]{1,0:T(8,128)(2,1)S(1)}, bf16[64,4096]{1,0:T(8,128)(2,1)S(1)}, u32[]{:S(2)}, u32[]{:S(2)}) collective-permute-start(bf16[64,4096]{1,0:T(8,128)(2,1)S(1)} %get-tuple-element.99.refs_0_), channel_id=1, source_target_pairs={{0,2},{1,7},{2,0},{3,5},{4,6},{5,3},{6,4},{7,1},{8,10},{9,15},{10,... | collective-permute-start | bytes 1572872 | tf_op jit(solution)/shard_map/ppermute | solution.py:38
  140.8 10.6 %collective-permute-start.29 = (bf16[64,4096]{1,0:T(8,128)(2,1)S(1)}, bf16[64,4096]{1,0:T(8,128)(2,1)S(1)}, u32[]{:S(2)}, u32[]{:S(2)}) collective-permute-start(bf16[64,4096]{1,0:T(8,128)(2,1)S(1)} %get-tuple-element.100.refs_1_), channel_id=1, source_target_pairs={{0,8},{1,25},{2,10},{3,27},{4,12},{5,29},{6,14},{7,31},{8,0},{9,17... | collective-permute-start | bytes 1572872 | tf_op jit(solution)/shard_map/ppermute | solution.py:38
  147.0 13.4 %collective-permute-start.25 = (bf16[64,4096]{1,0:T(8,128)(2,1)S(1)}, bf16[64,4096]{1,0:T(8,128)(2,1)S(1)}, u32[]{:S(2)}, u32[]{:S(2)}) collective-permute-start(bf16[64,4096]{1,0:T(8,128)(2,1)S(1)} %collective-permute-done.24.refs_2_), channel_id=1, source_target_pairs={{0,2},{1,7},{2,0},{3,5},{4,6},{5,3},{6,4},{7,1},{8,10},{9,15},{10,... | collective-permute-start | bytes 1572872 | tf_op jit(solution)/shard_map/ppermute | solution.py:38
  148.0 13.3 %collective-permute-start.27 = (bf16[64,4096]{1,0:T(8,128)(2,1)S(1)}, bf16[64,4096]{1,0:T(8,128)(2,1)S(1)}, u32[]{:S(2)}, u32[]{:S(2)}) collective-permute-start(bf16[64,4096]{1,0:T(8,128)(2,1)S(1)} %collective-permute-done.26.refs_3_), channel_id=1, source_target_pairs={{0,8},{1,25},{2,10},{3,27},{4,12},{5,29},{6,14},{7,31},{8,0},{9,17... | collective-permute-start | bytes 1572872 | tf_op jit(solution)/shard_map/ppermute | solution.py:38
  161.2 23.3 %collective-permute-start.31 = (bf16[384,4096]{1,0:T(8,128)(2,1)}, bf16[384,4096]{1,0:T(8,128)(2,1)}, u32[]{:S(2)}, u32[]{:S(2)}) collective-permute-start(bf16[384,4096]{1,0:T(8,128)(2,1)} %get-tuple-element.111.refs_4_), channel_id=1, source_target_pairs={{0,1},{1,0},{2,3},{3,2},{4,5},{5,4},{6,7},{7,6},{8,9},{9,8},{10,11... | collective-permute-start | bytes 9437192 | tf_op jit(solution)/shard_map/ppermute | solution.py:42
  176.6 33.5 %all-to-all-start.1 = ((bf16[8,128,512]{2,1,0:T(8,128)(2,1)}), bf16[8,128,512]{2,1,0:T(8,128)(2,1)}, u32[]{:S(2)}, u32[]{:S(2)}) async-start(bf16[8,128,512]{2,1,0:T(8,128)(2,1)} %copy-done.6), calls=%async_computation.1 | async-start | bytes 2097152 | tf_op jit(solution)/shard_map/all_to_all | solution.py:335
  (26 other events, 242.3 us)

commit v4 on v3

--- a/solution.py
+++ b/solution.py
@@ -58,19 +58,23 @@
     return pl.CostEstimate(flops=flops, bytes_accessed=nbytes, transcendentals=0)
 
 
-def recon_body(start, layer_ref, lat_ref, own_dec, other_dec, *refs):
-    outs, (own_ref, other_ref) = refs[:-2], refs[-2:]
-    layers, _, both = lat_ref.shape
-    tokens = own_ref.shape[0]
+def recon_body(start, layer_ref, *refs):
+    hops, (own_dec, other_dec), refs = refs[:8], refs[8:10], refs[10:]
+    outs, (own_ref, other_ref, all_ref) = refs[:-3], refs[-3:]
+    layers, both = len(hops), hops[0].shape[1]
     half = both // 2
+    tokens = all_ref.shape[0]
 
     @pl.when(pl.program_id(0) == 0)
     def _():
+        for hop in range(layers):
+            source = lax.rem(layer_ref[0] - hop + layers, layers)
+            at = pl.ds(pl.multiple_of(source * both, both), both)
+            piece = hops[hop][start : start + tokens, :]
+            all_ref[:, at] = jnp.where(hop <= layer_ref[0], piece, jnp.zeros_like(piece))
+        lat = all_ref[...]
         for k, ref in enumerate((own_ref, other_ref)):
-            pieces = []
-            for s in range(layers):
-                piece = lat_ref[s, start : start + tokens, k * half : (k + 1) * half]
-                pieces.append(jnp.where(s <= layer_ref[0], piece, jnp.zeros_like(piece)))
+            pieces = [lat[:, (2 * s + k) * half : (2 * s + k + 1) * half] for s in range(layers)]
             ref[...] = jnp.concatenate(pieces, axis=1)
 
     part = jnp.dot(own_ref[...], own_dec[...], preferred_element_type=F32)
@@ -81,8 +85,9 @@
         out[...] = part[i * rows : (i + 1) * rows]
 
 
-def recon(layer, latents, start, tokens, decs, streams, block=1024):
+def recon(layer, hops, start, tokens, decs, streams, block=1024):
     depth, width = decs[0].shape
+    both = hops[0].shape[1]
     rows = tokens // streams
     column = lambda i, layer_ref: (0, i)
     whole = lambda i, layer_ref: (0, 0)
@@ -91,25 +96,25 @@
         grid_spec=pltpu.PrefetchScalarGridSpec(
             num_scalar_prefetch=1,
             grid=(width // block,),
-            in_specs=[pl.BlockSpec(memory_space=pltpu.VMEM)]
+            in_specs=[pl.BlockSpec(memory_space=pltpu.VMEM)] * len(hops)
             + [pl.BlockSpec((depth, block), column)] * 2,
             out_specs=[pl.BlockSpec((rows, block), column)] * streams
             + [pl.BlockSpec((tokens, depth), whole)] * 2,
+            scratch_shapes=[pltpu.VMEM((tokens, 2 * depth), BF)],
         ),
         out_shape=[jax.ShapeDtypeStruct((rows, width), BF)] * streams
         + [jax.ShapeDtypeStruct((tokens, depth), BF)] * 2,
         compiler_params=params(),
         cost_estimate=cost(4 * tokens * depth * width, 4 * depth * width),
-    )(layer, latents, *decs)
-
-
-def grads_body(scale, count, layer_ref, own_dec, other_dec, *refs):
+    )(layer, *hops, *decs)
+
+
+def grads_body(scale, layers, count, layer_ref, own_dec, other_dec, *refs):
     errs, refs = refs[:count], refs[count:]
-    before, (out, err_ref), totals = refs[:-4], refs[-4:-2], refs[-2:]
-    layers, both, _ = out.shape
-    half = both // 2
+    before, outs, (err_ref, *totals) = refs[: -3 - layers], refs[-3 - layers : -3], refs[-3:]
+    half = outs[0].shape[0] // 2
     tokens = err_ref.shape[0]
-    at = out.shape[2] - tokens
+    at = outs[0].shape[1] - tokens
 
     @pl.when(pl.program_id(0) == 0)
     def _():
@@ -118,18 +123,19 @@
 
     err = jnp.concatenate([e[...] for e in errs], axis=0)
     err_ref[...] = err
-    totals[0][...] += dot(own_dec[...], err, 1, 1)
-    totals[1][...] += dot(other_dec[...], err, 1, 1)
+    for total, dec in zip(totals, (own_dec, other_dec)):
+        total[...] += dot(dec[...], err, 1, 1)
 
     @pl.when(pl.program_id(0) == pl.num_programs(0) - 1)
     def _():
-        for s in range(layers):
+        for hop, out in enumerate(outs):
+            source = lax.rem(layer_ref[0] - hop + layers, layers)
+            where = pl.ds(pl.multiple_of(source * half, half), half)
             for k, total in enumerate(totals):
-                value = scale * total[s * half : (s + 1) * half, :]
-                value = jnp.where(s <= layer_ref[0], value, 0.0)
-                out[s, k * half : (k + 1) * half, at:] = value.astype(BF)
-        for ref in before:
-            out[:, :, :at] = ref[...]
+                value = jnp.where(hop <= layer_ref[0], scale * total[where, :], 0.0)
+                out[k * half : (k + 1) * half, at:] = value.astype(BF)
+        for ref, out in zip(before, outs):
+            out[:, :at] = ref[...]
 
 
 def latent_grads(layer, decs, errs, before, scale, layers, block=1024):
@@ -137,26 +143,23 @@
     rows = errs[0].shape[0]
     tokens = rows * len(errs)
     both = 2 * depth // layers
-    span = tokens + sum(b.shape[2] for b in before)
+    span = tokens + (before[0].shape[1] if before else 0)
     column = lambda i, layer_ref: (0, i)
+    whole = lambda i, layer_ref: (0, 0)
     return pl.pallas_call(
-        functools.partial(grads_body, scale, len(errs)),
+        functools.partial(grads_body, scale, layers, len(errs)),
         grid_spec=pltpu.PrefetchScalarGridSpec(
             num_scalar_prefetch=1,
             grid=(width // block,),
             in_specs=[pl.BlockSpec((depth, block), column)] * 2
             + [pl.BlockSpec((rows, block), column)] * len(errs)
             + [pl.BlockSpec(memory_space=pltpu.VMEM)] * len(before),
-            out_specs=[
-                pl.BlockSpec((layers, both, span), lambda i, layer_ref: (0, 0, 0)),
-                pl.BlockSpec((tokens, block), column),
-            ],
+            out_specs=[pl.BlockSpec((both, span), whole)] * layers
+            + [pl.BlockSpec((tokens, block), column)],
             scratch_shapes=[pltpu.VMEM((depth, tokens), F32)] * 2,
         ),
-        out_shape=[
-            jax.ShapeDtypeStruct((layers, both, span), BF),
-            jax.ShapeDtypeStruct((tokens, width), BF),
-        ],
+        out_shape=[jax.ShapeDtypeStruct((both, span), BF)] * layers
+        + [jax.ShapeDtypeStruct((tokens, width), BF)],
         compiler_params=params(),
         cost_estimate=cost(4 * tokens * depth * width, 4 * depth * width),
     )(layer, *decs, *errs, *before)
@@ -179,27 +182,19 @@
         pre = total[...] + bias[...]
         value = jnp.maximum(pre, 0.0).astype(BF)
         mask[...] = jnp.where(pre > 0, 1.0, 0.0).T.astype(BF)
-        if before:
-            at = before[0].shape[0]
-            for i in range(latents.shape[0]):
-                latents[i, :at, :] = before[0][...]
-                latents[i, at:, :] = value
-        else:
-            latents[...] = value
-
-
-def encode(blocks, encs, bias, before=(), layers=0, block=1024):
+        at = latents.shape[0] - value.shape[0]
+        latents[at:, :] = value
+        for ref in before:
+            latents[:at, :] = ref[...]
+
+
+def encode(blocks, encs, bias, before=(), block=1024):
     rows, width = blocks[0].shape
     count = rows * len(blocks)
     both = bias.shape[1]
     column = lambda i: (0, i)
     whole = lambda i: (0, 0)
-    if before:
-        shape = (layers, before[0].shape[0] + count, both)
-        spec = pl.BlockSpec(shape, lambda i: (0, 0, 0))
-    else:
-        shape = (count, both)
-        spec = pl.BlockSpec(shape, whole)
+    span = count + sum(b.shape[0] for b in before)
     return pl.pallas_call(
         functools.partial(encode_body, len(blocks)),
         grid=(width // block,),
@@ -208,12 +203,12 @@
         + [pl.BlockSpec((1, both), whole)]
         + [pl.BlockSpec(b.shape, whole) for b in before],
         out_specs=[
-            spec,
+            pl.BlockSpec((span, both), whole),
             pl.BlockSpec((both, count), whole),
             pl.BlockSpec((count, block), column),
         ],
         out_shape=[
-            jax.ShapeDtypeStruct(shape, BF),
+            jax.ShapeDtypeStruct((span, both), BF),
             jax.ShapeDtypeStruct((both, count), BF),
             jax.ShapeDtypeStruct((count, width), BF),
         ],
@@ -331,20 +326,26 @@
     *early, dec_own = tie(*early, decs[0])
     decs.append(swap_cores(dec_own))
 
-    def along_layers(value):
-        return lax.all_to_all(value, "layer", 0, 0, tiled=True)
+    def shift(value, hop, least=0):
+        if hop > 0:
+            pairs = [(i, i + hop) for i in range(least, layers - hop)]
+        else:
+            pairs = [(i, i + hop) for i in range(max(least, -hop), layers)]
+        return lax.ppermute(value, "layer", pairs)
 
     early_latents, early_mask, early_acts = encode(early, encs, bias)
     *late, early_latents = tie(*late, early_latents)
-    latents, late_mask, late_acts = encode(late, encs, bias, [early_latents], layers)
-    latents = along_layers(latents)
+    latents, late_mask, late_acts = encode(late, encs, bias, [early_latents])
+    one, two = shift(latents, 1), shift(latents, 2)
+    hops = [latents, one, two, shift(one, 2, 1), shift(two, 2, 2)]
+    hops += [shift(latents, hop) for hop in range(5, layers)]
     span, count = early_latents.shape[0], late_mask.shape[1]
 
-    *send, late_own, late_other = recon(layer_arr, latents, span, count, decs, 2)
+    *send, late_own, late_other = recon(layer_arr, hops, span, count, decs, 2)
     late_swapped = swap_cores(late_other)
     send, late_swapped = tie(send, late_swapped)
     got = across(send, 1)
-    *parts, early_own, early_other = recon(layer_arr, latents, 0, span, decs, 6)
+    *parts, early_own, early_other = recon(layer_arr, hops, 0, span, decs, 6)
     others = [swap_cores(early_other), late_swapped]
     target = targets[0]
     half = ((4 * part, width), BF)
@@ -357,18 +358,22 @@
     outs = [((own_tokens, width), BF)] + [half] * 2
     rebuilt, *errs = vmem_call(finish_body, outs, *out[:2], *in_group(out[2:], 0), target)
     early, late = spread(errs)
-    partial, early_err = latent_grads(layer_arr, decs, early, [], grad_scale, layers)
-    late, partial, early_err = tie(late, partial, early_err)
-    partial, late_err = latent_grads(layer_arr, decs, late, [partial], grad_scale, layers)
-    grad = along_layers(partial)
+    *hops, early_err = latent_grads(layer_arr, decs, early, [], grad_scale, layers)
+    late, hops, early_err = tie(late, hops, early_err)
+    *hops, late_err = latent_grads(layer_arr, decs, late, hops, grad_scale, layers)
+    relayed = [shift(hops[3], -2, 3), shift(hops[4], -2, 4)]
+    grads = [hops[0]] + [shift(hops[hop], -hop) for hop in range(5, layers)]
+    near = vmem_call(add_body, [(h.shape, BF) for h in hops[1:3]], *hops[1:3], *relayed)
+    near, errs = tie(near, [early_err, late_err])
+    grads += [shift(near[0], -1), shift(near[1], -2)]
 
     lats = [early_own, others[0], late_own, others[1]]
-    errs = [early_err, swap_cores(early_err), late_err, swap_cores(late_err)]
+    errs = [errs[0], swap_cores(errs[0]), errs[1], swap_cores(errs[1])]
     dec_grad = dec_grads(lats, errs, grad_scale).reshape(layers, rows, width)
-    grad, dec_grad = tie(grad, dec_grad)
+    grads, dec_grad = tie(grads, dec_grad)
 
     mask = jnp.concatenate([early_mask, late_mask], axis=1).astype(F32)
-    grad = (jnp.sum(grad.astype(F32), axis=0) * mask).astype(BF)
+    grad = (sum(g.astype(F32) for g in grads) * mask).astype(BF)
     early_grad, late_grad = grad[:, :span], grad[:, span:]
 
     def enc_part(which):

time: 218 us -> 207 us (0.950)
  waiting for transfers between devices: 107 us -> 89 us
  starting transfers between devices: 55.4 us -> 69.6 us
  local copies, waits for them, and re-layouts: 9.35 us -> 4.87 us
    all_to_all x2 -> x0, waiting for transfers between devices: 43 us -> none  [along_layers(): return lax.all_to_all(value, 'layer', 0, 0, tiled=True)]
    ppermute x0 -> x14, starting transfers between devices: none -> 27 us  [shift(): return lax.ppermute(value, 'layer', pairs)]
    ppermute x0 -> x14, waiting for transfers between devices: none -> 23.3 us  [shift(): return lax.ppermute(value, 'layer', pairs)]
    all_to_all x2 -> x0, starting transfers between devices: 12.4 us -> none  [along_layers(): return lax.all_to_all(value, 'layer', 0, 0, tiled=True)]
    unnamed x28 -> x22, local copies, waits for them, and re-layouts: 8.31 us -> 3.83 us
  transfers between devices with their start and end apart: 36 -> 48, of which waited for: 25 -> 28; matrix products, arithmetic and copies ran while one was open for 0% -> 0% of each run, Pallas kernels for 15% -> 13%
where the time goes in v4:
time: 207 us; the launch traced here: 206 us
  waiting for transfers between devices  89 us (43%)
  starting transfers between devices  69.6 us (34%)
  Pallas kernels  38.2 us (18%)
  local copies, waits for them, and re-layouts  4.87 us (2%)
  matrix products  2.81 us (1%)
    ppermute x26, waiting for transfers between devices, exchange(): return lax.ppermute(value, 'tok', chip_pairs(axis, which))  54.5 us
    ppermute x26, starting transfers between devices, exchange(): return lax.ppermute(value, 'tok', chip_pairs(axis, which))  29.9 us
    ppermute x14, starting transfers between devices, shift(): return lax.ppermute(value, 'layer', pairs)  27 us
    ppermute x14, waiting for transfers between devices, shift(): return lax.ppermute(value, 'layer', pairs)  23.3 us
    ppermute x8, starting transfers between devices, swap_cores(): return lax.ppermute(value, 'tok', CORE_PAIRS)  12.6 us
    pallas_call x2, Pallas kernels, latent_grads(): pl.pallas_call(functools.partial(grads_body, scale, layers, len(errs)), g...  12.5 us
    pallas_call x2, Pallas kernels, recon(): pl.pallas_call(functools.partial(recon_body, start), grid_spec=pltpu.Pref...  11.3 us
    ppermute x8, waiting for transfers between devices, swap_cores(): return lax.ppermute(value, 'tok', CORE_PAIRS)  11.2 us
  transfers between devices with their start and end apart: 48, of which 28 were waited for; matrix products, arithmetic and copies ran while one was open for 0% of the time, Pallas kernels for 13%

profile of v4, /device:TPU:1, one launch (start us, length us, event | category | flops | bytes accessed | tf_op | source)
XLA Modules:
  0.0 205.7 jit_solution(16170546952466567002)
XLA Ops:
  6.3 3.0 %collective-permute-start.3 = (bf16[32,4096]{1,0:T(8,128)(2,1)S(1)}, bf16[32,4096]{1,0:T(8,128)(2,1)S(1)}, u32[]{:S(2)}, u32[]{:S(2)}) collective-permute-start(bf16[32,4096]{1,0:T(8,128)(2,1)S(1)} %pad_maximum_fusion.3), channel_id=1, source_target_pairs={{0,2},{1,7},{2,0},{3,5},{4,6},{5,3},{6,4},{7,1},{8,10},{9,15},{10,... | collective-permute-start | bytes 786440 | tf_op jit(solution)/shard_map/ppermute | solution.py:38
  9.3 2.6 %collective-permute-start.1 = (bf16[32,4096]{1,0:T(8,128)(2,1)S(1)}, bf16[32,4096]{1,0:T(8,128)(2,1)S(1)}, u32[]{:S(2)}, u32[]{:S(2)}) collective-permute-start(bf16[32,4096]{1,0:T(8,128)(2,1)S(1)} %pad_maximum_fusion.2), channel_id=1, source_target_pairs={{0,8},{1,25},{2,10},{3,27},{4,12},{5,29},{6,14},{7,31},{8,0},{9,17... | collective-permute-start | bytes 786440 | tf_op jit(solution)/shard_map/ppermute | solution.py:38
  19.5 6.8 %collective-permute-done.8.refs_4_ = bf16[64,4096]{1,0:T(8,128)(2,1)S(1)} collective-permute-done((bf16[64,4096]{1,0:T(8,128)(2,1)S(1)}, bf16[64,4096]{1,0:T(8,128)(2,1)S(1)}, u32[]{:S(2)}, u32[]{:S(2)}) %collective-permute-start.8) | collective-permute-done | bytes 524320 | tf_op jit(solution)/shard_map/ppermute | solution.py:38
  27.1 4.0 %collective-permute-done.6.refs_3_ = bf16[64,4096]{1,0:T(8,128)(2,1)S(1)} collective-permute-done((bf16[64,4096]{1,0:T(8,128)(2,1)S(1)}, bf16[64,4096]{1,0:T(8,128)(2,1)S(1)}, u32[]{:S(2)}, u32[]{:S(2)}) %collective-permute-start.6) | collective-permute-done | bytes 524320 | tf_op jit(solution)/shard_map/ppermute | solution.py:38
  31.1 2.7 %collective-permute-start.19 = (bf16[512,4096]{1,0:T(8,128)(2,1)}, bf16[512,4096]{1,0:T(8,128)(2,1)}, u32[]{:S(2)}, u32[]{:S(2)}) collective-permute-start(bf16[512,4096]{1,0:T(8,128)(2,1)} %bitcast.18), channel_id=1, source_target_pairs={{0,1},{1,0},{2,3},{3,2},{4,5},{5,4},{6,7},{7,6},{8,9},{9,8},{10,11... | collective-permute-start | bytes 12582920 | tf_op jit(solution)/shard_map/ppermute | solution.py:42
  36.7 4.7 %collective-permute-done.11 = f32[1,64]{1,0:T(1,128)S(1)} collective-permute-done((f32[1,64]{1,0:T(1,128)S(1)}, f32[1,64]{1,0:T(1,128)S(1)}, u32[]{:S(2)}, u32[]{:S(2)}) %collective-permute-start.11) | collective-permute-done | bytes 288 | tf_op jit(solution)/shard_map/ppermute | solution.py:42
  47.8 7.5 %collective-permute-start.18 = (bf16[512,128]{1,0:T(8,128)(2,1)S(1)}, bf16[512,128]{1,0:T(8,128)(2,1)S(1)}, u32[]{:S(2)}, u32[]{:S(2)}) collective-permute-start(bf16[512,128]{1,0:T(8,128)(2,1)S(1)} %get-tuple-element.107.refs_0_), channel_id=1, source_target_pairs={{0,224},{1,225},{2,226},{3,227},{4,228},{5,229},{6,230},{7,231},{8... | collective-permute-start | bytes 393224 | tf_op jit(solution)/shard_map/ppermute | solution.py:334
  58.5 3.1 %collective-permute-start.17 = (bf16[512,128]{1,0:T(8,128)(2,1)S(1)}, bf16[512,128]{1,0:T(8,128)(2,1)}, u32[]{:S(2)}, u32[]{:S(2)}) collective-permute-start(bf16[512,128]{1,0:T(8,128)(2,1)S(1)} %get-tuple-element.107.refs_0_), channel_id=1, source_target_pairs={{0,192},{32,224},{1,193},{33,225},{2,194},{34,226},{3,195},{35,227... | collective-permute-start | bytes 393224 | tf_op jit(solution)/shard_map/ppermute | solution.py:334
  61.6 2.8 %collective-permute-start.16 = (bf16[512,128]{1,0:T(8,128)(2,1)S(1)}, bf16[512,128]{1,0:T(8,128)(2,1)}, u32[]{:S(2)}, u32[]{:S(2)}) collective-permute-start(bf16[512,128]{1,0:T(8,128)(2,1)S(1)} %get-tuple-element.107.refs_0_), channel_id=1, source_target_pairs={{0,160},{32,192},{64,224},{1,161},{33,193},{65,225},{2,162},{34,19... | collective-permute-start | bytes 393224 | tf_op jit(solution)/shard_map/ppermute | solution.py:334
  67.1 5.4 %collective-permute-done.17.refs_6_ = bf16[512,128]{1,0:T(8,128)(2,1)} collective-permute-done((bf16[512,128]{1,0:T(8,128)(2,1)S(1)}, bf16[512,128]{1,0:T(8,128)(2,1)}, u32[]{:S(2)}, u32[]{:S(2)}) %collective-permute-start.17) | collective-permute-done | bytes 131104 | tf_op jit(solution)/shard_map/ppermute | solution.py:334
  72.5 2.8 %collective-permute-done.16.refs_5_ = bf16[512,128]{1,0:T(8,128)(2,1)} collective-permute-done((bf16[512,128]{1,0:T(8,128)(2,1)S(1)}, bf16[512,128]{1,0:T(8,128)(2,1)}, u32[]{:S(2)}, u32[]{:S(2)}) %collective-permute-start.16) | collective-permute-done | bytes 131104 | tf_op jit(solution)/shard_map/ppermute | solution.py:334
  77.5 4.6 %shard_map.79 = (bf16[64,4096]{1,0:T(8,128)(2,1)S(1)}, bf16[64,4096]{1,0:T(8,128)(2,1)S(1)}, bf16[128,512]{1,0:T(8,128)(2,1)S(1)}, bf16[128,512]{1,0:T(8,128)(2,1)S(1)}) custom-call(s32[1]{0:T(128)} %bitcast.layer_ref, bf16[512,128]{1,0:T(8,128)(2,1)S(1)} %get-tuple-element.107.refs_0_, bf16[512,128]{1,0:T(8,128)(2,1)} %collective-permute-done.12.refs_1_, ...), custom_call_target="tpu_custom_call" | custom-call | flops 1073741824 | bytes 8388608 | tf_op jit(solution)/shard_map/pallas_call | solution.py:94
  85.8 6.7 %shard_map.78 = (bf16[64,4096]{1,0:T(8,128)(2,1)S(1)}, bf16[64,4096]{1,0:T(8,128)(2,1)S(1)}, bf16[64,4096]{1,0:T(8,128)(2,1)S(1)}, bf16[64,4096]{1,0:T(8,128)(2,...) custom-call(s32[1]{0:T(128)} %bitcast.layer_ref, ...), custom_call_target="tpu_custom_call" | custom-call | flops 3221225472 | bytes 8388608 | tf_op jit(solution)/shard_map/pallas_call | solution.py:94
  96.2 8.3 %collective-permute-done.25.refs_4_ = bf16[64,4096]{1,0:T(8,128)(2,1)S(1)} collective-permute-done((bf16[64,4096]{1,0:T(8,128)(2,1)S(1)}, bf16[64,4096]{1,0:T(8,128)(2,1)S(1)}, u32[]{:S(2)}, u32[]{:S(2)}) %collective-permute-start.25) | collective-permute-done | bytes 524320 | tf_op jit(solution)/shard_map/ppermute | solution.py:38
  109.9 7.1 %collective-permute-done.27.refs_2_ = bf16[64,4096]{1,0:T(8,128)(2,1)S(1)} collective-permute-done((bf16[64,4096]{1,0:T(8,128)(2,1)S(1)}, bf16[64,4096]{1,0:T(8,128)(2,1)S(1)}, u32[]{:S(2)}, u32[]{:S(2)}) %collective-permute-start.27) | collective-permute-done | bytes 524320 | tf_op jit(solution)/shard_map/ppermute | solution.py:38
  119.3 7.7 %collective-permute-done.29.refs_2_ = bf16[64,4096]{1,0:T(8,128)(2,1)S(1)} collective-permute-done((bf16[64,4096]{1,0:T(8,128)(2,1)S(1)}, bf16[64,4096]{1,0:T(8,128)(2,1)S(1)}, u32[]{:S(2)}, u32[]{:S(2)}) %collective-permute-start.29) | collective-permute-done | bytes 524320 | tf_op jit(solution)/shard_map/ppermute | solution.py:38
  132.1 4.5 %collective-permute-done.31.refs_2_ = bf16[64,4096]{1,0:T(8,128)(2,1)S(1)} collective-permute-done((bf16[64,4096]{1,0:T(8,128)(2,1)S(1)}, bf16[64,4096]{1,0:T(8,128)(2,1)S(1)}, u32[]{:S(2)}, u32[]{:S(2)}) %collective-permute-start.31) | collective-permute-done | bytes 524320 | tf_op jit(solution)/shard_map/ppermute | solution.py:38
  140.9 7.3 %shard_map.84 = (bf16[128,384]{1,0:T(8,128)(2,1)S(1)}, bf16[128,384]{1,0:T(8,128)(2,1)S(1)}, bf16[128,384]{1,0:T(8,128)(2,1)S(1)}, bf16[128,384]{1,0:T(8,128)(2,...) custom-call(s32[1]{0:T(128)} %bitcast.layer_ref, ...), custom_call_target="tpu_custom_call" | custom-call | flops 3221225472 | bytes 8388608 | tf_op jit(solution)/shard_map/pallas_call | solution.py:149
  150.8 5.2 %shard_map.85 = (bf16[128,512]{1,0:T(8,128)(2,1)S(1)}, bf16[128,512]{1,0:T(8,128)(2,1)S(1)}, bf16[128,512]{1,0:T(8,128)(2,1)S(1)}, bf16[128,512]{1,0:T(8,128)(2,...) custom-call(s32[1]{0:T(128)} %bitcast.layer_ref, ...), custom_call_target="tpu_custom_call" | custom-call | flops 1073741824 | bytes 8388608 | tf_op jit(solution)/shard_map/pallas_call | solution.py:149
  157.4 8.3 %collective-permute-start.45 = (bf16[384,4096]{1,0:T(8,128)(2,1)S(1)}, bf16[384,4096]{1,0:T(8,128)(2,1)S(1)}, u32[]{:S(2)}, u32[]{:S(2)}) collective-permute-start(bf16[384,4096]{1,0:T(8,128)(2,1)S(1)} %get-tuple-element.170.refs_4_), channel_id=1, source_target_pairs={{0,1},{1,0},{2,3},{3,2},{4,5},{5,4},{6,7},{7,6},{8,9},{9,8},{10,11... | collective-permute-start | bytes 9437192 | tf_op jit(solution)/shard_map/ppermute | solution.py:42
  168.8 4.2 %collective-permute-done.44.refs_1_ = bf16[384,512]{1,0:T(8,128)(2,1)S(1)} collective-permute-done((bf16[384,512]{1,0:T(8,128)(2,1)S(1)}, bf16[384,512]{1,0:T(8,128)(2,1)S(1)}, u32[]{:S(2)}, u32[]{:S(2)}) %collective-permute-start.44) | collective-permute-done | bytes 393248 | tf_op jit(solution)/shard_map/ppermute | solution.py:42
  177.0 8.9 %shard_map.87 = bf16[512,4096]{1,0:T(8,128)(2,1)} custom-call(bf16[384,512]{1,0:T(8,128)(2,1)S(1)} %get-tuple-element.166.refs_0_, bf16[384,512]{1,0:T(8,128)(2,1)S(1)} %collective-permute-done.44.refs_1_, bf16[128,512]{1,0:T(8,128)(2,1)S(1)} %get-tuple-element.168.refs_2_, bf16[128,512]{1,0:T(8,128)(2,1)S(1)} %collective-permute-done.20.refs_3_, ...), custom_call_target="tpu_custom_call" | custom-call | flops 4294967296 | bytes 12582912 | tf_op jit(solution)/shard_map/pallas_call | solution.py:232
  188.2 4.1 %collective-permute-done.38 = bf16[128,512]{1,0:T(8,128)(2,1)S(1)} collective-permute-done((bf16[128,512]{1,0:T(8,128)(2,1)S(1)}, bf16[128,512]{1,0:T(8,128)(2,1)S(1)}, u32[]{:S(2)}, u32[]{:S(2)}) %collective-permute-start.38) | collective-permute-done | bytes 131104 | tf_op jit(solution)/shard_map/ppermute | solution.py:334
  192.3 8.6 %collective-permute-done.39 = bf16[128,512]{1,0:T(8,128)(2,1)S(1)} collective-permute-done((bf16[128,512]{1,0:T(8,128)(2,1)S(1)}, bf16[128,512]{1,0:T(8,128)(2,1)S(1)}, u32[]{:S(2)}, u32[]{:S(2)}) %collective-permute-start.39) | collective-permute-done | bytes 131104 | tf_op jit(solution)/shard_map/ppermute | solution.py:334
  (117 shorter events, 73.8 us)
Async XLA Ops:
  15.9 10.4 %collective-permute-start.8 = (bf16[64,4096]{1,0:T(8,128)(2,1)S(1)}, bf16[64,4096]{1,0:T(8,128)(2,1)S(1)}, u32[]{:S(2)}, u32[]{:S(2)}) collective-permute-start(bf16[64,4096]{1,0:T(8,128)(2,1)S(1)} %pad_maximum_fusion.refs_0_), channel_id=1, source_target_pairs={{0,2},{1,7},{2,0},{3,5},{4,6},{5,3},{6,4},{7,1},{8,10},{9,15},{10,... | collective-permute-start | bytes 1572872 | tf_op jit(solution)/shard_map/ppermute | solution.py:38
  16.4 10.7 %collective-permute-start.4 = (bf16[64,4096]{1,0:T(8,128)(2,1)S(1)}, bf16[64,4096]{1,0:T(8,128)(2,1)S(1)}, u32[]{:S(2)}, u32[]{:S(2)}) collective-permute-start(bf16[64,4096]{1,0:T(8,128)(2,1)S(1)} %pad_maximum_fusion.refs_0_), channel_id=1, source_target_pairs={{0,6},{1,3},{2,4},{3,1},{4,2},{5,7},{6,0},{7,5},{8,14},{9,11},{10,... | collective-permute-start | bytes 1572872 | tf_op jit(solution)/shard_map/ppermute | solution.py:38
  19.5 11.7 %collective-permute-start.6 = (bf16[64,4096]{1,0:T(8,128)(2,1)S(1)}, bf16[64,4096]{1,0:T(8,128)(2,1)S(1)}, u32[]{:S(2)}, u32[]{:S(2)}) collective-permute-start(bf16[64,4096]{1,0:T(8,128)(2,1)S(1)} %pad_maximum_fusion.1.refs_1_), channel_id=1, source_target_pairs={{0,24},{1,9},{2,26},{3,11},{4,28},{5,13},{6,30},{7,15},{8,16},{9,1... | collective-permute-start | bytes 1572872 | tf_op jit(solution)/shard_map/ppermute | solution.py:38
  31.1 44.2 %collective-permute-start.19 = (bf16[512,4096]{1,0:T(8,128)(2,1)}, bf16[512,4096]{1,0:T(8,128)(2,1)}, u32[]{:S(2)}, u32[]{:S(2)}) collective-permute-start(bf16[512,4096]{1,0:T(8,128)(2,1)} %bitcast.18), channel_id=1, source_target_pairs={{0,1},{1,0},{2,3},{3,2},{4,5},{5,4},{6,7},{7,6},{8,9},{9,8},{10,11... | collective-permute-start | bytes 12582920 | tf_op jit(solution)/shard_map/ppermute | solution.py:42
  47.8 13.8 %collective-permute-start.18 = (bf16[512,128]{1,0:T(8,128)(2,1)S(1)}, bf16[512,128]{1,0:T(8,128)(2,1)S(1)}, u32[]{:S(2)}, u32[]{:S(2)}) collective-permute-start(bf16[512,128]{1,0:T(8,128)(2,1)S(1)} %get-tuple-element.107.refs_0_), channel_id=1, source_target_pairs={{0,224},{1,225},{2,226},{3,227},{4,228},{5,229},{6,230},{7,231},{8... | collective-permute-start | bytes 393224 | tf_op jit(solution)/shard_map/ppermute | solution.py:334
  58.5 13.9 %collective-permute-start.17 = (bf16[512,128]{1,0:T(8,128)(2,1)S(1)}, bf16[512,128]{1,0:T(8,128)(2,1)}, u32[]{:S(2)}, u32[]{:S(2)}) collective-permute-start(bf16[512,128]{1,0:T(8,128)(2,1)S(1)} %get-tuple-element.107.refs_0_), channel_id=1, source_target_pairs={{0,192},{32,224},{1,193},{33,225},{2,194},{34,226},{3,195},{35,227... | collective-permute-start | bytes 393224 | tf_op jit(solution)/shard_map/ppermute | solution.py:334
  61.6 13.7 %collective-permute-start.16 = (bf16[512,128]{1,0:T(8,128)(2,1)S(1)}, bf16[512,128]{1,0:T(8,128)(2,1)}, u32[]{:S(2)}, u32[]{:S(2)}) collective-permute-start(bf16[512,128]{1,0:T(8,128)(2,1)S(1)} %get-tuple-element.107.refs_0_), channel_id=1, source_target_pairs={{0,160},{32,192},{64,224},{1,161},{33,193},{65,225},{2,162},{34,19... | collective-permute-start | bytes 393224 | tf_op jit(solution)/shard_map/ppermute | solution.py:334
  64.5 10.8 %collective-permute-start.15 = (bf16[512,128]{1,0:T(8,128)(2,1)S(1)}, bf16[512,128]{1,0:T(8,128)(2,1)}, u32[]{:S(2)}, u32[]{:S(2)}) collective-permute-start(bf16[512,128]{1,0:T(8,128)(2,1)S(1)} %collective-permute-done.13.refs_2_), channel_id=1, source_target_pairs={{64,128},{96,160},{128,192},{160,224},{65,129},{97,161},{129,193},... | collective-permute-start | bytes 393224 | tf_op jit(solution)/shard_map/ppermute | solution.py:334
  83.6 12.1 %collective-permute-start.21 = (bf16[64,4096]{1,0:T(8,128)(2,1)S(1)}, bf16[64,4096]{1,0:T(8,128)(2,1)S(1)}, u32[]{:S(2)}, u32[]{:S(2)}) collective-permute-start(bf16[64,4096]{1,0:T(8,128)(2,1)S(1)} %get-tuple-element.116), channel_id=1, source_target_pairs={{0,2},{1,7},{2,0},{3,5},{4,6},{5,3},{6,4},{7,1},{8,10},{9,15},{10,... | collective-permute-start | bytes 1572872 | tf_op jit(solution)/shard_map/ppermute | solution.py:38
  84.7 11.1 %collective-permute-start.22 = (bf16[64,4096]{1,0:T(8,128)(2,1)S(1)}, bf16[64,4096]{1,0:T(8,128)(2,1)S(1)}, u32[]{:S(2)}, u32[]{:S(2)}) collective-permute-start(bf16[64,4096]{1,0:T(8,128)(2,1)S(1)} %get-tuple-element.117), channel_id=1, source_target_pairs={{0,8},{1,25},{2,10},{3,27},{4,12},{5,29},{6,14},{7,31},{8,0},{9,17... | collective-permute-start | bytes 1572872 | tf_op jit(solution)/shard_map/ppermute | solution.py:38
  92.4 12.1 %collective-permute-start.25 = (bf16[64,4096]{1,0:T(8,128)(2,1)S(1)}, bf16[64,4096]{1,0:T(8,128)(2,1)S(1)}, u32[]{:S(2)}, u32[]{:S(2)}) collective-permute-start(bf16[64,4096]{1,0:T(8,128)(2,1)S(1)} %get-tuple-element.120), channel_id=1, source_target_pairs={{0,2},{1,7},{2,0},{3,5},{4,6},{5,3},{6,4},{7,1},{8,10},{9,15},{10,... | collective-permute-start | bytes 1572872 | tf_op jit(solution)/shard_map/ppermute | solution.py:38
  94.2 12.4 %collective-permute-start.26 = (bf16[64,4096]{1,0:T(8,128)(2,1)S(1)}, bf16[64,4096]{1,0:T(8,128)(2,1)S(1)}, u32[]{:S(2)}, u32[]{:S(2)}) collective-permute-start(bf16[64,4096]{1,0:T(8,128)(2,1)S(1)} %get-tuple-element.121), channel_id=1, source_target_pairs={{0,8},{1,25},{2,10},{3,27},{4,12},{5,29},{6,14},{7,31},{8,0},{9,17... | collective-permute-start | bytes 1572872 | tf_op jit(solution)/shard_map/ppermute | solution.py:38
  96.0 10.6 %collective-permute-start.23 = (bf16[64,4096]{1,0:T(8,128)(2,1)S(1)}, bf16[64,4096]{1,0:T(8,128)(2,1)S(1)}, u32[]{:S(2)}, u32[]{:S(2)}) collective-permute-start(bf16[64,4096]{1,0:T(8,128)(2,1)S(1)} %get-tuple-element.118), channel_id=1, source_target_pairs={{0,6},{1,3},{2,4},{3,1},{4,2},{5,7},{6,0},{7,5},{8,14},{9,11},{10,... | collective-permute-start | bytes 1572872 | tf_op jit(solution)/shard_map/ppermute | solution.py:38
  96.1 11.1 %collective-permute-start.24 = (bf16[64,4096]{1,0:T(8,128)(2,1)S(1)}, bf16[64,4096]{1,0:T(8,128)(2,1)S(1)}, u32[]{:S(2)}, u32[]{:S(2)}) collective-permute-start(bf16[64,4096]{1,0:T(8,128)(2,1)S(1)} %get-tuple-element.119), channel_id=1, source_target_pairs={{0,24},{1,9},{2,26},{3,11},{4,28},{5,13},{6,30},{7,15},{8,16},{9,1... | collective-permute-start | bytes 1572872 | tf_op jit(solution)/shard_map/ppermute | solution.py:38
  129.4 11.0 %collective-permute-start.35 = (bf16[64,4096]{1,0:T(8,128)(2,1)S(1)}, bf16[64,4096]{1,0:T(8,128)(2,1)S(1)}, u32[]{:S(2)}, u32[]{:S(2)}) collective-permute-start(bf16[64,4096]{1,0:T(8,128)(2,1)S(1)} %get-tuple-element.131.refs_0_), channel_id=1, source_target_pairs={{0,2},{1,7},{2,0},{3,5},{4,6},{5,3},{6,4},{7,1},{8,10},{9,15},{10,... | collective-permute-start | bytes 1572872 | tf_op jit(solution)/shard_map/ppermute | solution.py:38
  130.3 10.6 %collective-permute-start.36 = (bf16[64,4096]{1,0:T(8,128)(2,1)S(1)}, bf16[64,4096]{1,0:T(8,128)(2,1)S(1)}, u32[]{:S(2)}, u32[]{:S(2)}) collective-permute-start(bf16[64,4096]{1,0:T(8,128)(2,1)S(1)} %get-tuple-element.132.refs_1_), channel_id=1, source_target_pairs={{0,8},{1,25},{2,10},{3,27},{4,12},{5,29},{6,14},{7,31},{8,0},{9,17... | collective-permute-start | bytes 1572872 | tf_op jit(solution)/shard_map/ppermute | solution.py:38
  136.5 13.3 %collective-permute-start.32 = (bf16[64,4096]{1,0:T(8,128)(2,1)S(1)}, bf16[64,4096]{1,0:T(8,128)(2,1)S(1)}, u32[]{:S(2)}, u32[]{:S(2)}) collective-permute-start(bf16[64,4096]{1,0:T(8,128)(2,1)S(1)} %collective-permute-done.31.refs_2_), channel_id=1, source_target_pairs={{0,2},{1,7},{2,0},{3,5},{4,6},{5,3},{6,4},{7,1},{8,10},{9,15},{10,... | collective-permute-start | bytes 1572872 | tf_op jit(solution)/shard_map/ppermute | solution.py:38
  137.6 13.2 %collective-permute-start.34 = (bf16[64,4096]{1,0:T(8,128)(2,1)S(1)}, bf16[64,4096]{1,0:T(8,128)(2,1)S(1)}, u32[]{:S(2)}, u32[]{:S(2)}) collective-permute-start(bf16[64,4096]{1,0:T(8,128)(2,1)S(1)} %collective-permute-done.33.refs_3_), channel_id=1, source_target_pairs={{0,8},{1,25},{2,10},{3,27},{4,12},{5,29},{6,14},{7,31},{8,0},{9,17... | collective-permute-start | bytes 1572872 | tf_op jit(solution)/shard_map/ppermute | solution.py:38
  157.4 18.2 %collective-permute-start.45 = (bf16[384,4096]{1,0:T(8,128)(2,1)S(1)}, bf16[384,4096]{1,0:T(8,128)(2,1)S(1)}, u32[]{:S(2)}, u32[]{:S(2)}) collective-permute-start(bf16[384,4096]{1,0:T(8,128)(2,1)S(1)} %get-tuple-element.170.refs_4_), channel_id=1, source_target_pairs={{0,1},{1,0},{2,3},{3,2},{4,5},{5,4},{6,7},{7,6},{8,9},{9,8},{10,11... | collective-permute-start | bytes 9437192 | tf_op jit(solution)/shard_map/ppermute | solution.py:42
  166.2 22.0 %collective-permute-start.37 = (bf16[128,512]{1,0:T(8,128)(2,1)S(1)}, bf16[128,512]{1,0:T(8,128)(2,1)S(1)}, u32[]{:S(2)}, u32[]{:S(2)}) collective-permute-start(bf16[128,512]{1,0:T(8,128)(2,1)S(1)} %get-tuple-element.153), channel_id=1, source_target_pairs={{160,0},{192,32},{224,64},{161,1},{193,33},{225,65},{162,2},{194,3... | collective-permute-start | bytes 393224 | tf_op jit(solution)/shard_map/ppermute | solution.py:334
  167.5 24.8 %collective-permute-start.38 = (bf16[128,512]{1,0:T(8,128)(2,1)S(1)}, bf16[128,512]{1,0:T(8,128)(2,1)S(1)}, u32[]{:S(2)}, u32[]{:S(2)}) collective-permute-start(bf16[128,512]{1,0:T(8,128)(2,1)S(1)} %get-tuple-element.154), channel_id=1, source_target_pairs={{192,0},{224,32},{193,1},{225,33},{194,2},{226,34},{195,3},{227,35... | collective-permute-start | bytes 393224 | tf_op jit(solution)/shard_map/ppermute | solution.py:334
  173.0 27.9 %collective-permute-start.39 = (bf16[128,512]{1,0:T(8,128)(2,1)S(1)}, bf16[128,512]{1,0:T(8,128)(2,1)S(1)}, u32[]{:S(2)}, u32[]{:S(2)}) collective-permute-start(bf16[128,512]{1,0:T(8,128)(2,1)S(1)} %get-tuple-element.155), channel_id=1, source_target_pairs={{224,0},{225,1},{226,2},{227,3},{228,4},{229,5},{230,6},{231,7},{2... | collective-permute-start | bytes 393224 | tf_op jit(solution)/shard_map/ppermute | solution.py:334
  174.3 26.6 %collective-permute-start.42 = (bf16[128,512]{1,0:T(8,128)(2,1)S(1)}, bf16[128,512]{1,0:T(8,128)(2,1)S(1)}, u32[]{:S(2)}, u32[]{:S(2)}) collective-permute-start(bf16[128,512]{1,0:T(8,128)(2,1)S(1)} %get-tuple-element.164), channel_id=1, source_target_pairs={{32,0},{64,32},{96,64},{128,96},{160,128},{192,160},{224,192},{33,... | collective-permute-start | bytes 393224 | tf_op jit(solution)/shard_map/ppermute | solution.py:334
  175.6 25.3 %collective-permute-start.43 = (bf16[128,512]{1,0:T(8,128)(2,1)S(1)}, bf16[128,512]{1,0:T(8,128)(2,1)S(1)}, u32[]{:S(2)}, u32[]{:S(2)}) collective-permute-start(bf16[128,512]{1,0:T(8,128)(2,1)S(1)} %get-tuple-element.165), channel_id=1, source_target_pairs={{64,0},{96,32},{128,64},{160,96},{192,128},{224,160},{65,1},{97,33... | collective-permute-start | bytes 393224 | tf_op jit(solution)/shard_map/ppermute | solution.py:334
  (35 other events, 380.2 us)

commit v5 on v4

--- a/solution.py
+++ b/solution.py
@@ -310,11 +310,11 @@
         return [jnp.concatenate(pair, axis=0) for pair in zip(values, others)]
 
     group = [acts[0, c * part : (c + 1) * part] for c in chunks]
-    bias = jnp.concatenate([enc_bias, swap_cores(enc_bias)], axis=1)
     group = join(group, in_group(group, 0))
     group = join(group, in_group(group, 1))
-    *group, enc_own, dec_own = tie(*group, enc_weight[0], dec_weight[0])
+    *group, enc_own, dec_own, bias = tie(*group, enc_weight[0], dec_weight[0], enc_bias)
     encs = [enc_own, swap_cores(enc_own)]
+    bias = jnp.concatenate([bias, swap_cores(bias)], axis=1)
     decs = [dec_own.reshape(layers * rows, width)]
 
     def spread(group):
@@ -362,15 +362,13 @@
     late, hops, early_err = tie(late, hops, early_err)
     *hops, late_err = latent_grads(layer_arr, decs, late, hops, grad_scale, layers)
     relayed = [shift(hops[3], -2, 3), shift(hops[4], -2, 4)]
+    lats = [early_own, others[0], late_own, others[1]]
+    errs = [early_err, swap_cores(early_err), late_err, swap_cores(late_err)]
+    dec_grad = dec_grads(lats, errs, grad_scale).reshape(layers, rows, width)
     grads = [hops[0]] + [shift(hops[hop], -hop) for hop in range(5, layers)]
+    relayed, dec_grad = tie(relayed, dec_grad)
     near = vmem_call(add_body, [(h.shape, BF) for h in hops[1:3]], *hops[1:3], *relayed)
-    near, errs = tie(near, [early_err, late_err])
     grads += [shift(near[0], -1), shift(near[1], -2)]
-
-    lats = [early_own, others[0], late_own, others[1]]
-    errs = [errs[0], swap_cores(errs[0]), errs[1], swap_cores(errs[1])]
-    dec_grad = dec_grads(lats, errs, grad_scale).reshape(layers, rows, width)
-    grads, dec_grad = tie(grads, dec_grad)
 
     mask = jnp.concatenate([early_mask, late_mask], axis=1).astype(F32)
     grad = (sum(g.astype(F32) for g in grads) * mask).astype(BF)

time: 207 us -> 203 us (0.981)
  waiting for transfers between devices: 89 us -> 83.5 us
    ppermute x8, waiting for transfers between devices: 11.2 us -> 8.29 us  [swap_cores(): return lax.ppermute(value, 'tok', CORE_PAIRS)]
    ppermute x14, waiting for transfers between devices: 23.3 us -> 20.8 us  [shift(): return lax.ppermute(value, 'layer', pairs)]
  transfers between devices with their start and end apart: 48 -> 48, of which waited for: 28 -> 28; matrix products, arithmetic and copies ran while one was open for 0% -> 0% of each run, Pallas kernels for 13% -> 16%
where the time goes in v5:
time: 203 us; the launch traced here: 202 us
  waiting for transfers between devices  83.5 us (41%)
  starting transfers between devices  71.3 us (35%)
  Pallas kernels  38.2 us (19%)
  local copies, waits for them, and re-layouts  4.88 us (2%)
  matrix products  2.81 us (1%)
    ppermute x26, waiting for transfers between devices, exchange(): return lax.ppermute(value, 'tok', chip_pairs(axis, which))  54.5 us
    ppermute x26, starting transfers between devices, exchange(): return lax.ppermute(value, 'tok', chip_pairs(axis, which))  30 us
    ppermute x14, starting transfers between devices, shift(): return lax.ppermute(value, 'layer', pairs)  27 us
    ppermute x14, waiting for transfers between devices, shift(): return lax.ppermute(value, 'layer', pairs)  20.8 us
    ppermute x8, starting transfers between devices, swap_cores(): return lax.ppermute(value, 'tok', CORE_PAIRS)  14.3 us
    pallas_call x2, Pallas kernels, latent_grads(): pl.pallas_call(functools.partial(grads_body, scale, layers, len(errs)), g...  12.5 us
    pallas_call x2, Pallas kernels, recon(): pl.pallas_call(functools.partial(recon_body, start), grid_spec=pltpu.Pref...  11.3 us
    pallas_call x1, Pallas kernels, dec_grads(): pl.pallas_call(functools.partial(dec_grad_body, scale), grid=(width // bl...  8.9 us
  transfers between devices with their start and end apart: 48, of which 28 were waited for; matrix products, arithmetic and copies ran while one was open for 0% of the time, Pallas kernels for 16%

profile of v5, /device:TPU:1, one launch (start us, length us, event | category | flops | bytes accessed | tf_op | source)
XLA Modules:
  0.0 202.0 jit_solution(3156470770670647367)
XLA Ops:
  6.3 3.0 %collective-permute-start.3 = (bf16[32,4096]{1,0:T(8,128)(2,1)S(1)}, bf16[32,4096]{1,0:T(8,128)(2,1)S(1)}, u32[]{:S(2)}, u32[]{:S(2)}) collective-permute-start(bf16[32,4096]{1,0:T(8,128)(2,1)S(1)} %pad_maximum_fusion.3), channel_id=1, source_target_pairs={{0,2},{1,7},{2,0},{3,5},{4,6},{5,3},{6,4},{7,1},{8,10},{9,15},{10,... | collective-permute-start | bytes 786440 | tf_op jit(solution)/shard_map/ppermute | solution.py:38
  9.3 2.6 %collective-permute-start.1 = (bf16[32,4096]{1,0:T(8,128)(2,1)S(1)}, bf16[32,4096]{1,0:T(8,128)(2,1)S(1)}, u32[]{:S(2)}, u32[]{:S(2)}) collective-permute-start(bf16[32,4096]{1,0:T(8,128)(2,1)S(1)} %pad_maximum_fusion.2), channel_id=1, source_target_pairs={{0,8},{1,25},{2,10},{3,27},{4,12},{5,29},{6,14},{7,31},{8,0},{9,17... | collective-permute-start | bytes 786440 | tf_op jit(solution)/shard_map/ppermute | solution.py:38
  17.0 2.5 %collective-permute-start.9 = (bf16[64,4096]{1,0:T(8,128)(2,1)S(1)}, bf16[64,4096]{1,0:T(8,128)(2,1)S(1)}, u32[]{:S(2)}, u32[]{:S(2)}) collective-permute-start(bf16[64,4096]{1,0:T(8,128)(2,1)S(1)} %pad_maximum_fusion.1.refs_1_), channel_id=1, source_target_pairs={{0,8},{1,25},{2,10},{3,27},{4,12},{5,29},{6,14},{7,31},{8,0},{9,17... | collective-permute-start | bytes 1572872 | tf_op jit(solution)/shard_map/ppermute | solution.py:38
  19.5 6.8 %collective-permute-done.8.refs_4_ = bf16[64,4096]{1,0:T(8,128)(2,1)S(1)} collective-permute-done((bf16[64,4096]{1,0:T(8,128)(2,1)S(1)}, bf16[64,4096]{1,0:T(8,128)(2,1)S(1)}, u32[]{:S(2)}, u32[]{:S(2)}) %collective-permute-start.8) | collective-permute-done | bytes 524320 | tf_op jit(solution)/shard_map/ppermute | solution.py:38
  27.1 4.0 %collective-permute-done.6.refs_3_ = bf16[64,4096]{1,0:T(8,128)(2,1)S(1)} collective-permute-done((bf16[64,4096]{1,0:T(8,128)(2,1)S(1)}, bf16[64,4096]{1,0:T(8,128)(2,1)S(1)}, u32[]{:S(2)}, u32[]{:S(2)}) %collective-permute-start.6) | collective-permute-done | bytes 524320 | tf_op jit(solution)/shard_map/ppermute | solution.py:38
  31.1 2.7 %collective-permute-start.19 = (bf16[512,4096]{1,0:T(8,128)(2,1)}, bf16[512,4096]{1,0:T(8,128)(2,1)}, u32[]{:S(2)}, u32[]{:S(2)}) collective-permute-start(bf16[512,4096]{1,0:T(8,128)(2,1)} %bitcast.18), channel_id=1, source_target_pairs={{0,1},{1,0},{2,3},{3,2},{4,5},{5,4},{6,7},{7,6},{8,9},{9,8},{10,11... | collective-permute-start | bytes 12582920 | tf_op jit(solution)/shard_map/ppermute | solution.py:42
  36.7 4.7 %collective-permute-done.11 = f32[1,64]{1,0:T(1,128)S(1)} collective-permute-done((f32[1,64]{1,0:T(1,128)S(1)}, f32[1,64]{1,0:T(1,128)S(1)}, u32[]{:S(2)}, u32[]{:S(2)}) %collective-permute-start.11) | collective-permute-done | bytes 288 | tf_op jit(solution)/shard_map/ppermute | solution.py:42
  47.8 7.5 %collective-permute-start.18 = (bf16[512,128]{1,0:T(8,128)(2,1)S(1)}, bf16[512,128]{1,0:T(8,128)(2,1)S(1)}, u32[]{:S(2)}, u32[]{:S(2)}) collective-permute-start(bf16[512,128]{1,0:T(8,128)(2,1)S(1)} %get-tuple-element.101.refs_0_), channel_id=1, source_target_pairs={{0,224},{1,225},{2,226},{3,227},{4,228},{5,229},{6,230},{7,231},{8... | collective-permute-start | bytes 393224 | tf_op jit(solution)/shard_map/ppermute | solution.py:334
  58.5 3.1 %collective-permute-start.17 = (bf16[512,128]{1,0:T(8,128)(2,1)S(1)}, bf16[512,128]{1,0:T(8,128)(2,1)}, u32[]{:S(2)}, u32[]{:S(2)}) collective-permute-start(bf16[512,128]{1,0:T(8,128)(2,1)S(1)} %get-tuple-element.101.refs_0_), channel_id=1, source_target_pairs={{0,192},{32,224},{1,193},{33,225},{2,194},{34,226},{3,195},{35,227... | collective-permute-start | bytes 393224 | tf_op jit(solution)/shard_map/ppermute | solution.py:334
  61.6 2.8 %collective-permute-start.16 = (bf16[512,128]{1,0:T(8,128)(2,1)S(1)}, bf16[512,128]{1,0:T(8,128)(2,1)}, u32[]{:S(2)}, u32[]{:S(2)}) collective-permute-start(bf16[512,128]{1,0:T(8,128)(2,1)S(1)} %get-tuple-element.101.refs_0_), channel_id=1, source_target_pairs={{0,160},{32,192},{64,224},{1,161},{33,193},{65,225},{2,162},{34,19... | collective-permute-start | bytes 393224 | tf_op jit(solution)/shard_map/ppermute | solution.py:334
  67.1 5.4 %collective-permute-done.17.refs_6_ = bf16[512,128]{1,0:T(8,128)(2,1)} collective-permute-done((bf16[512,128]{1,0:T(8,128)(2,1)S(1)}, bf16[512,128]{1,0:T(8,128)(2,1)}, u32[]{:S(2)}, u32[]{:S(2)}) %collective-permute-start.17) | collective-permute-done | bytes 131104 | tf_op jit(solution)/shard_map/ppermute | solution.py:334
  72.5 2.8 %collective-permute-done.16.refs_5_ = bf16[512,128]{1,0:T(8,128)(2,1)} collective-permute-done((bf16[512,128]{1,0:T(8,128)(2,1)S(1)}, bf16[512,128]{1,0:T(8,128)(2,1)}, u32[]{:S(2)}, u32[]{:S(2)}) %collective-permute-start.16) | collective-permute-done | bytes 131104 | tf_op jit(solution)/shard_map/ppermute | solution.py:334
  77.5 4.6 %shard_map.79 = (bf16[64,4096]{1,0:T(8,128)(2,1)S(1)}, bf16[64,4096]{1,0:T(8,128)(2,1)S(1)}, bf16[128,512]{1,0:T(8,128)(2,1)S(1)}, bf16[128,512]{1,0:T(8,128)(2,1)S(1)}) custom-call(s32[1]{0:T(128)} %bitcast.layer_ref, bf16[512,128]{1,0:T(8,128)(2,1)S(1)} %get-tuple-element.101.refs_0_, bf16[512,128]{1,0:T(8,128)(2,1)} %collective-permute-done.12.refs_1_, ...), custom_call_target="tpu_custom_call" | custom-call | flops 1073741824 | bytes 8388608 | tf_op jit(solution)/shard_map/pallas_call | solution.py:94
  85.8 6.7 %shard_map.78 = (bf16[64,4096]{1,0:T(8,128)(2,1)S(1)}, bf16[64,4096]{1,0:T(8,128)(2,1)S(1)}, bf16[64,4096]{1,0:T(8,128)(2,1)S(1)}, bf16[64,4096]{1,0:T(8,128)(2,...) custom-call(s32[1]{0:T(128)} %bitcast.layer_ref, ...), custom_call_target="tpu_custom_call" | custom-call | flops 3221225472 | bytes 8388608 | tf_op jit(solution)/shard_map/pallas_call | solution.py:94
  96.2 8.3 %collective-permute-done.25.refs_4_ = bf16[64,4096]{1,0:T(8,128)(2,1)S(1)} collective-permute-done((bf16[64,4096]{1,0:T(8,128)(2,1)S(1)}, bf16[64,4096]{1,0:T(8,128)(2,1)S(1)}, u32[]{:S(2)}, u32[]{:S(2)}) %collective-permute-start.25) | collective-permute-done | bytes 524320 | tf_op jit(solution)/shard_map/ppermute | solution.py:38
  109.9 7.1 %collective-permute-done.27.refs_2_ = bf16[64,4096]{1,0:T(8,128)(2,1)S(1)} collective-permute-done((bf16[64,4096]{1,0:T(8,128)(2,1)S(1)}, bf16[64,4096]{1,0:T(8,128)(2,1)S(1)}, u32[]{:S(2)}, u32[]{:S(2)}) %collective-permute-start.27) | collective-permute-done | bytes 524320 | tf_op jit(solution)/shard_map/ppermute | solution.py:38
  119.3 7.7 %collective-permute-done.29.refs_2_ = bf16[64,4096]{1,0:T(8,128)(2,1)S(1)} collective-permute-done((bf16[64,4096]{1,0:T(8,128)(2,1)S(1)}, bf16[64,4096]{1,0:T(8,128)(2,1)S(1)}, u32[]{:S(2)}, u32[]{:S(2)}) %collective-permute-start.29) | collective-permute-done | bytes 524320 | tf_op jit(solution)/shard_map/ppermute | solution.py:38
  132.1 4.5 %collective-permute-done.31.refs_2_ = bf16[64,4096]{1,0:T(8,128)(2,1)S(1)} collective-permute-done((bf16[64,4096]{1,0:T(8,128)(2,1)S(1)}, bf16[64,4096]{1,0:T(8,128)(2,1)S(1)}, u32[]{:S(2)}, u32[]{:S(2)}) %collective-permute-start.31) | collective-permute-done | bytes 524320 | tf_op jit(solution)/shard_map/ppermute | solution.py:38
  140.9 7.3 %shard_map.84 = (bf16[128,384]{1,0:T(8,128)(2,1)S(1)}, bf16[128,384]{1,0:T(8,128)(2,1)S(1)}, bf16[128,384]{1,0:T(8,128)(2,1)S(1)}, bf16[128,384]{1,0:T(8,128)(2,...) custom-call(s32[1]{0:T(128)} %bitcast.layer_ref, ...), custom_call_target="tpu_custom_call" | custom-call | flops 3221225472 | bytes 8388608 | tf_op jit(solution)/shard_map/pallas_call | solution.py:149
  150.8 8.2 %collective-permute-start.40 = (bf16[384,4096]{1,0:T(8,128)(2,1)S(1)}, bf16[384,4096]{1,0:T(8,128)(2,1)S(1)}, u32[]{:S(2)}, u32[]{:S(2)}) collective-permute-start(bf16[384,4096]{1,0:T(8,128)(2,1)S(1)} %get-tuple-element.152.refs_4_), channel_id=1, source_target_pairs={{0,1},{1,0},{2,3},{3,2},{4,5},{5,4},{6,7},{7,6},{8,9},{9,8},{10,11... | collective-permute-start | bytes 9437192 | tf_op jit(solution)/shard_map/ppermute | solution.py:42
  158.9 5.2 %shard_map.85 = (bf16[128,512]{1,0:T(8,128)(2,1)S(1)}, bf16[128,512]{1,0:T(8,128)(2,1)S(1)}, bf16[128,512]{1,0:T(8,128)(2,1)S(1)}, bf16[128,512]{1,0:T(8,128)(2,...) custom-call(s32[1]{0:T(128)} %bitcast.layer_ref, ...), custom_call_target="tpu_custom_call" | custom-call | flops 1073741824 | bytes 8388608 | tf_op jit(solution)/shard_map/pallas_call | solution.py:149
  171.4 8.9 %shard_map.86 = bf16[512,4096]{1,0:T(8,128)(2,1)} custom-call(bf16[384,512]{1,0:T(8,128)(2,1)S(1)} %get-tuple-element.148.refs_0_, bf16[384,512]{1,0:T(8,128)(2,1)S(1)} %collective-permute-done.39.refs_1_, bf16[128,512]{1,0:T(8,128)(2,1)S(1)} %get-tuple-element.150.refs_2_, bf16[128,512]{1,0:T(8,128)(2,1)S(1)} %collective-permute-done.20.refs_3_, ...), custom_call_target="tpu_custom_call" | custom-call | flops 4294967296 | bytes 12582912 | tf_op jit(solution)/shard_map/pallas_call | solution.py:232
  183.0 3.5 %collective-permute-done.43 = bf16[128,512]{1,0:T(8,128)(2,1)S(1)} collective-permute-done((bf16[128,512]{1,0:T(8,128)(2,1)S(1)}, bf16[128,512]{1,0:T(8,128)(2,1)S(1)}, u32[]{:S(2)}, u32[]{:S(2)}) %collective-permute-start.43) | collective-permute-done | bytes 131104 | tf_op jit(solution)/shard_map/ppermute | solution.py:334
  186.5 8.8 %collective-permute-done.44 = bf16[128,512]{1,0:T(8,128)(2,1)S(1)} collective-permute-done((bf16[128,512]{1,0:T(8,128)(2,1)S(1)}, bf16[128,512]{1,0:T(8,128)(2,1)S(1)}, u32[]{:S(2)}, u32[]{:S(2)}) %collective-permute-start.44) | collective-permute-done | bytes 131104 | tf_op jit(solution)/shard_map/ppermute | solution.py:334
  (117 shorter events, 72.4 us)
Async XLA Ops:
  16.4 10.7 %collective-permute-start.4 = (bf16[64,4096]{1,0:T(8,128)(2,1)S(1)}, bf16[64,4096]{1,0:T(8,128)(2,1)S(1)}, u32[]{:S(2)}, u32[]{:S(2)}) collective-permute-start(bf16[64,4096]{1,0:T(8,128)(2,1)S(1)} %pad_maximum_fusion.refs_0_), channel_id=1, source_target_pairs={{0,6},{1,3},{2,4},{3,1},{4,2},{5,7},{6,0},{7,5},{8,14},{9,11},{10,... | collective-permute-start | bytes 1572872 | tf_op jit(solution)/shard_map/ppermute | solution.py:38
  19.5 11.7 %collective-permute-start.6 = (bf16[64,4096]{1,0:T(8,128)(2,1)S(1)}, bf16[64,4096]{1,0:T(8,128)(2,1)S(1)}, u32[]{:S(2)}, u32[]{:S(2)}) collective-permute-start(bf16[64,4096]{1,0:T(8,128)(2,1)S(1)} %pad_maximum_fusion.1.refs_1_), channel_id=1, source_target_pairs={{0,24},{1,9},{2,26},{3,11},{4,28},{5,13},{6,30},{7,15},{8,16},{9,1... | collective-permute-start | bytes 1572872 | tf_op jit(solution)/shard_map/ppermute | solution.py:38
  31.1 44.1 %collective-permute-start.19 = (bf16[512,4096]{1,0:T(8,128)(2,1)}, bf16[512,4096]{1,0:T(8,128)(2,1)}, u32[]{:S(2)}, u32[]{:S(2)}) collective-permute-start(bf16[512,4096]{1,0:T(8,128)(2,1)} %bitcast.18), channel_id=1, source_target_pairs={{0,1},{1,0},{2,3},{3,2},{4,5},{5,4},{6,7},{7,6},{8,9},{9,8},{10,11... | collective-permute-start | bytes 12582920 | tf_op jit(solution)/shard_map/ppermute | solution.py:42
  47.8 13.8 %collective-permute-start.18 = (bf16[512,128]{1,0:T(8,128)(2,1)S(1)}, bf16[512,128]{1,0:T(8,128)(2,1)S(1)}, u32[]{:S(2)}, u32[]{:S(2)}) collective-permute-start(bf16[512,128]{1,0:T(8,128)(2,1)S(1)} %get-tuple-element.101.refs_0_), channel_id=1, source_target_pairs={{0,224},{1,225},{2,226},{3,227},{4,228},{5,229},{6,230},{7,231},{8... | collective-permute-start | bytes 393224 | tf_op jit(solution)/shard_map/ppermute | solution.py:334
  58.5 13.9 %collective-permute-start.17 = (bf16[512,128]{1,0:T(8,128)(2,1)S(1)}, bf16[512,128]{1,0:T(8,128)(2,1)}, u32[]{:S(2)}, u32[]{:S(2)}) collective-permute-start(bf16[512,128]{1,0:T(8,128)(2,1)S(1)} %get-tuple-element.101.refs_0_), channel_id=1, source_target_pairs={{0,192},{32,224},{1,193},{33,225},{2,194},{34,226},{3,195},{35,227... | collective-permute-start | bytes 393224 | tf_op jit(solution)/shard_map/ppermute | solution.py:334
  61.6 13.7 %collective-permute-start.16 = (bf16[512,128]{1,0:T(8,128)(2,1)S(1)}, bf16[512,128]{1,0:T(8,128)(2,1)}, u32[]{:S(2)}, u32[]{:S(2)}) collective-permute-start(bf16[512,128]{1,0:T(8,128)(2,1)S(1)} %get-tuple-element.101.refs_0_), channel_id=1, source_target_pairs={{0,160},{32,192},{64,224},{1,161},{33,193},{65,225},{2,162},{34,19... | collective-permute-start | bytes 393224 | tf_op jit(solution)/shard_map/ppermute | solution.py:334
  64.5 10.8 %collective-permute-start.15 = (bf16[512,128]{1,0:T(8,128)(2,1)S(1)}, bf16[512,128]{1,0:T(8,128)(2,1)}, u32[]{:S(2)}, u32[]{:S(2)}) collective-permute-start(bf16[512,128]{1,0:T(8,128)(2,1)S(1)} %collective-permute-done.13.refs_2_), channel_id=1, source_target_pairs={{64,128},{96,160},{128,192},{160,224},{65,129},{97,161},{129,193},... | collective-permute-start | bytes 393224 | tf_op jit(solution)/shard_map/ppermute | solution.py:334
  83.6 12.1 %collective-permute-start.21 = (bf16[64,4096]{1,0:T(8,128)(2,1)S(1)}, bf16[64,4096]{1,0:T(8,128)(2,1)S(1)}, u32[]{:S(2)}, u32[]{:S(2)}) collective-permute-start(bf16[64,4096]{1,0:T(8,128)(2,1)S(1)} %get-tuple-element.110), channel_id=1, source_target_pairs={{0,2},{1,7},{2,0},{3,5},{4,6},{5,3},{6,4},{7,1},{8,10},{9,15},{10,... | collective-permute-start | bytes 1572872 | tf_op jit(solution)/shard_map/ppermute | solution.py:38
  84.7 11.1 %collective-permute-start.22 = (bf16[64,4096]{1,0:T(8,128)(2,1)S(1)}, bf16[64,4096]{1,0:T(8,128)(2,1)S(1)}, u32[]{:S(2)}, u32[]{:S(2)}) collective-permute-start(bf16[64,4096]{1,0:T(8,128)(2,1)S(1)} %get-tuple-element.111), channel_id=1, source_target_pairs={{0,8},{1,25},{2,10},{3,27},{4,12},{5,29},{6,14},{7,31},{8,0},{9,17... | collective-permute-start | bytes 1572872 | tf_op jit(solution)/shard_map/ppermute | solution.py:38
  92.5 12.1 %collective-permute-start.25 = (bf16[64,4096]{1,0:T(8,128)(2,1)S(1)}, bf16[64,4096]{1,0:T(8,128)(2,1)S(1)}, u32[]{:S(2)}, u32[]{:S(2)}) collective-permute-start(bf16[64,4096]{1,0:T(8,128)(2,1)S(1)} %get-tuple-element.114), channel_id=1, source_target_pairs={{0,2},{1,7},{2,0},{3,5},{4,6},{5,3},{6,4},{7,1},{8,10},{9,15},{10,... | collective-permute-start | bytes 1572872 | tf_op jit(solution)/shard_map/ppermute | solution.py:38
  94.2 12.4 %collective-permute-start.26 = (bf16[64,4096]{1,0:T(8,128)(2,1)S(1)}, bf16[64,4096]{1,0:T(8,128)(2,1)S(1)}, u32[]{:S(2)}, u32[]{:S(2)}) collective-permute-start(bf16[64,4096]{1,0:T(8,128)(2,1)S(1)} %get-tuple-element.115), channel_id=1, source_target_pairs={{0,8},{1,25},{2,10},{3,27},{4,12},{5,29},{6,14},{7,31},{8,0},{9,17... | collective-permute-start | bytes 1572872 | tf_op jit(solution)/shard_map/ppermute | solution.py:38
  96.1 11.1 %collective-permute-start.24 = (bf16[64,4096]{1,0:T(8,128)(2,1)S(1)}, bf16[64,4096]{1,0:T(8,128)(2,1)S(1)}, u32[]{:S(2)}, u32[]{:S(2)}) collective-permute-start(bf16[64,4096]{1,0:T(8,128)(2,1)S(1)} %get-tuple-element.113), channel_id=1, source_target_pairs={{0,24},{1,9},{2,26},{3,11},{4,28},{5,13},{6,30},{7,15},{8,16},{9,1... | collective-permute-start | bytes 1572872 | tf_op jit(solution)/shard_map/ppermute | solution.py:38
  129.4 11.0 %collective-permute-start.35 = (bf16[64,4096]{1,0:T(8,128)(2,1)S(1)}, bf16[64,4096]{1,0:T(8,128)(2,1)S(1)}, u32[]{:S(2)}, u32[]{:S(2)}) collective-permute-start(bf16[64,4096]{1,0:T(8,128)(2,1)S(1)} %get-tuple-element.125.refs_0_), channel_id=1, source_target_pairs={{0,2},{1,7},{2,0},{3,5},{4,6},{5,3},{6,4},{7,1},{8,10},{9,15},{10,... | collective-permute-start | bytes 1572872 | tf_op jit(solution)/shard_map/ppermute | solution.py:38
  130.3 10.6 %collective-permute-start.36 = (bf16[64,4096]{1,0:T(8,128)(2,1)S(1)}, bf16[64,4096]{1,0:T(8,128)(2,1)S(1)}, u32[]{:S(2)}, u32[]{:S(2)}) collective-permute-start(bf16[64,4096]{1,0:T(8,128)(2,1)S(1)} %get-tuple-element.126.refs_1_), channel_id=1, source_target_pairs={{0,8},{1,25},{2,10},{3,27},{4,12},{5,29},{6,14},{7,31},{8,0},{9,17... | collective-permute-start | bytes 1572872 | tf_op jit(solution)/shard_map/ppermute | solution.py:38
  136.5 13.3 %collective-permute-start.32 = (bf16[64,4096]{1,0:T(8,128)(2,1)S(1)}, bf16[64,4096]{1,0:T(8,128)(2,1)S(1)}, u32[]{:S(2)}, u32[]{:S(2)}) collective-permute-start(bf16[64,4096]{1,0:T(8,128)(2,1)S(1)} %collective-permute-done.31.refs_2_), channel_id=1, source_target_pairs={{0,2},{1,7},{2,0},{3,5},{4,6},{5,3},{6,4},{7,1},{8,10},{9,15},{10,... | collective-permute-start | bytes 1572872 | tf_op jit(solution)/shard_map/ppermute | solution.py:38
  137.6 13.2 %collective-permute-start.34 = (bf16[64,4096]{1,0:T(8,128)(2,1)S(1)}, bf16[64,4096]{1,0:T(8,128)(2,1)S(1)}, u32[]{:S(2)}, u32[]{:S(2)}) collective-permute-start(bf16[64,4096]{1,0:T(8,128)(2,1)S(1)} %collective-permute-done.33.refs_3_), channel_id=1, source_target_pairs={{0,8},{1,25},{2,10},{3,27},{4,12},{5,29},{6,14},{7,31},{8,0},{9,17... | collective-permute-start | bytes 1572872 | tf_op jit(solution)/shard_map/ppermute | solution.py:38
  150.8 19.3 %collective-permute-start.40 = (bf16[384,4096]{1,0:T(8,128)(2,1)S(1)}, bf16[384,4096]{1,0:T(8,128)(2,1)S(1)}, u32[]{:S(2)}, u32[]{:S(2)}) collective-permute-start(bf16[384,4096]{1,0:T(8,128)(2,1)S(1)} %get-tuple-element.152.refs_4_), channel_id=1, source_target_pairs={{0,1},{1,0},{2,3},{3,2},{4,5},{5,4},{6,7},{7,6},{8,9},{9,8},{10,11... | collective-permute-start | bytes 9437192 | tf_op jit(solution)/shard_map/ppermute | solution.py:42
  164.7 15.6 %collective-permute-start.37 = (bf16[128,512]{1,0:T(8,128)(2,1)S(1)}, bf16[128,512]{1,0:T(8,128)(2,1)S(1)}, u32[]{:S(2)}, u32[]{:S(2)}) collective-permute-start(bf16[128,512]{1,0:T(8,128)(2,1)S(1)} %get-tuple-element.146), channel_id=1, source_target_pairs={{96,32},{128,64},{160,96},{192,128},{224,160},{97,33},{129,65},{16... | collective-permute-start | bytes 393224 | tf_op jit(solution)/shard_map/ppermute | solution.py:334
  165.4 14.9 %collective-permute-start.38 = (bf16[128,512]{1,0:T(8,128)(2,1)S(1)}, bf16[128,512]{1,0:T(8,128)(2,1)S(1)}, u32[]{:S(2)}, u32[]{:S(2)}) collective-permute-start(bf16[128,512]{1,0:T(8,128)(2,1)S(1)} %get-tuple-element.147), channel_id=1, source_target_pairs={{128,64},{160,96},{192,128},{224,160},{129,65},{161,97},{193,129},... | collective-permute-start | bytes 393224 | tf_op jit(solution)/shard_map/ppermute | solution.py:334
  167.5 15.5 %collective-permute-start.42 = (bf16[128,512]{1,0:T(8,128)(2,1)S(1)}, bf16[128,512]{1,0:T(8,128)(2,1)S(1)}, u32[]{:S(2)}, u32[]{:S(2)}) collective-permute-start(bf16[128,512]{1,0:T(8,128)(2,1)S(1)} %get-tuple-element.156), channel_id=1, source_target_pairs={{160,0},{192,32},{224,64},{161,1},{193,33},{225,65},{162,2},{194,3... | collective-permute-start | bytes 393224 | tf_op jit(solution)/shard_map/ppermute | solution.py:334
  168.8 17.7 %collective-permute-start.43 = (bf16[128,512]{1,0:T(8,128)(2,1)S(1)}, bf16[128,512]{1,0:T(8,128)(2,1)S(1)}, u32[]{:S(2)}, u32[]{:S(2)}) collective-permute-start(bf16[128,512]{1,0:T(8,128)(2,1)S(1)} %get-tuple-element.157), channel_id=1, source_target_pairs={{192,0},{224,32},{193,1},{225,33},{194,2},{226,34},{195,3},{227,35... | collective-permute-start | bytes 393224 | tf_op jit(solution)/shard_map/ppermute | solution.py:334
  170.1 25.2 %collective-permute-start.44 = (bf16[128,512]{1,0:T(8,128)(2,1)S(1)}, bf16[128,512]{1,0:T(8,128)(2,1)S(1)}, u32[]{:S(2)}, u32[]{:S(2)}) collective-permute-start(bf16[128,512]{1,0:T(8,128)(2,1)S(1)} %get-tuple-element.158), channel_id=1, source_target_pairs={{224,0},{225,1},{226,2},{227,3},{228,4},{229,5},{230,6},{231,7},{2... | collective-permute-start | bytes 393224 | tf_op jit(solution)/shard_map/ppermute | solution.py:334
  180.4 14.9 %collective-permute-start.45 = (bf16[128,512]{1,0:T(8,128)(2,1)S(1)}, bf16[128,512]{1,0:T(8,128)(2,1)S(1)}, u32[]{:S(2)}, u32[]{:S(2)}) collective-permute-start(bf16[128,512]{1,0:T(8,128)(2,1)S(1)} %get-tuple-element.163), channel_id=1, source_target_pairs={{32,0},{64,32},{96,64},{128,96},{160,128},{192,160},{224,192},{33,... | collective-permute-start | bytes 393224 | tf_op jit(solution)/shard_map/ppermute | solution.py:334
  181.7 13.9 %collective-permute-start.46 = (bf16[128,512]{1,0:T(8,128)(2,1)S(1)}, bf16[128,512]{1,0:T(8,128)(2,1)S(1)}, u32[]{:S(2)}, u32[]{:S(2)}) collective-permute-start(bf16[128,512]{1,0:T(8,128)(2,1)S(1)} %get-tuple-element.164), channel_id=1, source_target_pairs={{64,0},{96,32},{128,64},{160,96},{192,128},{224,160},{65,1},{97,33... | collective-permute-start | bytes 393224 | tf_op jit(solution)/shard_map/ppermute | solution.py:334
  (35 other events, 393.3 us)

commit v6 on v5

--- a/solution.py
+++ b/solution.py
@@ -219,26 +219,30 @@
 
 
 def dec_grad_body(scale, *refs):
-    lats, errs, out = refs[:4], refs[4:8], refs[8]
+    lats, errs, out = refs[:4], refs[4:8], refs[-1]
     total = dot(lats[0][...], errs[0][...], 0, 0)
     for lat, err in zip(lats[1:], errs[1:]):
         total += dot(lat[...], err[...], 0, 0)
     out[...] = (scale * total).astype(BF)
 
 
-def dec_grads(lats, errs, scale, block=1024):
+def dec_grads(lats, errs, scale, start, before=(), block=1024):
     tokens = sum(lat.shape[0] for lat in lats) // 4
     depth, width = lats[0].shape[1], errs[0].shape[1]
+    steps = width // block // 2
+    column = lambda i: (0, i + start * steps)
     return pl.pallas_call(
         functools.partial(dec_grad_body, scale),
-        grid=(width // block,),
+        grid=(steps,),
         in_specs=[pl.BlockSpec(lat.shape, lambda i: (0, 0)) for lat in lats]
-        + [pl.BlockSpec((err.shape[0], block), lambda i: (0, i)) for err in errs],
-        out_specs=pl.BlockSpec((depth, block), lambda i: (0, i)),
+        + [pl.BlockSpec((err.shape[0], block), column) for err in errs]
+        + [pl.BlockSpec(memory_space=pl.ANY)] * len(before),
+        out_specs=pl.BlockSpec((depth, block), column),
         out_shape=jax.ShapeDtypeStruct((depth, width), BF),
+        input_output_aliases={8: 0} if before else {},
         compiler_params=params(),
-        cost_estimate=cost(8 * tokens * depth * width, 8 * tokens * width + 2 * depth * width),
-    )(*lats, *errs)
+        cost_estimate=cost(4 * tokens * depth * width, 4 * tokens * width + depth * width),
+    )(*lats, *errs, *before)
 
 
 def vmem_call(body, outs, *operands):
@@ -364,11 +368,15 @@
     relayed = [shift(hops[3], -2, 3), shift(hops[4], -2, 4)]
     lats = [early_own, others[0], late_own, others[1]]
     errs = [early_err, swap_cores(early_err), late_err, swap_cores(late_err)]
-    dec_grad = dec_grads(lats, errs, grad_scale).reshape(layers, rows, width)
+    dec_grad = dec_grads(lats, errs, grad_scale, 0)
     grads = [hops[0]] + [shift(hops[hop], -hop) for hop in range(5, layers)]
     relayed, dec_grad = tie(relayed, dec_grad)
     near = vmem_call(add_body, [(h.shape, BF) for h in hops[1:3]], *hops[1:3], *relayed)
+    near, dec_grad = tie(near, dec_grad)
     grads += [shift(near[0], -1), shift(near[1], -2)]
+    dec_grad = dec_grads(lats, errs, grad_scale, 1, [dec_grad])
+    grads, dec_grad = tie(grads, dec_grad)
+    dec_grad = dec_grad.reshape(layers, rows, width)
 
     mask = jnp.concatenate([early_mask, late_mask], axis=1).astype(F32)
     grad = (sum(g.astype(F32) for g in grads) * mask).astype(BF)

time: 203 us -> 206 us (1.015)
  waiting for transfers between devices: 83.5 us -> 85.9 us
    ppermute x14, waiting for transfers between devices: 20.8 us -> 24.4 us  [shift(): return lax.ppermute(value, 'layer', pairs)]
    pallas_call x1 -> x2, Pallas kernels: 8.9 us -> 9.9 us  [dec_grads(): pl.pallas_call(functools.partial(dec_grad_body, scale), grid=(steps,), in...]
  transfers between devices with their start and end apart: 48 -> 48, of which waited for: 28 -> 27; matrix products, arithmetic and copies ran while one was open for 0% -> 0% of each run, Pallas kernels for 16% -> 16%
where the time goes in v6:
time: 206 us; the launch traced here: 205 us
  waiting for transfers between devices  85.9 us (42%)
  starting transfers between devices  70.6 us (34%)
  Pallas kernels  39.2 us (19%)
  local copies, waits for them, and re-layouts  4.88 us (2%)
  matrix products  2.81 us (1%)
    ppermute x26, waiting for transfers between devices, exchange(): return lax.ppermute(value, 'tok', chip_pairs(axis, which))  54.4 us
    ppermute x26, starting transfers between devices, exchange(): return lax.ppermute(value, 'tok', chip_pairs(axis, which))  30 us
    ppermute x14, starting transfers between devices, shift(): return lax.ppermute(value, 'layer', pairs)  27.2 us
    ppermute x14, waiting for transfers between devices, shift(): return lax.ppermute(value, 'layer', pairs)  24.4 us
    ppermute x8, starting transfers between devices, swap_cores(): return lax.ppermute(value, 'tok', CORE_PAIRS)  13.4 us
    pallas_call x2, Pallas kernels, latent_grads(): pl.pallas_call(functools.partial(grads_body, scale, layers, len(errs)), g...  12.5 us
    pallas_call x2, Pallas kernels, recon(): pl.pallas_call(functools.partial(recon_body, start), grid_spec=pltpu.Pref...  11.3 us
    pallas_call x2, Pallas kernels, dec_grads(): pl.pallas_call(functools.partial(dec_grad_body, scale), grid=(steps,), in...  9.9 us
  transfers between devices with their start and end apart: 48, of which 27 were waited for; matrix products, arithmetic and copies ran while one was open for 0% of the time, Pallas kernels for 16%

profile of v6, /device:TPU:1, one launch (start us, length us, event | category | flops | bytes accessed | tf_op | source)
XLA Modules:
  0.0 204.7 jit_solution(6312866285524900433)
XLA Ops:
  6.3 3.0 %collective-permute-start.3 = (bf16[32,4096]{1,0:T(8,128)(2,1)S(1)}, bf16[32,4096]{1,0:T(8,128)(2,1)S(1)}, u32[]{:S(2)}, u32[]{:S(2)}) collective-permute-start(bf16[32,4096]{1,0:T(8,128)(2,1)S(1)} %pad_maximum_fusion.3), channel_id=1, source_target_pairs={{0,2},{1,7},{2,0},{3,5},{4,6},{5,3},{6,4},{7,1},{8,10},{9,15},{10,... | collective-permute-start | bytes 786440 | tf_op jit(solution)/shard_map/ppermute | solution.py:38
  9.3 2.6 %collective-permute-start.1 = (bf16[32,4096]{1,0:T(8,128)(2,1)S(1)}, bf16[32,4096]{1,0:T(8,128)(2,1)S(1)}, u32[]{:S(2)}, u32[]{:S(2)}) collective-permute-start(bf16[32,4096]{1,0:T(8,128)(2,1)S(1)} %pad_maximum_fusion.2), channel_id=1, source_target_pairs={{0,8},{1,25},{2,10},{3,27},{4,12},{5,29},{6,14},{7,31},{8,0},{9,17... | collective-permute-start | bytes 786440 | tf_op jit(solution)/shard_map/ppermute | solution.py:38
  19.5 6.8 %collective-permute-done.8.refs_4_ = bf16[64,4096]{1,0:T(8,128)(2,1)S(1)} collective-permute-done((bf16[64,4096]{1,0:T(8,128)(2,1)S(1)}, bf16[64,4096]{1,0:T(8,128)(2,1)S(1)}, u32[]{:S(2)}, u32[]{:S(2)}) %collective-permute-start.8) | collective-permute-done | bytes 524320 | tf_op jit(solution)/shard_map/ppermute | solution.py:38
  27.1 4.0 %collective-permute-done.6.refs_3_ = bf16[64,4096]{1,0:T(8,128)(2,1)S(1)} collective-permute-done((bf16[64,4096]{1,0:T(8,128)(2,1)S(1)}, bf16[64,4096]{1,0:T(8,128)(2,1)S(1)}, u32[]{:S(2)}, u32[]{:S(2)}) %collective-permute-start.6) | collective-permute-done | bytes 524320 | tf_op jit(solution)/shard_map/ppermute | solution.py:38
  31.1 2.7 %collective-permute-start.19 = (bf16[512,4096]{1,0:T(8,128)(2,1)}, bf16[512,4096]{1,0:T(8,128)(2,1)}, u32[]{:S(2)}, u32[]{:S(2)}) collective-permute-start(bf16[512,4096]{1,0:T(8,128)(2,1)} %bitcast.17), channel_id=1, source_target_pairs={{0,1},{1,0},{2,3},{3,2},{4,5},{5,4},{6,7},{7,6},{8,9},{9,8},{10,11... | collective-permute-start | bytes 12582920 | tf_op jit(solution)/shard_map/ppermute | solution.py:42
  36.7 4.7 %collective-permute-done.11 = f32[1,64]{1,0:T(1,128)S(1)} collective-permute-done((f32[1,64]{1,0:T(1,128)S(1)}, f32[1,64]{1,0:T(1,128)S(1)}, u32[]{:S(2)}, u32[]{:S(2)}) %collective-permute-start.11) | collective-permute-done | bytes 288 | tf_op jit(solution)/shard_map/ppermute | solution.py:42
  47.8 7.5 %collective-permute-start.18 = (bf16[512,128]{1,0:T(8,128)(2,1)S(1)}, bf16[512,128]{1,0:T(8,128)(2,1)S(1)}, u32[]{:S(2)}, u32[]{:S(2)}) collective-permute-start(bf16[512,128]{1,0:T(8,128)(2,1)S(1)} %get-tuple-element.111.refs_0_), channel_id=1, source_target_pairs={{0,224},{1,225},{2,226},{3,227},{4,228},{5,229},{6,230},{7,231},{8... | collective-permute-start | bytes 393224 | tf_op jit(solution)/shard_map/ppermute | solution.py:338
  58.5 3.1 %collective-permute-start.17 = (bf16[512,128]{1,0:T(8,128)(2,1)S(1)}, bf16[512,128]{1,0:T(8,128)(2,1)}, u32[]{:S(2)}, u32[]{:S(2)}) collective-permute-start(bf16[512,128]{1,0:T(8,128)(2,1)S(1)} %get-tuple-element.111.refs_0_), channel_id=1, source_target_pairs={{0,192},{32,224},{1,193},{33,225},{2,194},{34,226},{3,195},{35,227... | collective-permute-start | bytes 393224 | tf_op jit(solution)/shard_map/ppermute | solution.py:338
  61.6 2.8 %collective-permute-start.16 = (bf16[512,128]{1,0:T(8,128)(2,1)S(1)}, bf16[512,128]{1,0:T(8,128)(2,1)}, u32[]{:S(2)}, u32[]{:S(2)}) collective-permute-start(bf16[512,128]{1,0:T(8,128)(2,1)S(1)} %get-tuple-element.111.refs_0_), channel_id=1, source_target_pairs={{0,160},{32,192},{64,224},{1,161},{33,193},{65,225},{2,162},{34,19... | collective-permute-start | bytes 393224 | tf_op jit(solution)/shard_map/ppermute | solution.py:338
  67.1 5.4 %collective-permute-done.17.refs_6_ = bf16[512,128]{1,0:T(8,128)(2,1)} collective-permute-done((bf16[512,128]{1,0:T(8,128)(2,1)S(1)}, bf16[512,128]{1,0:T(8,128)(2,1)}, u32[]{:S(2)}, u32[]{:S(2)}) %collective-permute-start.17) | collective-permute-done | bytes 131104 | tf_op jit(solution)/shard_map/ppermute | solution.py:338
  72.5 2.8 %collective-permute-done.16.refs_5_ = bf16[512,128]{1,0:T(8,128)(2,1)} collective-permute-done((bf16[512,128]{1,0:T(8,128)(2,1)S(1)}, bf16[512,128]{1,0:T(8,128)(2,1)}, u32[]{:S(2)}, u32[]{:S(2)}) %collective-permute-start.16) | collective-permute-done | bytes 131104 | tf_op jit(solution)/shard_map/ppermute | solution.py:338
  77.5 4.6 %shard_map.79 = (bf16[64,4096]{1,0:T(8,128)(2,1)S(1)}, bf16[64,4096]{1,0:T(8,128)(2,1)S(1)}, bf16[128,512]{1,0:T(8,128)(2,1)S(1)}, bf16[128,512]{1,0:T(8,128)(2,1)S(1)}) custom-call(s32[1]{0:T(128)} %bitcast.layer_ref, bf16[512,128]{1,0:T(8,128)(2,1)S(1)} %get-tuple-element.111.refs_0_, bf16[512,128]{1,0:T(8,128)(2,1)} %collective-permute-done.12.refs_1_, ...), custom_call_target="tpu_custom_call" | custom-call | flops 1073741824 | bytes 8388608 | tf_op jit(solution)/shard_map/pallas_call | solution.py:94
  85.8 6.7 %shard_map.78 = (bf16[64,4096]{1,0:T(8,128)(2,1)S(1)}, bf16[64,4096]{1,0:T(8,128)(2,1)S(1)}, bf16[64,4096]{1,0:T(8,128)(2,1)S(1)}, bf16[64,4096]{1,0:T(8,128)(2,...) custom-call(s32[1]{0:T(128)} %bitcast.layer_ref, ...), custom_call_target="tpu_custom_call" | custom-call | flops 3221225472 | bytes 8388608 | tf_op jit(solution)/shard_map/pallas_call | solution.py:94
  96.2 8.3 %collective-permute-done.25.refs_4_ = bf16[64,4096]{1,0:T(8,128)(2,1)S(1)} collective-permute-done((bf16[64,4096]{1,0:T(8,128)(2,1)S(1)}, bf16[64,4096]{1,0:T(8,128)(2,1)S(1)}, u32[]{:S(2)}, u32[]{:S(2)}) %collective-permute-start.25) | collective-permute-done | bytes 524320 | tf_op jit(solution)/shard_map/ppermute | solution.py:38
  109.9 7.1 %collective-permute-done.27.refs_2_ = bf16[64,4096]{1,0:T(8,128)(2,1)S(1)} collective-permute-done((bf16[64,4096]{1,0:T(8,128)(2,1)S(1)}, bf16[64,4096]{1,0:T(8,128)(2,1)S(1)}, u32[]{:S(2)}, u32[]{:S(2)}) %collective-permute-start.27) | collective-permute-done | bytes 524320 | tf_op jit(solution)/shard_map/ppermute | solution.py:38
  119.3 7.7 %collective-permute-done.29.refs_2_ = bf16[64,4096]{1,0:T(8,128)(2,1)S(1)} collective-permute-done((bf16[64,4096]{1,0:T(8,128)(2,1)S(1)}, bf16[64,4096]{1,0:T(8,128)(2,1)S(1)}, u32[]{:S(2)}, u32[]{:S(2)}) %collective-permute-start.29) | collective-permute-done | bytes 524320 | tf_op jit(solution)/shard_map/ppermute | solution.py:38
  132.1 4.5 %collective-permute-done.31.refs_2_ = bf16[64,4096]{1,0:T(8,128)(2,1)S(1)} collective-permute-done((bf16[64,4096]{1,0:T(8,128)(2,1)S(1)}, bf16[64,4096]{1,0:T(8,128)(2,1)S(1)}, u32[]{:S(2)}, u32[]{:S(2)}) %collective-permute-start.31) | collective-permute-done | bytes 524320 | tf_op jit(solution)/shard_map/ppermute | solution.py:38
  140.9 7.3 %shard_map.84 = (bf16[128,384]{1,0:T(8,128)(2,1)S(1)}, bf16[128,384]{1,0:T(8,128)(2,1)S(1)}, bf16[128,384]{1,0:T(8,128)(2,1)S(1)}, bf16[128,384]{1,0:T(8,128)(2,...) custom-call(s32[1]{0:T(128)} %bitcast.layer_ref, ...), custom_call_target="tpu_custom_call" | custom-call | flops 3221225472 | bytes 8388608 | tf_op jit(solution)/shard_map/pallas_call | solution.py:149
  150.8 8.2 %collective-permute-start.43 = (bf16[384,4096]{1,0:T(8,128)(2,1)S(1)}, bf16[384,4096]{1,0:T(8,128)(2,1)S(1)}, u32[]{:S(2)}, u32[]{:S(2)}) collective-permute-start(bf16[384,4096]{1,0:T(8,128)(2,1)S(1)} %get-tuple-element.168.refs_4_), channel_id=1, source_target_pairs={{0,1},{1,0},{2,3},{3,2},{4,5},{5,4},{6,7},{7,6},{8,9},{9,8},{10,11... | collective-permute-start | bytes 9437192 | tf_op jit(solution)/shard_map/ppermute | solution.py:42
  159.0 5.2 %shard_map.85 = (bf16[128,512]{1,0:T(8,128)(2,1)S(1)}, bf16[128,512]{1,0:T(8,128)(2,1)S(1)}, bf16[128,512]{1,0:T(8,128)(2,1)S(1)}, bf16[128,512]{1,0:T(8,128)(2,...) custom-call(s32[1]{0:T(128)} %bitcast.layer_ref, ...), custom_call_target="tpu_custom_call" | custom-call | flops 1073741824 | bytes 8388608 | tf_op jit(solution)/shard_map/pallas_call | solution.py:149
  170.1 4.9 %shard_map.86.refs_8_ = bf16[512,4096]{1,0:T(8,128)(2,1)} custom-call(bf16[384,512]{1,0:T(8,128)(2,1)S(1)} %get-tuple-element.164.refs_0_, bf16[384,512]{1,0:T(8,128)(2,1)S(1)} %collective-permute-done.42.refs_1_, bf16[128,512]{1,0:T(8,128)(2,1)S(1)} %get-tuple-element.166.refs_2_, bf16[128,512]{1,0:T(8,128)(2,1)S(1)} %collective-permute-done.20.refs_3_, ...), custom_call_target="tpu_custom_call" | custom-call | flops 2147483648 | bytes 6291456 | tf_op jit(solution)/shard_map/pallas_call | solution.py:234
  177.9 5.0 %shard_map.88 = bf16[512,4096]{1,0:T(8,128)(2,1)} custom-call(bf16[384,512]{1,0:T(8,128)(2,1)S(1)} %get-tuple-element.164.refs_0_, bf16[384,512]{1,0:T(8,128)(2,1)S(1)} %collective-permute-done.42.refs_1_, bf16[128,512]{1,0:T(8,128)(2,1)S(1)} %get-tuple-element.166.refs_2_, ...), custom_call_target="tpu_custom_call", output_to_operand_aliasing={{}: (8, {})} | custom-call | flops 2147483648 | bytes 6291456 | tf_op jit(solution)/shard_map/pallas_call | solution.py:234
  182.9 6.8 %collective-permute-done.39 = bf16[128,512]{1,0:T(8,128)(2,1)S(1)} collective-permute-done((bf16[128,512]{1,0:T(8,128)(2,1)S(1)}, bf16[128,512]{1,0:T(8,128)(2,1)S(1)}, u32[]{:S(2)}, u32[]{:S(2)}) %collective-permute-start.39) | collective-permute-done | bytes 131104 | tf_op jit(solution)/shard_map/ppermute | solution.py:338
  189.6 9.4 %collective-permute-done.46 = bf16[128,512]{1,0:T(8,128)(2,1)S(1)} collective-permute-done((bf16[128,512]{1,0:T(8,128)(2,1)S(1)}, bf16[128,512]{1,0:T(8,128)(2,1)S(1)}, u32[]{:S(2)}, u32[]{:S(2)}) %collective-permute-start.46) | collective-permute-done | bytes 131104 | tf_op jit(solution)/shard_map/ppermute | solution.py:338
  (118 shorter events, 72.7 us)
Async XLA Ops:
  15.9 10.4 %collective-permute-start.8 = (bf16[64,4096]{1,0:T(8,128)(2,1)S(1)}, bf16[64,4096]{1,0:T(8,128)(2,1)S(1)}, u32[]{:S(2)}, u32[]{:S(2)}) collective-permute-start(bf16[64,4096]{1,0:T(8,128)(2,1)S(1)} %pad_maximum_fusion.refs_0_), channel_id=1, source_target_pairs={{0,2},{1,7},{2,0},{3,5},{4,6},{5,3},{6,4},{7,1},{8,10},{9,15},{10,... | collective-permute-start | bytes 1572872 | tf_op jit(solution)/shard_map/ppermute | solution.py:38
  16.4 10.7 %collective-permute-start.4 = (bf16[64,4096]{1,0:T(8,128)(2,1)S(1)}, bf16[64,4096]{1,0:T(8,128)(2,1)S(1)}, u32[]{:S(2)}, u32[]{:S(2)}) collective-permute-start(bf16[64,4096]{1,0:T(8,128)(2,1)S(1)} %pad_maximum_fusion.refs_0_), channel_id=1, source_target_pairs={{0,6},{1,3},{2,4},{3,1},{4,2},{5,7},{6,0},{7,5},{8,14},{9,11},{10,... | collective-permute-start | bytes 1572872 | tf_op jit(solution)/shard_map/ppermute | solution.py:38
  19.5 11.7 %collective-permute-start.6 = (bf16[64,4096]{1,0:T(8,128)(2,1)S(1)}, bf16[64,4096]{1,0:T(8,128)(2,1)S(1)}, u32[]{:S(2)}, u32[]{:S(2)}) collective-permute-start(bf16[64,4096]{1,0:T(8,128)(2,1)S(1)} %pad_maximum_fusion.1.refs_1_), channel_id=1, source_target_pairs={{0,24},{1,9},{2,26},{3,11},{4,28},{5,13},{6,30},{7,15},{8,16},{9,1... | collective-permute-start | bytes 1572872 | tf_op jit(solution)/shard_map/ppermute | solution.py:38
  31.1 44.1 %collective-permute-start.19 = (bf16[512,4096]{1,0:T(8,128)(2,1)}, bf16[512,4096]{1,0:T(8,128)(2,1)}, u32[]{:S(2)}, u32[]{:S(2)}) collective-permute-start(bf16[512,4096]{1,0:T(8,128)(2,1)} %bitcast.17), channel_id=1, source_target_pairs={{0,1},{1,0},{2,3},{3,2},{4,5},{5,4},{6,7},{7,6},{8,9},{9,8},{10,11... | collective-permute-start | bytes 12582920 | tf_op jit(solution)/shard_map/ppermute | solution.py:42
  47.8 13.8 %collective-permute-start.18 = (bf16[512,128]{1,0:T(8,128)(2,1)S(1)}, bf16[512,128]{1,0:T(8,128)(2,1)S(1)}, u32[]{:S(2)}, u32[]{:S(2)}) collective-permute-start(bf16[512,128]{1,0:T(8,128)(2,1)S(1)} %get-tuple-element.111.refs_0_), channel_id=1, source_target_pairs={{0,224},{1,225},{2,226},{3,227},{4,228},{5,229},{6,230},{7,231},{8... | collective-permute-start | bytes 393224 | tf_op jit(solution)/shard_map/ppermute | solution.py:338
  58.5 13.9 %collective-permute-start.17 = (bf16[512,128]{1,0:T(8,128)(2,1)S(1)}, bf16[512,128]{1,0:T(8,128)(2,1)}, u32[]{:S(2)}, u32[]{:S(2)}) collective-permute-start(bf16[512,128]{1,0:T(8,128)(2,1)S(1)} %get-tuple-element.111.refs_0_), channel_id=1, source_target_pairs={{0,192},{32,224},{1,193},{33,225},{2,194},{34,226},{3,195},{35,227... | collective-permute-start | bytes 393224 | tf_op jit(solution)/shard_map/ppermute | solution.py:338
  61.6 13.7 %collective-permute-start.16 = (bf16[512,128]{1,0:T(8,128)(2,1)S(1)}, bf16[512,128]{1,0:T(8,128)(2,1)}, u32[]{:S(2)}, u32[]{:S(2)}) collective-permute-start(bf16[512,128]{1,0:T(8,128)(2,1)S(1)} %get-tuple-element.111.refs_0_), channel_id=1, source_target_pairs={{0,160},{32,192},{64,224},{1,161},{33,193},{65,225},{2,162},{34,19... | collective-permute-start | bytes 393224 | tf_op jit(solution)/shard_map/ppermute | solution.py:338
  64.5 10.8 %collective-permute-start.15 = (bf16[512,128]{1,0:T(8,128)(2,1)S(1)}, bf16[512,128]{1,0:T(8,128)(2,1)}, u32[]{:S(2)}, u32[]{:S(2)}) collective-permute-start(bf16[512,128]{1,0:T(8,128)(2,1)S(1)} %collective-permute-done.13.refs_2_), channel_id=1, source_target_pairs={{64,128},{96,160},{128,192},{160,224},{65,129},{97,161},{129,193},... | collective-permute-start | bytes 393224 | tf_op jit(solution)/shard_map/ppermute | solution.py:338
  83.6 12.1 %collective-permute-start.21 = (bf16[64,4096]{1,0:T(8,128)(2,1)S(1)}, bf16[64,4096]{1,0:T(8,128)(2,1)S(1)}, u32[]{:S(2)}, u32[]{:S(2)}) collective-permute-start(bf16[64,4096]{1,0:T(8,128)(2,1)S(1)} %get-tuple-element.120), channel_id=1, source_target_pairs={{0,2},{1,7},{2,0},{3,5},{4,6},{5,3},{6,4},{7,1},{8,10},{9,15},{10,... | collective-permute-start | bytes 1572872 | tf_op jit(solution)/shard_map/ppermute | solution.py:38
  84.7 11.1 %collective-permute-start.22 = (bf16[64,4096]{1,0:T(8,128)(2,1)S(1)}, bf16[64,4096]{1,0:T(8,128)(2,1)S(1)}, u32[]{:S(2)}, u32[]{:S(2)}) collective-permute-start(bf16[64,4096]{1,0:T(8,128)(2,1)S(1)} %get-tuple-element.121), channel_id=1, source_target_pairs={{0,8},{1,25},{2,10},{3,27},{4,12},{5,29},{6,14},{7,31},{8,0},{9,17... | collective-permute-start | bytes 1572872 | tf_op jit(solution)/shard_map/ppermute | solution.py:38
  92.5 12.1 %collective-permute-start.25 = (bf16[64,4096]{1,0:T(8,128)(2,1)S(1)}, bf16[64,4096]{1,0:T(8,128)(2,1)S(1)}, u32[]{:S(2)}, u32[]{:S(2)}) collective-permute-start(bf16[64,4096]{1,0:T(8,128)(2,1)S(1)} %get-tuple-element.124), channel_id=1, source_target_pairs={{0,2},{1,7},{2,0},{3,5},{4,6},{5,3},{6,4},{7,1},{8,10},{9,15},{10,... | collective-permute-start | bytes 1572872 | tf_op jit(solution)/shard_map/ppermute | solution.py:38
  94.2 12.4 %collective-permute-start.26 = (bf16[64,4096]{1,0:T(8,128)(2,1)S(1)}, bf16[64,4096]{1,0:T(8,128)(2,1)S(1)}, u32[]{:S(2)}, u32[]{:S(2)}) collective-permute-start(bf16[64,4096]{1,0:T(8,128)(2,1)S(1)} %get-tuple-element.125), channel_id=1, source_target_pairs={{0,8},{1,25},{2,10},{3,27},{4,12},{5,29},{6,14},{7,31},{8,0},{9,17... | collective-permute-start | bytes 1572872 | tf_op jit(solution)/shard_map/ppermute | solution.py:38
  96.0 10.6 %collective-permute-start.23 = (bf16[64,4096]{1,0:T(8,128)(2,1)S(1)}, bf16[64,4096]{1,0:T(8,128)(2,1)S(1)}, u32[]{:S(2)}, u32[]{:S(2)}) collective-permute-start(bf16[64,4096]{1,0:T(8,128)(2,1)S(1)} %get-tuple-element.122), channel_id=1, source_target_pairs={{0,6},{1,3},{2,4},{3,1},{4,2},{5,7},{6,0},{7,5},{8,14},{9,11},{10,... | collective-permute-start | bytes 1572872 | tf_op jit(solution)/shard_map/ppermute | solution.py:38
  96.1 11.1 %collective-permute-start.24 = (bf16[64,4096]{1,0:T(8,128)(2,1)S(1)}, bf16[64,4096]{1,0:T(8,128)(2,1)S(1)}, u32[]{:S(2)}, u32[]{:S(2)}) collective-permute-start(bf16[64,4096]{1,0:T(8,128)(2,1)S(1)} %get-tuple-element.123), channel_id=1, source_target_pairs={{0,24},{1,9},{2,26},{3,11},{4,28},{5,13},{6,30},{7,15},{8,16},{9,1... | collective-permute-start | bytes 1572872 | tf_op jit(solution)/shard_map/ppermute | solution.py:38
  129.4 11.0 %collective-permute-start.35 = (bf16[64,4096]{1,0:T(8,128)(2,1)S(1)}, bf16[64,4096]{1,0:T(8,128)(2,1)S(1)}, u32[]{:S(2)}, u32[]{:S(2)}) collective-permute-start(bf16[64,4096]{1,0:T(8,128)(2,1)S(1)} %get-tuple-element.135.refs_0_), channel_id=1, source_target_pairs={{0,2},{1,7},{2,0},{3,5},{4,6},{5,3},{6,4},{7,1},{8,10},{9,15},{10,... | collective-permute-start | bytes 1572872 | tf_op jit(solution)/shard_map/ppermute | solution.py:38
  130.3 10.6 %collective-permute-start.36 = (bf16[64,4096]{1,0:T(8,128)(2,1)S(1)}, bf16[64,4096]{1,0:T(8,128)(2,1)S(1)}, u32[]{:S(2)}, u32[]{:S(2)}) collective-permute-start(bf16[64,4096]{1,0:T(8,128)(2,1)S(1)} %get-tuple-element.136.refs_1_), channel_id=1, source_target_pairs={{0,8},{1,25},{2,10},{3,27},{4,12},{5,29},{6,14},{7,31},{8,0},{9,17... | collective-permute-start | bytes 1572872 | tf_op jit(solution)/shard_map/ppermute | solution.py:38
  136.5 13.3 %collective-permute-start.32 = (bf16[64,4096]{1,0:T(8,128)(2,1)S(1)}, bf16[64,4096]{1,0:T(8,128)(2,1)S(1)}, u32[]{:S(2)}, u32[]{:S(2)}) collective-permute-start(bf16[64,4096]{1,0:T(8,128)(2,1)S(1)} %collective-permute-done.31.refs_2_), channel_id=1, source_target_pairs={{0,2},{1,7},{2,0},{3,5},{4,6},{5,3},{6,4},{7,1},{8,10},{9,15},{10,... | collective-permute-start | bytes 1572872 | tf_op jit(solution)/shard_map/ppermute | solution.py:38
  137.6 13.2 %collective-permute-start.34 = (bf16[64,4096]{1,0:T(8,128)(2,1)S(1)}, bf16[64,4096]{1,0:T(8,128)(2,1)S(1)}, u32[]{:S(2)}, u32[]{:S(2)}) collective-permute-start(bf16[64,4096]{1,0:T(8,128)(2,1)S(1)} %collective-permute-done.33.refs_3_), channel_id=1, source_target_pairs={{0,8},{1,25},{2,10},{3,27},{4,12},{5,29},{6,14},{7,31},{8,0},{9,17... | collective-permute-start | bytes 1572872 | tf_op jit(solution)/shard_map/ppermute | solution.py:38
  150.8 18.7 %collective-permute-start.43 = (bf16[384,4096]{1,0:T(8,128)(2,1)S(1)}, bf16[384,4096]{1,0:T(8,128)(2,1)S(1)}, u32[]{:S(2)}, u32[]{:S(2)}) collective-permute-start(bf16[384,4096]{1,0:T(8,128)(2,1)S(1)} %get-tuple-element.168.refs_4_), channel_id=1, source_target_pairs={{0,1},{1,0},{2,3},{3,2},{4,5},{5,4},{6,7},{7,6},{8,9},{9,8},{10,11... | collective-permute-start | bytes 9437192 | tf_op jit(solution)/shard_map/ppermute | solution.py:42
  164.8 18.1 %collective-permute-start.37 = (bf16[128,512]{1,0:T(8,128)(2,1)S(1)}, bf16[128,512]{1,0:T(8,128)(2,1)S(1)}, u32[]{:S(2)}, u32[]{:S(2)}) collective-permute-start(bf16[128,512]{1,0:T(8,128)(2,1)S(1)} %get-tuple-element.157), channel_id=1, source_target_pairs={{160,0},{192,32},{224,64},{161,1},{193,33},{225,65},{162,2},{194,3... | collective-permute-start | bytes 393224 | tf_op jit(solution)/shard_map/ppermute | solution.py:338
  166.0 16.8 %collective-permute-start.38 = (bf16[128,512]{1,0:T(8,128)(2,1)S(1)}, bf16[128,512]{1,0:T(8,128)(2,1)S(1)}, u32[]{:S(2)}, u32[]{:S(2)}) collective-permute-start(bf16[128,512]{1,0:T(8,128)(2,1)S(1)} %get-tuple-element.158), channel_id=1, source_target_pairs={{192,0},{224,32},{193,1},{225,33},{194,2},{226,34},{195,3},{227,35... | collective-permute-start | bytes 393224 | tf_op jit(solution)/shard_map/ppermute | solution.py:338
  167.5 22.2 %collective-permute-start.39 = (bf16[128,512]{1,0:T(8,128)(2,1)S(1)}, bf16[128,512]{1,0:T(8,128)(2,1)S(1)}, u32[]{:S(2)}, u32[]{:S(2)}) collective-permute-start(bf16[128,512]{1,0:T(8,128)(2,1)S(1)} %get-tuple-element.159), channel_id=1, source_target_pairs={{224,0},{225,1},{226,2},{227,3},{228,4},{229,5},{230,6},{231,7},{2... | collective-permute-start | bytes 393224 | tf_op jit(solution)/shard_map/ppermute | solution.py:338
  175.2 14.5 %collective-permute-start.45 = (bf16[128,512]{1,0:T(8,128)(2,1)S(1)}, bf16[128,512]{1,0:T(8,128)(2,1)S(1)}, u32[]{:S(2)}, u32[]{:S(2)}) collective-permute-start(bf16[128,512]{1,0:T(8,128)(2,1)S(1)} %get-tuple-element.175), channel_id=1, source_target_pairs={{32,0},{64,32},{96,64},{128,96},{160,128},{192,160},{224,192},{33,... | collective-permute-start | bytes 393224 | tf_op jit(solution)/shard_map/ppermute | solution.py:338
  176.6 22.5 %collective-permute-start.46 = (bf16[128,512]{1,0:T(8,128)(2,1)S(1)}, bf16[128,512]{1,0:T(8,128)(2,1)S(1)}, u32[]{:S(2)}, u32[]{:S(2)}) collective-permute-start(bf16[128,512]{1,0:T(8,128)(2,1)S(1)} %get-tuple-element.176), channel_id=1, source_target_pairs={{64,0},{96,32},{128,64},{160,96},{192,128},{224,160},{65,1},{97,33... | collective-permute-start | bytes 393224 | tf_op jit(solution)/shard_map/ppermute | solution.py:338
  (35 other events, 382.6 us)
